TPU v7x, 128 devices: a whole 4x4x4 slice. The times are simulated.
128 devices in a mesh: tile: 32 (over y, z, core), cam: 4 (over x).
Axes of the slice: x: 4, y: 4, z: 4, core: 2. Of those that a mesh axis runs over, the one named last changes fastest.
Arguments:
- pixels: bfloat16 [256, 4096, 128], P('cam', 'tile'), may hold values from -6 to 6
- pixel_hidden: bfloat16 [256, 4096, 128], P('cam', 'tile'), may hold values from -6 to 6
- pixel_upstream: bfloat16 [256, 4096, 128], P('cam', 'tile'), may hold values from -1.5 to 1.5
- points: bfloat16 [262144, 128], P(('tile', 'cam')), may hold values from -6 to 6
- point_hidden: bfloat16 [262144, 128], P(('tile', 'cam')), may hold values from -6 to 6
- point_upstream: bfloat16 [262144, 128], P(('tile', 'cam')), may hold values from -1.5 to 1.5
- mixing: bfloat16 [4096, 256, 384], P(('tile', 'cam')), may hold values from -0.3125 to 0.3125
- neighbors: int32 [4096, 6], P(('tile', 'cam')), may hold values from 0 to 255
- send_list: int32 [128, 128, 2], P(('tile', 'cam')), may hold values from 0 to 31
- pixel_weight: bfloat16 [128, 128], replicated, may hold values from -0.5 to 0.5
- point_weight: bfloat16 [128, 128], replicated, may hold values from -0.5 to 0.5
- kernel: float32 [3, 3, 128], replicated, may hold values from -2 to 2
Outputs:
- pixel_gradient: bfloat16 [256, 4096, 128], P('cam', 'tile')
- point_gradient: bfloat16 [262144, 128], P(('tile', 'cam'))
- mixing_gradient: bfloat16 [4096, 256, 384], P(('tile', 'cam'))
Inputs may be any that keep to these rules, and one draw needn't show every extreme that they name: `neighbors`: entry s names slot s % 2 of the slots filled by device s // 2. `send_list`: entry [o, d, s] is the block of device o, counted within that device, that fills slot s from device o at device d.
All inputs are finite; a program needn't handle non-finite values.
Results may differ from a plain program's by a relative error of at most 0.0054.
Values may be sent and summed in bfloat16 or wider, within the bound.
No kernel may reach another device: no remote copies, remote signals or barrier semaphores. Data moves between devices by JAX's collectives and lax.ppermute only.
A program may use at most 192 MiB of HBM per device.

v0:
```python
import functools

import jax
import jax.numpy as jnp
from jax import lax
from jax.experimental import pallas as pl
from jax.experimental.pallas import tpu as pltpu
from jax.sharding import PartitionSpec as P

C = 128
ROWS_DEV = 64
COLS_DEV = 128
K = 6
BS = 64
CAP = 2
BLK_DEV = 32
PB = 32
PIXB = 256
STRIPS = 4
MIB = 1024 * 1024
VMEM = 60 * MIB
DESTS = 8
OWNERS = 8


def slope_of(upstream, hidden):
    argument = hidden.astype(jnp.float32)
    logistic = jax.nn.sigmoid(argument)
    slope = logistic * (1.0 + argument * (1.0 - logistic))
    return (upstream.astype(jnp.float32) * slope).astype(jnp.bfloat16)


def pack_kernel(targets, points, hidden, upstream, out, slope):
    step = pl.program_id(0)

    @pl.when(step == 0)
    def _():
        def body(b, carry):
            slope[b] = slope_of(upstream[b], hidden[b])
            return carry

        lax.fori_loop(0, BLK_DEV, body, 0)

    for d in range(DESTS):
        for s in range(CAP):
            block = targets[(step * DESTS + d) * CAP + s]
            out[d, s] = points[block]
            out[d, CAP + s] = slope[block]


def pack(targets, points, hidden, upstream, devices):
    whole = pl.BlockSpec((BLK_DEV, BS, C), lambda i, t: (0, 0, 0))
    return pl.pallas_call(
        pack_kernel,
        grid_spec=pltpu.PrefetchScalarGridSpec(
            num_scalar_prefetch=1,
            grid=(devices // DESTS,),
            in_specs=[whole, whole, whole],
            out_specs=[
                pl.BlockSpec((DESTS, 2 * CAP, BS, C), lambda i, t: (i, 0, 0, 0)),
                whole,
            ],
        ),
        out_shape=[
            jax.ShapeDtypeStruct((devices, 2 * CAP, BS, C), jnp.bfloat16),
            jax.ShapeDtypeStruct((BLK_DEV, BS, C), jnp.bfloat16),
        ],
        compiler_params=pltpu.CompilerParams(vmem_limit_bytes=VMEM),
        cost_estimate=pl.CostEstimate(flops=10 * MIB, bytes_accessed=12 * MIB, transcendentals=0),
        name="pack",
    )(targets, points, hidden, upstream)


def pixel_kernel(
    neighbors, hidden, upstream, mixing, weight, slope, mixed, sums, first, last, total
):
    q = pl.program_id(0)

    @pl.when(q == 0)
    def _():
        total[...] = jnp.zeros_like(total)

    values = slope_of(upstream[...], hidden[...])
    slope[...] = values
    wide = values.astype(jnp.float32)
    for r in range(2):
        first[pl.ds(2 * q + r, 1), :] = wide[r, 0:1, :]
        last[pl.ds(2 * q + r, 1), :] = wide[r, COLS_DEV - 1 : COLS_DEV, :]
    projected = lax.dot_general(
        values.reshape(PIXB, C),
        weight[...],
        (((1,), (1,)), ((), ())),
        preferred_element_type=jnp.float32,
    ).astype(jnp.bfloat16)
    mixed[0] = projected
    term = lax.dot_general(
        mixing[0], projected, (((0,), (0,)), ((), ())), preferred_element_type=jnp.float32
    )
    for k in range(K):
        slot = neighbors[q * K + k]
        total[slot] += term[k * BS : (k + 1) * BS]

    @pl.when(q == PB - 1)
    def _():
        def body(i, carry):
            sums[i] = total[i].astype(jnp.bfloat16)
            return carry

        lax.fori_loop(0, total.shape[0], body, 0)


def pixel_part(neighbors, hidden, upstream, mixing, weight, slots):
    rows = pl.BlockSpec((2, COLS_DEV, C), lambda q, n: (q, 0, 0))
    return pl.pallas_call(
        pixel_kernel,
        grid_spec=pltpu.PrefetchScalarGridSpec(
            num_scalar_prefetch=1,
            grid=(PB,),
            in_specs=[
                rows,
                rows,
                pl.BlockSpec((1, PIXB, K * BS), lambda q, n: (q, 0, 0)),
                pl.BlockSpec((C, C), lambda q, n: (0, 0)),
            ],
            out_specs=[
                rows,
                pl.BlockSpec((1, PIXB, C), lambda q, n: (q, 0, 0)),
                pl.BlockSpec((slots, BS, C), lambda q, n: (0, 0, 0)),
                pl.BlockSpec((ROWS_DEV, C), lambda q, n: (0, 0)),
                pl.BlockSpec((ROWS_DEV, C), lambda q, n: (0, 0)),
            ],
            scratch_shapes=[pltpu.VMEM((slots, BS, C), jnp.float32)],
        ),
        out_shape=[
            jax.ShapeDtypeStruct((ROWS_DEV, COLS_DEV, C), jnp.bfloat16),
            jax.ShapeDtypeStruct((PB, PIXB, C), jnp.bfloat16),
            jax.ShapeDtypeStruct((slots, BS, C), jnp.bfloat16),
            jax.ShapeDtypeStruct((ROWS_DEV, C), jnp.float32),
            jax.ShapeDtypeStruct((ROWS_DEV, C), jnp.float32),
        ],
        compiler_params=pltpu.CompilerParams(vmem_limit_bytes=VMEM),
        cost_estimate=pl.CostEstimate(
            flops=1200 * MIB, bytes_accessed=18 * MIB, transcendentals=MIB
        ),
        name="pixel_part",
    )(neighbors, hidden, upstream, mixing, weight)


def main_kernel(
    neighbors, incoming, mixed, pixels, mixing, upstream, padded, left, right, kernel,
    mixing_gradient, pixel_gradient, left_side, right_side,
):
    q = pl.program_id(0)
    for k in range(K):
        slot = neighbors[q * K + k]
        owner = lax.div(slot, CAP)
        place = lax.rem(slot, CAP)
        right_side[k * BS : (k + 1) * BS, 0:C] = incoming[owner, place]
        right_side[k * BS : (k + 1) * BS, C : 2 * C] = incoming[owner, CAP + place]
    left_side[:, 0:C] = mixed[0]
    left_side[:, C : 2 * C] = pixels[...].reshape(PIXB, C)
    mixing_gradient[0] = lax.dot_general(
        left_side[...],
        right_side[...],
        (((1,), (1,)), ((), ())),
        preferred_element_type=jnp.float32,
    ).astype(jnp.bfloat16)
    term = jnp.dot(mixing[0], right_side[:, C : 2 * C], preferred_element_type=jnp.float32)
    column = lax.broadcasted_iota(jnp.int32, (COLS_DEV, C), 0)
    for r in range(2):
        row = 2 * q + r
        total = upstream[r].astype(jnp.float32) + term[r * COLS_DEV : (r + 1) * COLS_DEV]
        sides = []
        for e in range(3):
            part = None
            edge = None
            for a in range(3):
                gain = kernel[a, e : e + 1, :]
                piece = padded[row + 2 - a].astype(jnp.float32) * gain
                part = piece if part is None else part + piece
                if e != 1:
                    rim = right if e == 0 else left
                    corner = rim[pl.ds(row + 2 - a, 1), :] * gain
                    edge = corner if edge is None else edge + corner
            sides.append((part, edge))
        total = total + sides[1][0]
        ahead = pltpu.roll(sides[0][0], COLS_DEV - 1, 0)
        total = total + jnp.where(column == COLS_DEV - 1, sides[0][1], ahead)
        behind = pltpu.roll(sides[2][0], 1, 0)
        total = total + jnp.where(column == 0, sides[2][1], behind)
        pixel_gradient[r] = total.astype(jnp.bfloat16)


def main_part(neighbors, incoming, mixed, pixels, mixing, upstream, padded, left, right, kernel):
    rows = pl.BlockSpec((2, COLS_DEV, C), lambda q, n: (q, 0, 0))
    once = pl.Buffered(1)
    return pl.pallas_call(
        main_kernel,
        grid_spec=pltpu.PrefetchScalarGridSpec(
            num_scalar_prefetch=1,
            grid=(PB,),
            in_specs=[
                pl.BlockSpec(incoming.shape, lambda q, n: (0, 0, 0, 0), pipeline_mode=once),
                pl.BlockSpec((1, PIXB, C), lambda q, n: (q, 0, 0)),
                rows,
                pl.BlockSpec((1, PIXB, K * BS), lambda q, n: (q, 0, 0)),
                rows,
                pl.BlockSpec(padded.shape, lambda q, n: (0, 0, 0), pipeline_mode=once),
                pl.BlockSpec(left.shape, lambda q, n: (0, 0)),
                pl.BlockSpec(right.shape, lambda q, n: (0, 0)),
                pl.BlockSpec((3, 3, C), lambda q, n: (0, 0, 0)),
            ],
            out_specs=[
                pl.BlockSpec((1, PIXB, K * BS), lambda q, n: (q, 0, 0)),
                rows,
            ],
            scratch_shapes=[
                pltpu.VMEM((PIXB, 2 * C), jnp.bfloat16),
                pltpu.VMEM((K * BS, 2 * C), jnp.bfloat16),
            ],
        ),
        out_shape=[
            jax.ShapeDtypeStruct((PB, PIXB, K * BS), jnp.bfloat16),
            jax.ShapeDtypeStruct((ROWS_DEV, COLS_DEV, C), jnp.bfloat16),
        ],
        compiler_params=pltpu.CompilerParams(vmem_limit_bytes=VMEM),
        cost_estimate=pl.CostEstimate(
            flops=2600 * MIB, bytes_accessed=30 * MIB, transcendentals=0
        ),
        name="main_part",
    )(neighbors, incoming, mixed, pixels, mixing, upstream, padded, left, right, kernel)


def return_kernel(targets, received, base, out, total):
    step = pl.program_id(0)

    @pl.when(step == 0)
    def _():
        total[...] = base[...]

    for o in range(OWNERS):
        for s in range(CAP):
            block = targets[(step * OWNERS + o) * CAP + s]
            total[block] += received[o, s].astype(jnp.float32)

    @pl.when(step == pl.num_programs(0) - 1)
    def _():
        out[...] = total[...].astype(jnp.bfloat16)


def return_part(targets, received, base):
    devices = received.shape[0]
    whole = pl.BlockSpec((BLK_DEV, BS, C), lambda i, t: (0, 0, 0))
    return pl.pallas_call(
        return_kernel,
        grid_spec=pltpu.PrefetchScalarGridSpec(
            num_scalar_prefetch=1,
            grid=(devices // OWNERS,),
            in_specs=[
                pl.BlockSpec((OWNERS, CAP, BS, C), lambda i, t: (i, 0, 0, 0)),
                whole,
            ],
            out_specs=whole,
            scratch_shapes=[pltpu.VMEM((BLK_DEV, BS, C), jnp.float32)],
        ),
        out_shape=jax.ShapeDtypeStruct((BLK_DEV, BS, C), jnp.bfloat16),
        compiler_params=pltpu.CompilerParams(vmem_limit_bytes=VMEM),
        cost_estimate=pl.CostEstimate(flops=4 * MIB, bytes_accessed=6 * MIB, transcendentals=0),
        name="return_part",
    )(targets, received, base)


def shifted(block, tiles, cams, tile_step, cam_step):
    pairs = []
    for t in range(tiles):
        for c in range(cams):
            strip = (t + 1) % STRIPS + tile_step
            cam = c + cam_step
            if 0 <= strip < STRIPS and 0 <= cam < cams:
                pairs.append((t * cams + c, (t + tile_step) % tiles * cams + cam))
    return lax.ppermute(block, ("tile", "cam"), pairs)


def per_device(
    pixels,
    pixel_hidden,
    pixel_upstream,
    points,
    point_hidden,
    point_upstream,
    mixing,
    neighbors,
    send_list,
    pixel_weight,
    point_weight,
    kernel,
):
    tiles = lax.axis_size("tile")
    cams = lax.axis_size("cam")
    devices = tiles * cams
    slots = devices * CAP
    targets = send_list.reshape(-1)
    reads = neighbors.reshape(-1)
    blocks = (BLK_DEV, BS, C)
    outgoing, point_slope = pack(
        targets,
        points.reshape(blocks),
        point_hidden.reshape(blocks),
        point_upstream.reshape(blocks),
        devices,
    )
    outgoing, reads = lax.optimization_barrier((outgoing, reads))
    incoming = lax.all_to_all(
        outgoing, ("tile", "cam"), split_axis=0, concat_axis=0, tiled=True
    )
    pixel_slope, mixed, sums, first, last = pixel_part(
        reads, pixel_hidden, pixel_upstream, mixing, pixel_weight, slots
    )
    move = functools.partial(shifted, tiles=tiles, cams=cams)
    rim_left = jnp.concatenate(
        [
            move(last[-1:], tile_step=1, cam_step=1),
            move(last, tile_step=1, cam_step=0),
            move(last[:1], tile_step=1, cam_step=-1),
        ],
        axis=0,
    )
    rim_right = jnp.concatenate(
        [
            move(first[-1:], tile_step=-1, cam_step=1),
            move(first, tile_step=-1, cam_step=0),
            move(first[:1], tile_step=-1, cam_step=-1),
        ],
        axis=0,
    )
    padded = jnp.concatenate(
        [
            move(pixel_slope[-1:], tile_step=0, cam_step=1),
            pixel_slope,
            move(pixel_slope[:1], tile_step=0, cam_step=-1),
        ],
        axis=0,
    )
    sums, incoming, rim_left, rim_right, padded = lax.optimization_barrier(
        (sums, incoming, rim_left, rim_right, padded)
    )
    received = lax.all_to_all(
        sums.reshape(devices, CAP, BS, C),
        ("tile", "cam"),
        split_axis=0,
        concat_axis=0,
        tiled=True,
    )
    mixing_gradient, pixel_gradient = main_part(
        reads, incoming, mixed, pixels, mixing, pixel_upstream, padded, rim_left, rim_right, kernel
    )
    base = point_upstream.astype(jnp.float32) + jnp.dot(
        point_slope.reshape(BLK_DEV * BS, C), point_weight.T, preferred_element_type=jnp.float32
    )
    base, pixel_gradient = lax.optimization_barrier((base, pixel_gradient))
    point_gradient = return_part(targets, received, base.reshape(blocks))
    return (pixel_gradient, point_gradient.reshape(BLK_DEV * BS, C), mixing_gradient)


def solution(mesh):
    return jax.shard_map(
        per_device,
        mesh=mesh,
        in_specs=(
            P("cam", "tile", None),
            P("cam", "tile", None),
            P("cam", "tile", None),
            P(("tile", "cam"), None),
            P(("tile", "cam"), None),
            P(("tile", "cam"), None),
            P(("tile", "cam"), None, None),
            P(("tile", "cam"), None),
            P(("tile", "cam"), None, None),
            P(),
            P(),
            P(),
        ),
        out_specs=(
            P("cam", "tile", None),
            P(("tile", "cam"), None),
            P(("tile", "cam"), None, None),
        ),
        check_vma=False,
    )
```

profile of v0, /device:TPU:1, one launch (start us, length us, event | category | flops | bytes accessed | tf_op | source)
XLA Modules:
  0.0 211.4 jit_solution(6510961873135236358)
XLA Ops:
  0.6 0.0 copy-start
  0.6 0.8 copy.15
  1.4 0.7 reshape.33.targets
  2.2 0.8 copy.16
  2.9 0.7 reshape.38.neighbors
  3.6 9.9 %pack.1 = (bf16[128,4,64,128]{3,2,1,0:T(8,128)(2,1)}, bf16[32,64,128]{2,1,0:T(8,128)(2,1)}) custom-call(s32[256]{0:T(256)} %reshape.33.targets, bf16[32,64,128]{2,1,0:T(8,128)(2,1)} %bitcast.13, bf16[32,64,128]{2,1,0:T(8,128)(2,1)} %bitcast.14, bf16[32,64,128]{2,1,0:T(8,128)(2,1)} %bitcast.11), custom_call_target="tpu_custom_call" | custom-call | flops 10485760 | bytes 12582912 | tf_op jit(solution)/shard_map/pack/pallas_call | solution.py:53
  13.5 12.0 %all-to-all-start = ((bf16[128,4,64,128]{3,2,1,0:T(8,128)(2,1)}), bf16[128,4,64,128]{3,2,1,0:T(8,128)(2,1)}, u32[]{:S(2)}, u32[]{:S(2)}) async-start(bf16[128,4,64,128]{3,2,1,0:T(8,128)(2,1)} %get-tuple-element.25), calls=%async_computation | async-start | bytes 16777216 | tf_op jit(solution)/shard_map/all_to_all | solution.py:313
  25.4 29.0 %pixel_part.1 = (bf16[64,128,128]{2,1,0:T(8,128)(2,1)}, bf16[32,256,128]{2,1,0:T(8,128)(2,1)}, bf16[256,64,128]{2,1,0:T(8,128)(2,1)}, f32[64,128]{1,0:T(8,128)}, f32[64,128]{1,0:T(8,128)}) custom-call(s32[192]{0:T(256)} %reshape.38.neighbors, bf16[64,128,128]{2,1,0:T(8,128)(2,1)} %hidden.1, bf16[64,128,128]{2,1,0:T(8,128)(2,1)} %upstream.3, ...), custom_call_target="tpu_custom_call" | custom-call | flops 1258291200 | bytes 18874368 | tf_op jit(solution)/shard_map/pixel_part/pallas_call | solution.py:114
  54.4 0.8 fusion
  55.2 3.3 %collective-permute-start.6 = (bf16[1,128,128]{2,1,0:T(8,128)(2,1)S(1)}, bf16[1,128,128]{2,1,0:T(8,128)(2,1)S(1)}, u32[]{:S(2)}, u32[]{:S(2)}) collective-permute-start(bf16[1,128,128]{2,1,0:T(8,128)(2,1)S(1)} %get-tuple-element.39), channel_id=1, source_target_pairs={{0,1},{1,2},{2,3},{4,5},{5,6},{6,7},{8,9},{9,10},{10,11},{12,13},{... | collective-permute-start | bytes 98312 | tf_op jit(solution)/shard_map/ppermute | solution.py:281
  58.5 2.5 %collective-permute-start.4 = (f32[64,128]{1,0:T(8,128)}, f32[64,128]{1,0:T(8,128)S(1)}, u32[]{:S(2)}, u32[]{:S(2)}) collective-permute-start(f32[64,128]{1,0:T(8,128)} %get-tuple-element.27), channel_id=1, source_target_pairs={{0,124},{1,125},{2,126},{3,127},{4,0},{5,1},{6,2},{7,3},{8,4},{9,5... | collective-permute-start | bytes 98312 | tf_op jit(solution)/shard_map/ppermute | solution.py:281
  61.0 0.7 fusion.1
  61.7 8.1 %collective-permute-start.3 = (f32[1,128]{1,0:T(1,128)S(1)}, f32[1,128]{1,0:T(1,128)S(1)}, u32[]{:S(2)}, u32[]{:S(2)}) collective-permute-start(f32[1,128]{1,0:T(1,128)S(1)} %get-tuple-element.41), channel_id=1, source_target_pairs={{0,125},{1,126},{2,127},{4,1},{5,2},{6,3},{8,5},{9,6},{10,7},{16,1... | collective-permute-start | bytes 1544 | tf_op jit(solution)/shard_map/ppermute | solution.py:281
  69.9 1.3 collective-permute-start.5
  71.2 1.9 collective-permute-start.1
  73.1 0.7 fusion.2
  73.8 40.5 %collective-permute-done.3 = f32[1,128]{1,0:T(1,128)S(1)} collective-permute-done((f32[1,128]{1,0:T(1,128)S(1)}, f32[1,128]{1,0:T(1,128)S(1)}, u32[]{:S(2)}, u32[]{:S(2)}) %collective-permute-start.3) | collective-permute-done | bytes 544 | tf_op jit(solution)/shard_map/ppermute | solution.py:281
  114.3 1.3 collective-permute-start.7
  115.6 4.4 %collective-permute-done.5 = f32[1,128]{1,0:T(1,128)S(1)} collective-permute-done((f32[1,128]{1,0:T(1,128)S(1)}, f32[1,128]{1,0:T(1,128)S(1)}, u32[]{:S(2)}, u32[]{:S(2)}) %collective-permute-start.5) | collective-permute-done | bytes 544 | tf_op jit(solution)/shard_map/ppermute | solution.py:281
  120.0 9.0 %collective-permute-start = (f32[1,128]{1,0:T(1,128)S(1)}, f32[1,128]{1,0:T(1,128)S(1)}, u32[]{:S(2)}, u32[]{:S(2)}) collective-permute-start(f32[1,128]{1,0:T(1,128)S(1)} %get-tuple-element.43), channel_id=1, source_target_pairs={{0,5},{1,6},{2,7},{4,9},{5,10},{6,11},{12,17},{13,18},{14,19},{16,... | collective-permute-start | bytes 1544 | tf_op jit(solution)/shard_map/ppermute | solution.py:281
  129.0 0.0 collective-permute-done.4
  129.1 1.3 collective-permute-start.2
  130.4 0.6 pad_maximum_fusion.2.right
  131.0 0.0 collective-permute-done
  131.0 3.6 %collective-permute-done.2 = f32[1,128]{1,0:T(1,128)S(1)} collective-permute-done((f32[1,128]{1,0:T(1,128)S(1)}, f32[1,128]{1,0:T(1,128)S(1)}, u32[]{:S(2)}, u32[]{:S(2)}) %collective-permute-start.2) | collective-permute-done | bytes 544 | tf_op jit(solution)/shard_map/ppermute | solution.py:281
  134.6 0.0 collective-permute-done.1
  134.6 0.6 pad_maximum_fusion.1.left
  135.2 0.0 collective-permute-done.6
  135.2 0.0 collective-permute-done.7
  135.2 3.2 %pad_maximum_fusion.padded = bf16[66,128,128]{2,1,0:T(8,128)(2,1)} fusion(bf16[1,128,128]{2,1,0:T(8,128)(2,1)S(1)} %collective-permute-done.7, bf16[64,128,128]{2,1,0:T(8,128)(2,1)} %get-tuple-element.28, bf16[1,128,128]{2,1,0:T(8,128)(2,1)S(1)} %collective-permute-done.6), kind=kLoop, calls=%fused_computation.1 | loop fusion | flops 2162688 | bytes 4325376 | tf_op jit(solution)/shard_map/concatenate | solution.py:336
  138.4 0.0 all-to-all-done.incoming
  138.4 0.0 copy-start.1
  138.4 0.0 copy-start.2
  138.4 9.3 %all-to-all-start.1 = ((bf16[128,2,64,128]{3,2,1,0:T(8,128)(2,1)}), bf16[128,2,64,128]{3,2,1,0:T(8,128)(2,1)}, u32[]{:S(2)}, u32[]{:S(2)}) async-start(bf16[128,2,64,128]{3,2,1,0:T(8,128)(2,1)} %bitcast.9), calls=%async_computation.1 | async-start | bytes 8388608 | tf_op jit(solution)/shard_map/all_to_all | solution.py:347
  147.7 0.0 copy-done
  147.8 0.0 copy-done.1
  147.8 0.0 copy-done.2
  147.8 1.3 convolution_add_fusion
  149.1 28.1 %main_part.1 = (bf16[32,256,384]{2,1,0:T(8,128)(2,1)}, bf16[64,128,128]{2,1,0:T(8,128)(2,1)}) custom-call(s32[192]{0:T(256)} %reshape.38.neighbors, bf16[128,4,64,128]{3,2,1,0:T(8,128)(2,1)} %all-to-all-done.incoming, bf16[32,256,128]{2,1,0:T(8,128)(2,1)} %get-tuple-element.30.mixed, bf16[64,128,128]{2,1,0:T(8,128)(2,1)} %pixels.1, ...), custom_call_target="tpu_custom_call" | custom-call | flops 2726297600 | bytes 31457280 | tf_op jit(solution)/shard_map/main_part/pallas_call | solution.py:197
  177.2 23.8 %all-to-all-done.1.received = bf16[128,2,64,128]{3,2,1,0:T(8,128)(2,1)} async-done(((bf16[128,2,64,128]{3,2,1,0:T(8,128)(2,1)}), bf16[128,2,64,128]{3,2,1,0:T(8,128)(2,1)}, u32[]{:S(2)}, u32[]{:S(2)}) %all-to-all-start.1) | async-done | bytes 4194336 | tf_op jit(solution)/shard_map/all_to_all | solution.py:347
  201.0 10.5 %return_part.1 = bf16[32,64,128]{2,1,0:T(8,128)(2,1)} custom-call(s32[256]{0:T(256)} %reshape.33.targets, bf16[128,2,64,128]{3,2,1,0:T(8,128)(2,1)} %all-to-all-done.1.received, f32[32,64,128]{2,1,0:T(8,128)} %bitcast.10), custom_call_target="tpu_custom_call" | custom-call | flops 4194304 | bytes 6291456 | tf_op jit(solution)/shard_map/return_part/pallas_call | solution.py:254
Async XLA Ops:
  0.6 147.1 %copy-start = (bf16[128,128]{1,0:T(8,128)(2,1)S(1)}, bf16[128,128]{1,0:T(8,128)(2,1)}, u32[]{:S(2)}) copy-start(bf16[128,128]{1,0:T(8,128)(2,1)} %param.22) | copy-start | bytes 98308
  13.5 125.0 %all-to-all-start = ((bf16[128,4,64,128]{3,2,1,0:T(8,128)(2,1)}), bf16[128,4,64,128]{3,2,1,0:T(8,128)(2,1)}, u32[]{:S(2)}, u32[]{:S(2)}) async-start(bf16[128,4,64,128]{3,2,1,0:T(8,128)(2,1)} %get-tuple-element.25), calls=%async_computation | async-start | bytes 16777216 | tf_op jit(solution)/shard_map/all_to_all | solution.py:313
  55.2 80.0 %collective-permute-start.6 = (bf16[1,128,128]{2,1,0:T(8,128)(2,1)S(1)}, bf16[1,128,128]{2,1,0:T(8,128)(2,1)S(1)}, u32[]{:S(2)}, u32[]{:S(2)}) collective-permute-start(bf16[1,128,128]{2,1,0:T(8,128)(2,1)S(1)} %get-tuple-element.39), channel_id=1, source_target_pairs={{0,1},{1,2},{2,3},{4,5},{5,6},{6,7},{8,9},{9,10},{10,11},{12,13},{... | collective-permute-start | bytes 98312 | tf_op jit(solution)/shard_map/ppermute | solution.py:281
  58.5 70.6 %collective-permute-start.4 = (f32[64,128]{1,0:T(8,128)}, f32[64,128]{1,0:T(8,128)S(1)}, u32[]{:S(2)}, u32[]{:S(2)}) collective-permute-start(f32[64,128]{1,0:T(8,128)} %get-tuple-element.27), channel_id=1, source_target_pairs={{0,124},{1,125},{2,126},{3,127},{4,0},{5,1},{6,2},{7,3},{8,4},{9,5... | collective-permute-start | bytes 98312 | tf_op jit(solution)/shard_map/ppermute | solution.py:281
  61.7 52.6 %collective-permute-start.3 = (f32[1,128]{1,0:T(1,128)S(1)}, f32[1,128]{1,0:T(1,128)S(1)}, u32[]{:S(2)}, u32[]{:S(2)}) collective-permute-start(f32[1,128]{1,0:T(1,128)S(1)} %get-tuple-element.41), channel_id=1, source_target_pairs={{0,125},{1,126},{2,127},{4,1},{5,2},{6,3},{8,5},{9,6},{10,7},{16,1... | collective-permute-start | bytes 1544 | tf_op jit(solution)/shard_map/ppermute | solution.py:281
  69.9 50.1 %collective-permute-start.5 = (f32[1,128]{1,0:T(1,128)S(1)}, f32[1,128]{1,0:T(1,128)S(1)}, u32[]{:S(2)}, u32[]{:S(2)}) collective-permute-start(f32[1,128]{1,0:T(1,128)S(1)} %get-tuple-element.42), channel_id=1, source_target_pairs={{1,124},{2,125},{3,126},{5,0},{6,1},{7,2},{9,4},{10,5},{11,6},{17,... | collective-permute-start | bytes 1544 | tf_op jit(solution)/shard_map/ppermute | solution.py:281
  71.2 63.4 %collective-permute-start.1 = (f32[64,128]{1,0:T(8,128)}, f32[64,128]{1,0:T(8,128)S(1)}, u32[]{:S(2)}, u32[]{:S(2)}) collective-permute-start(f32[64,128]{1,0:T(8,128)} %get-tuple-element.26), channel_id=1, source_target_pairs={{0,4},{1,5},{2,6},{3,7},{4,8},{5,9},{6,10},{7,11},{12,16},{13,17},... | collective-permute-start | bytes 98312 | tf_op jit(solution)/shard_map/ppermute | solution.py:281
  114.3 20.9 %collective-permute-start.7 = (bf16[1,128,128]{2,1,0:T(8,128)(2,1)S(1)}, bf16[1,128,128]{2,1,0:T(8,128)(2,1)S(1)}, u32[]{:S(2)}, u32[]{:S(2)}) collective-permute-start(bf16[1,128,128]{2,1,0:T(8,128)(2,1)S(1)} %get-tuple-element.40), channel_id=1, source_target_pairs={{1,0},{2,1},{3,2},{5,4},{6,5},{7,6},{9,8},{10,9},{11,10},{13,12},{... | collective-permute-start | bytes 98312 | tf_op jit(solution)/shard_map/ppermute | solution.py:281
  120.0 11.0 %collective-permute-start = (f32[1,128]{1,0:T(1,128)S(1)}, f32[1,128]{1,0:T(1,128)S(1)}, u32[]{:S(2)}, u32[]{:S(2)}) collective-permute-start(f32[1,128]{1,0:T(1,128)S(1)} %get-tuple-element.43), channel_id=1, source_target_pairs={{0,5},{1,6},{2,7},{4,9},{5,10},{6,11},{12,17},{13,18},{14,19},{16,... | collective-permute-start | bytes 1544 | tf_op jit(solution)/shard_map/ppermute | solution.py:281
  129.1 5.5 %collective-permute-start.2 = (f32[1,128]{1,0:T(1,128)S(1)}, f32[1,128]{1,0:T(1,128)S(1)}, u32[]{:S(2)}, u32[]{:S(2)}) collective-permute-start(f32[1,128]{1,0:T(1,128)S(1)} %get-tuple-element.44), channel_id=1, source_target_pairs={{1,4},{2,5},{3,6},{5,8},{6,9},{7,10},{13,16},{14,17},{15,18},{17,2... | collective-permute-start | bytes 1544 | tf_op jit(solution)/shard_map/ppermute | solution.py:281
  138.4 9.3 %copy-start.1 = (bf16[2048,128]{1,0:T(8,128)(2,1)S(1)}, bf16[2048,128]{1,0:T(8,128)(2,1)}, u32[]{:S(2)}) copy-start(bf16[2048,128]{1,0:T(8,128)(2,1)} %param.17) | copy-start | bytes 1572868
  138.4 9.3 %copy-start.2 = (bf16[32,64,128]{2,1,0:T(8,128)(2,1)S(1)}, bf16[32,64,128]{2,1,0:T(8,128)(2,1)}, u32[]{:S(2)}) copy-start(bf16[32,64,128]{2,1,0:T(8,128)(2,1)} %get-tuple-element.21) | copy-start | bytes 1572868
  138.4 62.6 %all-to-all-start.1 = ((bf16[128,2,64,128]{3,2,1,0:T(8,128)(2,1)}), bf16[128,2,64,128]{3,2,1,0:T(8,128)(2,1)}, u32[]{:S(2)}, u32[]{:S(2)}) async-start(bf16[128,2,64,128]{3,2,1,0:T(8,128)(2,1)} %bitcast.9), calls=%async_computation.1 | async-start | bytes 8388608 | tf_op jit(solution)/shard_map/all_to_all | solution.py:347
where the time goes:
time: 214 us; the launch traced here: 211 us
  Pallas kernels  77.4 us (36%)
  waiting for transfers between devices  72.3 us (34%)
  starting transfers between devices  50.1 us (23%)
  local copies, waits for them, and re-layouts  5.19 us (2%)
  other arithmetic  4.45 us (2%)
    ppermute x8, waiting for transfers between devices, shifted(): return lax.ppermute(block, ('tile', 'cam'), pairs)  48.5 us
    pallas_call x1, Pallas kernels, pixel_part(): pl.pallas_call(pixel_kernel, grid_spec=pltpu.PrefetchScalarGridSpec(num_s...  29 us
    ppermute x8, starting transfers between devices, shifted(): return lax.ppermute(block, ('tile', 'cam'), pairs)  28.8 us
    pallas_call x1, Pallas kernels, main_part(): pl.pallas_call(main_kernel, grid_spec=pltpu.PrefetchScalarGridSpec(num_sc...  28.1 us
    all_to_all x1, waiting for transfers between devices, per_device(): lax.all_to_all(sums.reshape(devices, CAP, BS, C), ('tile', 'cam'), split_...  23.8 us
    all_to_all x1, starting transfers between devices, per_device(): lax.all_to_all(outgoing, ('tile', 'cam'), split_axis=0, concat_axis=0, ti...  12 us
    pallas_call x1, Pallas kernels, return_part(): pl.pallas_call(return_kernel, grid_spec=pltpu.PrefetchScalarGridSpec(num_...  10.5 us
    pallas_call x1, Pallas kernels, pack(): pl.pallas_call(pack_kernel, grid_spec=pltpu.PrefetchScalarGridSpec(num_sc...  9.86 us
  transfers between devices with their start and end apart: 10, of which 4 were waited for; matrix products, arithmetic and copies ran while one was open for 4% of the time, Pallas kernels for 27%

commit v1 on v0

--- a/solution.py
+++ b/solution.py
@@ -19,47 +19,55 @@
 STRIPS = 4
 MIB = 1024 * 1024
 VMEM = 60 * MIB
-DESTS = 8
-OWNERS = 8
+DESTS = 16
+OWNERS = 16
+SPREAD = 4
 
 
 def slope_of(upstream, hidden):
     argument = hidden.astype(jnp.float32)
-    logistic = jax.nn.sigmoid(argument)
+    logistic = 0.5 + 0.5 * jnp.tanh(0.5 * argument)
     slope = logistic * (1.0 + argument * (1.0 - logistic))
     return (upstream.astype(jnp.float32) * slope).astype(jnp.bfloat16)
 
 
-def pack_kernel(targets, points, hidden, upstream, out, slope):
+def pack_kernel(targets, points, hidden, upstream, out, slope_out, slope):
     step = pl.program_id(0)
-
-    @pl.when(step == 0)
-    def _():
-        def body(b, carry):
-            slope[b] = slope_of(upstream[b], hidden[b])
-            return carry
-
-        lax.fori_loop(0, BLK_DEV, body, 0)
-
-    for d in range(DESTS):
-        for s in range(CAP):
-            block = targets[(step * DESTS + d) * CAP + s]
-            out[d, s] = points[block]
-            out[d, CAP + s] = slope[block]
+    half = pl.num_programs(0) // 2
+    count = hidden.shape[0]
+
+    def fill(source, first):
+        for d in range(DESTS):
+            for s in range(CAP):
+                out[d, s] = source[targets[0, s, first + d]]
+
+    @pl.when(step < half)
+    def _():
+        values = slope_of(upstream[...], hidden[...])
+        slope[pl.ds(step * count, count)] = values
+        slope_out[...] = values
+        fill(points, step * DESTS)
+
+    @pl.when(step >= half)
+    def _():
+        fill(slope, (step - half) * DESTS)
 
 
 def pack(targets, points, hidden, upstream, devices):
-    whole = pl.BlockSpec((BLK_DEV, BS, C), lambda i, t: (0, 0, 0))
+    half = devices // DESTS
+    count = BLK_DEV // half
+    part = pl.BlockSpec((count, BS, C), lambda i, t: (jnp.minimum(i, half - 1), 0, 0))
     return pl.pallas_call(
         pack_kernel,
         grid_spec=pltpu.PrefetchScalarGridSpec(
             num_scalar_prefetch=1,
-            grid=(devices // DESTS,),
-            in_specs=[whole, whole, whole],
+            grid=(2 * half,),
+            in_specs=[pl.BlockSpec((BLK_DEV, BS, C), lambda i, t: (0, 0, 0)), part, part],
             out_specs=[
-                pl.BlockSpec((DESTS, 2 * CAP, BS, C), lambda i, t: (i, 0, 0, 0)),
-                whole,
-            ],
+                pl.BlockSpec((DESTS, CAP, BS, C), lambda i, t: (i % half, i // half, 0, 0)),
+                part,
+            ],
+            scratch_shapes=[pltpu.VMEM((BLK_DEV, BS, C), jnp.bfloat16)],
         ),
         out_shape=[
             jax.ShapeDtypeStruct((devices, 2 * CAP, BS, C), jnp.bfloat16),
@@ -97,7 +105,7 @@
         mixing[0], projected, (((0,), (0,)), ((), ())), preferred_element_type=jnp.float32
     )
     for k in range(K):
-        slot = neighbors[q * K + k]
+        slot = neighbors[k, q]
         total[slot] += term[k * BS : (k + 1) * BS]
 
     @pl.when(q == PB - 1)
@@ -152,7 +160,7 @@
 ):
     q = pl.program_id(0)
     for k in range(K):
-        slot = neighbors[q * K + k]
+        slot = neighbors[k, q]
         owner = lax.div(slot, CAP)
         place = lax.rem(slot, CAP)
         right_side[k * BS : (k + 1) * BS, 0:C] = incoming[owner, place]
@@ -231,21 +239,26 @@
     )(neighbors, incoming, mixed, pixels, mixing, upstream, padded, left, right, kernel)
 
 
-def return_kernel(targets, received, base, out, total):
+def return_kernel(targets, received, base, out, *totals):
     step = pl.program_id(0)
 
     @pl.when(step == 0)
     def _():
-        total[...] = base[...]
+        totals[0][...] = base[...]
+        for total in totals[1:]:
+            total[...] = jnp.zeros_like(total)
 
     for o in range(OWNERS):
         for s in range(CAP):
-            block = targets[(step * OWNERS + o) * CAP + s]
-            total[block] += received[o, s].astype(jnp.float32)
+            block = targets[0, s, step * OWNERS + o]
+            totals[(o * CAP + s) % SPREAD][block] += received[o, s].astype(jnp.float32)
 
     @pl.when(step == pl.num_programs(0) - 1)
     def _():
-        out[...] = total[...].astype(jnp.bfloat16)
+        whole = totals[0][...]
+        for total in totals[1:]:
+            whole = whole + total[...]
+        out[...] = whole.astype(jnp.bfloat16)
 
 
 def return_part(targets, received, base):
@@ -261,7 +274,7 @@
                 whole,
             ],
             out_specs=whole,
-            scratch_shapes=[pltpu.VMEM((BLK_DEV, BS, C), jnp.float32)],
+            scratch_shapes=[pltpu.VMEM((BLK_DEV, BS, C), jnp.float32)] * SPREAD,
         ),
         out_shape=jax.ShapeDtypeStruct((BLK_DEV, BS, C), jnp.bfloat16),
         compiler_params=pltpu.CompilerParams(vmem_limit_bytes=VMEM),
@@ -299,9 +312,12 @@
     cams = lax.axis_size("cam")
     devices = tiles * cams
     slots = devices * CAP
-    targets = send_list.reshape(-1)
-    reads = neighbors.reshape(-1)
+    targets = jnp.transpose(send_list, (0, 2, 1))
+    reads = neighbors.T
     blocks = (BLK_DEV, BS, C)
+    move = functools.partial(shifted, tiles=tiles, cams=cams)
+    above = move(slope_of(pixel_upstream[-1:], pixel_hidden[-1:]), tile_step=0, cam_step=1)
+    below = move(slope_of(pixel_upstream[:1], pixel_hidden[:1]), tile_step=0, cam_step=-1)
     outgoing, point_slope = pack(
         targets,
         points.reshape(blocks),
@@ -309,38 +325,22 @@
         point_upstream.reshape(blocks),
         devices,
     )
-    outgoing, reads = lax.optimization_barrier((outgoing, reads))
+    outgoing, reads, above, below = lax.optimization_barrier((outgoing, reads, above, below))
     incoming = lax.all_to_all(
         outgoing, ("tile", "cam"), split_axis=0, concat_axis=0, tiled=True
     )
     pixel_slope, mixed, sums, first, last = pixel_part(
         reads, pixel_hidden, pixel_upstream, mixing, pixel_weight, slots
     )
-    move = functools.partial(shifted, tiles=tiles, cams=cams)
-    rim_left = jnp.concatenate(
-        [
-            move(last[-1:], tile_step=1, cam_step=1),
-            move(last, tile_step=1, cam_step=0),
-            move(last[:1], tile_step=1, cam_step=-1),
-        ],
-        axis=0,
-    )
-    rim_right = jnp.concatenate(
-        [
-            move(first[-1:], tile_step=-1, cam_step=1),
-            move(first, tile_step=-1, cam_step=0),
-            move(first[:1], tile_step=-1, cam_step=-1),
-        ],
-        axis=0,
-    )
-    padded = jnp.concatenate(
-        [
-            move(pixel_slope[-1:], tile_step=0, cam_step=1),
-            pixel_slope,
-            move(pixel_slope[:1], tile_step=0, cam_step=-1),
-        ],
-        axis=0,
-    )
+    padded = jnp.concatenate([above, pixel_slope, below], axis=0)
+    first = jnp.concatenate(
+        [above[:, 0].astype(jnp.float32), first, below[:, 0].astype(jnp.float32)], axis=0
+    )
+    last = jnp.concatenate(
+        [above[:, -1].astype(jnp.float32), last, below[:, -1].astype(jnp.float32)], axis=0
+    )
+    rim_left = move(last, tile_step=1, cam_step=0)
+    rim_right = move(first, tile_step=-1, cam_step=0)
     sums, incoming, rim_left, rim_right, padded = lax.optimization_barrier(
         (sums, incoming, rim_left, rim_right, padded)
     )

time: 214 us -> 201 us (0.939)
  starting transfers between devices: 50.1 us -> 29.1 us
  waiting for transfers between devices: 72.3 us -> 87.3 us
  local copies, waits for them, and re-layouts: 5.19 us -> 0.02 us
  Pallas kernels: 77.4 us -> 74.6 us
    all_to_all x1, waiting for transfers between devices: 0.01 us -> 54.7 us  [per_device(): lax.all_to_all(outgoing, ('tile', 'cam'), split_axis=0, concat_axis=0, ti...]
    ppermute x8 -> x4, waiting for transfers between devices: 48.5 us -> 9.11 us  [shifted(): return lax.ppermute(block, ('tile', 'cam'), pairs)]
    ppermute x8 -> x4, starting transfers between devices: 28.8 us -> 10.8 us  [shifted(): return lax.ppermute(block, ('tile', 'cam'), pairs)]
    all_to_all x1, starting transfers between devices: 9.31 us -> 5.76 us  [per_device(): lax.all_to_all(sums.reshape(devices, CAP, BS, C), ('tile', 'cam'), split_...]
    pallas_call x1, Pallas kernels: 10.5 us -> 7.11 us  [return_part(): pl.pallas_call(return_kernel, grid_spec=pltpu.PrefetchScalarGridSpec(num_...]
    slice x3 -> x0, local copies, waits for them, and re-layouts: 2.21 us -> none  [the longest x1 0.78 us: per_device(): pixel_slope[-1:]]
  transfers between devices with their start and end apart: 10 -> 6, of which waited for: 4 -> 4; matrix products, arithmetic and copies ran while one was open for 4% -> 3% of each run, Pallas kernels for 27% -> 34%
where the time goes in v1:
time: 201 us; the launch traced here: 199 us
  waiting for transfers between devices  87.3 us (43%)
  Pallas kernels  74.6 us (37%)
  starting transfers between devices  29.1 us (14%)
  other arithmetic  5.65 us (3%)
    all_to_all x1, waiting for transfers between devices, per_device(): lax.all_to_all(outgoing, ('tile', 'cam'), split_axis=0, concat_axis=0, ti...  54.7 us
    pallas_call x1, Pallas kernels, pixel_part(): pl.pallas_call(pixel_kernel, grid_spec=pltpu.PrefetchScalarGridSpec(num_s...  29 us
    pallas_call x1, Pallas kernels, main_part(): pl.pallas_call(main_kernel, grid_spec=pltpu.PrefetchScalarGridSpec(num_sc...  28.2 us
    all_to_all x1, waiting for transfers between devices, per_device(): lax.all_to_all(sums.reshape(devices, CAP, BS, C), ('tile', 'cam'), split_...  23.5 us
    all_to_all x1, starting transfers between devices, per_device(): lax.all_to_all(outgoing, ('tile', 'cam'), split_axis=0, concat_axis=0, ti...  12.6 us
    ppermute x4, starting transfers between devices, shifted(): return lax.ppermute(block, ('tile', 'cam'), pairs)  10.8 us
    pallas_call x1, Pallas kernels, pack(): pl.pallas_call(pack_kernel, grid_spec=pltpu.PrefetchScalarGridSpec(num_sc...  10.3 us
    ppermute x4, waiting for transfers between devices, shifted(): return lax.ppermute(block, ('tile', 'cam'), pairs)  9.11 us
  transfers between devices with their start and end apart: 6, of which 4 were waited for; matrix products, arithmetic and copies ran while one was open for 3% of the time, Pallas kernels for 34%

profile of v1, /device:TPU:1, one launch (start us, length us, event | category | flops | bytes accessed | tf_op | source)
XLA Modules:
  0.0 198.8 jit_solution(14439286242345268643)
XLA Ops:
  0.6 0.0 copy-start
  0.6 0.9 fusion.14
  1.5 3.9 %collective-permute-start = (bf16[1,128,128]{2,1,0:T(8,128)(2,1)S(1)}, bf16[1,128,128]{2,1,0:T(8,128)(2,1)S(1)}, u32[]{:S(2)}, u32[]{:S(2)}) collective-permute-start(bf16[1,128,128]{2,1,0:T(8,128)(2,1)S(1)} %get-tuple-element.44), channel_id=1, source_target_pairs={{0,1},{1,2},{2,3},{4,5},{5,6},{6,7},{8,9},{9,10},{10,11},{12,13},{... | collective-permute-start | bytes 98312 | tf_op jit(solution)/shard_map/ppermute | solution.py:294
  5.5 1.3 collective-permute-start.1
  6.8 10.3 %pack.1 = (bf16[128,4,64,128]{3,2,1,0:T(8,128)(2,1)}, bf16[32,64,128]{2,1,0:T(8,128)(2,1)}) custom-call(s32[1,2,128]{2,1,0:T(2,128)} %bitcast.32, bf16[32,64,128]{2,1,0:T(8,128)(2,1)} %bitcast.27, bf16[32,64,128]{2,1,0:T(8,128)(2,1)} %bitcast.28, bf16[32,64,128]{2,1,0:T(8,128)(2,1)} %bitcast.25), custom_call_target="tpu_custom_call" | custom-call | flops 10485760 | bytes 12582912 | tf_op jit(solution)/shard_map/pack/pallas_call | solution.py:60
  17.1 0.0 collective-permute-done
  17.1 0.0 collective-permute-done.1
  17.1 12.6 %all-to-all-start = ((bf16[128,4,64,128]{3,2,1,0:T(8,128)(2,1)}), bf16[128,4,64,128]{3,2,1,0:T(8,128)(2,1)}, u32[]{:S(2)}, u32[]{:S(2)}) async-start(bf16[128,4,64,128]{3,2,1,0:T(8,128)(2,1)} %get-tuple-element.27), calls=%async_computation | async-start | bytes 16777216 | tf_op jit(solution)/shard_map/all_to_all | solution.py:329
  29.7 29.0 %pixel_part.1 = (bf16[64,128,128]{2,1,0:T(8,128)(2,1)}, bf16[32,256,128]{2,1,0:T(8,128)(2,1)}, bf16[256,64,128]{2,1,0:T(8,128)(2,1)}, f32[64,128]{1,0:T(8,128)}, f32[64,128]{1,0:T(8,128)}) custom-call(s32[6,32]{1,0:T(8,128)} %bitcast.30, bf16[64,128,128]{2,1,0:T(8,128)(2,1)} %hidden.1, bf16[64,128,128]{2,1,0:T(8,128)(2,1)} %upstream.3, ...), custom_call_target="tpu_custom_call" | custom-call | flops 1258291200 | bytes 18874368 | tf_op jit(solution)/shard_map/pixel_part/pallas_call | solution.py:122
  58.7 0.8 pad_maximum_fusion.2
  59.5 3.0 %collective-permute-start.3 = (f32[66,128]{1,0:T(8,128)S(1)}, f32[66,128]{1,0:T(8,128)S(1)}, u32[]{:S(2)}, u32[]{:S(2)}) collective-permute-start(f32[66,128]{1,0:T(8,128)S(1)} %pad_maximum_fusion.2), channel_id=1, source_target_pairs={{0,124},{1,125},{2,126},{3,127},{4,0},{5,1},{6,2},{7,3},{8,4},{9,5... | collective-permute-start | bytes 101384 | tf_op jit(solution)/shard_map/ppermute | solution.py:294
  62.5 0.8 pad_maximum_fusion.1
  63.3 2.5 %collective-permute-start.2 = (f32[66,128]{1,0:T(8,128)S(1)}, f32[66,128]{1,0:T(8,128)S(1)}, u32[]{:S(2)}, u32[]{:S(2)}) collective-permute-start(f32[66,128]{1,0:T(8,128)S(1)} %pad_maximum_fusion.1), channel_id=1, source_target_pairs={{0,4},{1,5},{2,6},{3,7},{4,8},{5,9},{6,10},{7,11},{12,16},{13,17},... | collective-permute-start | bytes 101384 | tf_op jit(solution)/shard_map/ppermute | solution.py:294
  65.8 3.2 %pad_maximum_fusion.padded = bf16[66,128,128]{2,1,0:T(8,128)(2,1)} fusion(bf16[1,128,128]{2,1,0:T(8,128)(2,1)S(1)} %collective-permute-done.1, bf16[64,128,128]{2,1,0:T(8,128)(2,1)} %get-tuple-element.32, bf16[1,128,128]{2,1,0:T(8,128)(2,1)S(1)} %collective-permute-done), kind=kLoop, calls=%fused_computation.1 | loop fusion | flops 2162688 | bytes 4325376 | tf_op jit(solution)/shard_map/concatenate | solution.py:335
  69.0 5.7 %collective-permute-done.3.right = f32[66,128]{1,0:T(8,128)S(1)} collective-permute-done((f32[66,128]{1,0:T(8,128)S(1)}, f32[66,128]{1,0:T(8,128)S(1)}, u32[]{:S(2)}, u32[]{:S(2)}) %collective-permute-start.3) | collective-permute-done | bytes 33824 | tf_op jit(solution)/shard_map/ppermute | solution.py:294
  74.7 0.0 copy-start.3
  74.7 3.4 %collective-permute-done.2.left = f32[66,128]{1,0:T(8,128)S(1)} collective-permute-done((f32[66,128]{1,0:T(8,128)S(1)}, f32[66,128]{1,0:T(8,128)S(1)}, u32[]{:S(2)}, u32[]{:S(2)}) %collective-permute-start.2) | collective-permute-done | bytes 33824 | tf_op jit(solution)/shard_map/ppermute | solution.py:294
  78.1 0.0 copy-start.4
  78.1 54.7 %all-to-all-done.incoming = bf16[128,4,64,128]{3,2,1,0:T(8,128)(2,1)} async-done(((bf16[128,4,64,128]{3,2,1,0:T(8,128)(2,1)}), bf16[128,4,64,128]{3,2,1,0:T(8,128)(2,1)}, u32[]{:S(2)}, u32[]{:S(2)}) %all-to-all-start) | async-done | bytes 8388640 | tf_op jit(solution)/shard_map/all_to_all | solution.py:329
  132.9 0.0 copy-start.1
  132.9 0.0 copy-start.2
  132.9 0.0 copy-done.3
  132.9 0.0 copy-done.4
  132.9 5.8 %all-to-all-start.1 = ((bf16[128,2,64,128]{3,2,1,0:T(8,128)(2,1)}), bf16[128,2,64,128]{3,2,1,0:T(8,128)(2,1)}, u32[]{:S(2)}, u32[]{:S(2)}) async-start(bf16[128,2,64,128]{3,2,1,0:T(8,128)(2,1)} %bitcast.23), calls=%async_computation.1 | async-start | bytes 8388608 | tf_op jit(solution)/shard_map/all_to_all | solution.py:347
  138.6 0.0 copy-done
  138.6 0.0 copy-done.1
  138.7 0.0 copy-done.2
  138.7 1.3 convolution_add_fusion
  140.0 28.2 %main_part.1 = (bf16[32,256,384]{2,1,0:T(8,128)(2,1)}, bf16[64,128,128]{2,1,0:T(8,128)(2,1)}) custom-call(s32[6,32]{1,0:T(8,128)} %bitcast.31, bf16[128,4,64,128]{3,2,1,0:T(8,128)(2,1)} %all-to-all-done.incoming, bf16[32,256,128]{2,1,0:T(8,128)(2,1)} %get-tuple-element.34.mixed, bf16[64,128,128]{2,1,0:T(8,128)(2,1)} %pixels.1, bf16[32,256,384]{2,1,0:T(8,128)(2,1)} %mixing.3, ...), custom_call_target="tpu_custom_call" | custom-call | flops 2726297600 | bytes 31457280 | tf_op jit(solution)/shard_map/main_part/pallas_call | solution.py:205
  168.2 23.5 %all-to-all-done.1.received = bf16[128,2,64,128]{3,2,1,0:T(8,128)(2,1)} async-done(((bf16[128,2,64,128]{3,2,1,0:T(8,128)(2,1)}), bf16[128,2,64,128]{3,2,1,0:T(8,128)(2,1)}, u32[]{:S(2)}, u32[]{:S(2)}) %all-to-all-start.1) | async-done | bytes 4194336 | tf_op jit(solution)/shard_map/all_to_all | solution.py:347
  191.7 7.1 %return_part.1 = bf16[32,64,128]{2,1,0:T(8,128)(2,1)} custom-call(s32[1,2,128]{2,1,0:T(2,128)} %bitcast.33, bf16[128,2,64,128]{3,2,1,0:T(8,128)(2,1)} %all-to-all-done.1.received, f32[32,64,128]{2,1,0:T(8,128)} %bitcast.24), custom_call_target="tpu_custom_call" | custom-call | flops 4194304 | bytes 6291456 | tf_op jit(solution)/shard_map/return_part/pallas_call | solution.py:267
  (1 shorter events, 0.0 us)
Async XLA Ops:
  0.6 138.0 %copy-start = (bf16[128,128]{1,0:T(8,128)(2,1)S(1)}, bf16[128,128]{1,0:T(8,128)(2,1)}, u32[]{:S(2)}) copy-start(bf16[128,128]{1,0:T(8,128)(2,1)} %param.22) | copy-start | bytes 98308
  1.5 15.6 %collective-permute-start = (bf16[1,128,128]{2,1,0:T(8,128)(2,1)S(1)}, bf16[1,128,128]{2,1,0:T(8,128)(2,1)S(1)}, u32[]{:S(2)}, u32[]{:S(2)}) collective-permute-start(bf16[1,128,128]{2,1,0:T(8,128)(2,1)S(1)} %get-tuple-element.44), channel_id=1, source_target_pairs={{0,1},{1,2},{2,3},{4,5},{5,6},{6,7},{8,9},{9,10},{10,11},{12,13},{... | collective-permute-start | bytes 98312 | tf_op jit(solution)/shard_map/ppermute | solution.py:294
  5.5 11.6 %collective-permute-start.1 = (bf16[1,128,128]{2,1,0:T(8,128)(2,1)S(1)}, bf16[1,128,128]{2,1,0:T(8,128)(2,1)S(1)}, u32[]{:S(2)}, u32[]{:S(2)}) collective-permute-start(bf16[1,128,128]{2,1,0:T(8,128)(2,1)S(1)} %get-tuple-element.43), channel_id=1, source_target_pairs={{1,0},{2,1},{3,2},{5,4},{6,5},{7,6},{9,8},{10,9},{11,10},{13,12},{... | collective-permute-start | bytes 98312 | tf_op jit(solution)/shard_map/ppermute | solution.py:294
  17.1 115.7 %all-to-all-start = ((bf16[128,4,64,128]{3,2,1,0:T(8,128)(2,1)}), bf16[128,4,64,128]{3,2,1,0:T(8,128)(2,1)}, u32[]{:S(2)}, u32[]{:S(2)}) async-start(bf16[128,4,64,128]{3,2,1,0:T(8,128)(2,1)} %get-tuple-element.27), calls=%async_computation | async-start | bytes 16777216 | tf_op jit(solution)/shard_map/all_to_all | solution.py:329
  59.5 15.3 %collective-permute-start.3 = (f32[66,128]{1,0:T(8,128)S(1)}, f32[66,128]{1,0:T(8,128)S(1)}, u32[]{:S(2)}, u32[]{:S(2)}) collective-permute-start(f32[66,128]{1,0:T(8,128)S(1)} %pad_maximum_fusion.2), channel_id=1, source_target_pairs={{0,124},{1,125},{2,126},{3,127},{4,0},{5,1},{6,2},{7,3},{8,4},{9,5... | collective-permute-start | bytes 101384 | tf_op jit(solution)/shard_map/ppermute | solution.py:294
  63.3 14.9 %collective-permute-start.2 = (f32[66,128]{1,0:T(8,128)S(1)}, f32[66,128]{1,0:T(8,128)S(1)}, u32[]{:S(2)}, u32[]{:S(2)}) collective-permute-start(f32[66,128]{1,0:T(8,128)S(1)} %pad_maximum_fusion.1), channel_id=1, source_target_pairs={{0,4},{1,5},{2,6},{3,7},{4,8},{5,9},{6,10},{7,11},{12,16},{13,17},... | collective-permute-start | bytes 101384 | tf_op jit(solution)/shard_map/ppermute | solution.py:294
  74.7 58.1 %copy-start.3 = (f32[66,128]{1,0:T(8,128)}, f32[66,128]{1,0:T(8,128)S(1)}, u32[]{:S(2)}) copy-start(f32[66,128]{1,0:T(8,128)S(1)} %collective-permute-done.3.right) | copy-start | bytes 101380
  78.1 54.7 %copy-start.4 = (f32[66,128]{1,0:T(8,128)}, f32[66,128]{1,0:T(8,128)S(1)}, u32[]{:S(2)}) copy-start(f32[66,128]{1,0:T(8,128)S(1)} %collective-permute-done.2.left) | copy-start | bytes 101380
  132.9 5.8 %copy-start.1 = (bf16[2048,128]{1,0:T(8,128)(2,1)S(1)}, bf16[2048,128]{1,0:T(8,128)(2,1)}, u32[]{:S(2)}) copy-start(bf16[2048,128]{1,0:T(8,128)(2,1)} %param.17) | copy-start | bytes 1572868
  132.9 5.8 %copy-start.2 = (bf16[32,64,128]{2,1,0:T(8,128)(2,1)S(1)}, bf16[32,64,128]{2,1,0:T(8,128)(2,1)}, u32[]{:S(2)}) copy-start(bf16[32,64,128]{2,1,0:T(8,128)(2,1)} %get-tuple-element.23) | copy-start | bytes 1572868
  132.9 58.9 %all-to-all-start.1 = ((bf16[128,2,64,128]{3,2,1,0:T(8,128)(2,1)}), bf16[128,2,64,128]{3,2,1,0:T(8,128)(2,1)}, u32[]{:S(2)}, u32[]{:S(2)}) async-start(bf16[128,2,64,128]{3,2,1,0:T(8,128)(2,1)} %bitcast.23), calls=%async_computation.1 | async-start | bytes 8388608 | tf_op jit(solution)/shard_map/all_to_all | solution.py:347

commit v2 on v1

--- a/solution.py
+++ b/solution.py
@@ -19,7 +19,7 @@
 STRIPS = 4
 MIB = 1024 * 1024
 VMEM = 60 * MIB
-DESTS = 16
+DESTS = 4
 OWNERS = 16
 SPREAD = 4
 
@@ -31,48 +31,40 @@
     return (upstream.astype(jnp.float32) * slope).astype(jnp.bfloat16)
 
 
-def pack_kernel(targets, points, hidden, upstream, out, slope_out, slope):
-    step = pl.program_id(0)
-    half = pl.num_programs(0) // 2
-    count = hidden.shape[0]
-
-    def fill(source, first):
-        for d in range(DESTS):
-            for s in range(CAP):
-                out[d, s] = source[targets[0, s, first + d]]
-
-    @pl.when(step < half)
-    def _():
-        values = slope_of(upstream[...], hidden[...])
-        slope[pl.ds(step * count, count)] = values
-        slope_out[...] = values
-        fill(points, step * DESTS)
-
-    @pl.when(step >= half)
-    def _():
-        fill(slope, (step - half) * DESTS)
+def pack_kernel(targets, points, hidden, upstream, out, slope, sem):
+    def send(source, first):
+        def body(i, carry):
+            for j in range(DESTS):
+                d = i * DESTS + j
+                for s in range(CAP):
+                    block = source.at[targets[0, s, d]]
+                    pltpu.make_async_copy(block, out.at[d, first + s], sem).start()
+            return carry
+
+        lax.fori_loop(0, out.shape[0] // DESTS, body, 0)
+
+    def fill(i, carry):
+        part = pl.ds(2 * i, 2)
+        slope[part] = slope_of(upstream[part], hidden[part])
+        return carry
+
+    send(points, 0)
+    lax.fori_loop(0, BLK_DEV // 2, fill, 0)
+    send(slope, CAP)
+    pltpu.make_async_copy(out, out, sem).wait()
 
 
 def pack(targets, points, hidden, upstream, devices):
-    half = devices // DESTS
-    count = BLK_DEV // half
-    part = pl.BlockSpec((count, BS, C), lambda i, t: (jnp.minimum(i, half - 1), 0, 0))
+    whole = pl.BlockSpec(memory_space=pltpu.VMEM)
     return pl.pallas_call(
         pack_kernel,
-        grid_spec=pltpu.PrefetchScalarGridSpec(
-            num_scalar_prefetch=1,
-            grid=(2 * half,),
-            in_specs=[pl.BlockSpec((BLK_DEV, BS, C), lambda i, t: (0, 0, 0)), part, part],
-            out_specs=[
-                pl.BlockSpec((DESTS, CAP, BS, C), lambda i, t: (i % half, i // half, 0, 0)),
-                part,
-            ],
-            scratch_shapes=[pltpu.VMEM((BLK_DEV, BS, C), jnp.bfloat16)],
-        ),
+        in_specs=[pl.BlockSpec(memory_space=pltpu.SMEM), whole, whole, whole],
+        out_specs=[pl.BlockSpec(memory_space=pl.ANY), whole],
         out_shape=[
             jax.ShapeDtypeStruct((devices, 2 * CAP, BS, C), jnp.bfloat16),
             jax.ShapeDtypeStruct((BLK_DEV, BS, C), jnp.bfloat16),
         ],
+        scratch_shapes=[pltpu.SemaphoreType.DMA(())],
         compiler_params=pltpu.CompilerParams(vmem_limit_bytes=VMEM),
         cost_estimate=pl.CostEstimate(flops=10 * MIB, bytes_accessed=12 * MIB, transcendentals=0),
         name="pack",
@@ -239,43 +231,50 @@
     )(neighbors, incoming, mixed, pixels, mixing, upstream, padded, left, right, kernel)
 
 
-def return_kernel(targets, received, base, out, *totals):
-    step = pl.program_id(0)
-
-    @pl.when(step == 0)
-    def _():
-        totals[0][...] = base[...]
-        for total in totals[1:]:
-            total[...] = jnp.zeros_like(total)
-
-    for o in range(OWNERS):
-        for s in range(CAP):
-            block = targets[0, s, step * OWNERS + o]
-            totals[(o * CAP + s) % SPREAD][block] += received[o, s].astype(jnp.float32)
-
-    @pl.when(step == pl.num_programs(0) - 1)
-    def _():
-        whole = totals[0][...]
-        for total in totals[1:]:
-            whole = whole + total[...]
-        out[...] = whole.astype(jnp.bfloat16)
+def return_kernel(targets, received, base, out, landed, sems, *totals):
+    parts = received.shape[0] // OWNERS
+
+    def fetch(i):
+        part = pl.ds(i * OWNERS, OWNERS)
+        return pltpu.make_async_copy(received.at[part], landed.at[part], sems.at[i])
+
+    for i in range(parts):
+        fetch(i).start()
+    totals[0][...] = base[...]
+    for total in totals[1:]:
+        total[...] = jnp.zeros_like(total)
+
+    def body(i, carry):
+        fetch(i).wait()
+        for j in range(OWNERS):
+            for s in range(CAP):
+                o = i * OWNERS + j
+                block = targets[0, s, o]
+                totals[(j * CAP + s) % SPREAD][block] += landed[o, s].astype(jnp.float32)
+        return carry
+
+    lax.fori_loop(0, parts, body, 0)
+    whole = totals[0][...]
+    for total in totals[1:]:
+        whole = whole + total[...]
+    out[...] = whole.astype(jnp.bfloat16)
 
 
 def return_part(targets, received, base):
-    devices = received.shape[0]
-    whole = pl.BlockSpec((BLK_DEV, BS, C), lambda i, t: (0, 0, 0))
+    whole = pl.BlockSpec(memory_space=pltpu.VMEM)
     return pl.pallas_call(
         return_kernel,
-        grid_spec=pltpu.PrefetchScalarGridSpec(
-            num_scalar_prefetch=1,
-            grid=(devices // OWNERS,),
-            in_specs=[
-                pl.BlockSpec((OWNERS, CAP, BS, C), lambda i, t: (i, 0, 0, 0)),
-                whole,
-            ],
-            out_specs=whole,
-            scratch_shapes=[pltpu.VMEM((BLK_DEV, BS, C), jnp.float32)] * SPREAD,
-        ),
+        in_specs=[
+            pl.BlockSpec(memory_space=pltpu.SMEM),
+            pl.BlockSpec(memory_space=pl.ANY),
+            whole,
+        ],
+        out_specs=whole,
+        scratch_shapes=[
+            pltpu.VMEM(received.shape, jnp.bfloat16),
+            pltpu.SemaphoreType.DMA((received.shape[0] // OWNERS,)),
+        ]
+        + [pltpu.VMEM((BLK_DEV, BS, C), jnp.float32)] * SPREAD,
         out_shape=jax.ShapeDtypeStruct((BLK_DEV, BS, C), jnp.bfloat16),
         compiler_params=pltpu.CompilerParams(vmem_limit_bytes=VMEM),
         cost_estimate=pl.CostEstimate(flops=4 * MIB, bytes_accessed=6 * MIB, transcendentals=0),

time: 201 us -> 193 us (0.960)
  Pallas kernels: 74.6 us -> 67 us
    pallas_call x2, Pallas kernels: 17.4 us -> 9.87 us  [the longest x1 5.36 us: pack(): pl.pallas_call(pack_kernel, in_specs=[pl.BlockSpec(memory_space=pltpu.SME...]
  transfers between devices with their start and end apart: 6 -> 6, of which waited for: 4 -> 4; matrix products, arithmetic and copies ran while one was open for 3% -> 3% of each run, Pallas kernels for 34% -> 33%
where the time goes in v2:
time: 193 us; the launch traced here: 191 us
  waiting for transfers between devices  87.4 us (45%)
  Pallas kernels  67 us (35%)
  starting transfers between devices  29.1 us (15%)
  other arithmetic  5.65 us (3%)
    all_to_all x1, waiting for transfers between devices, per_device(): lax.all_to_all(outgoing, ('tile', 'cam'), split_axis=0, concat_axis=0, ti...  54.7 us
    pallas_call x1, Pallas kernels, pixel_part(): pl.pallas_call(pixel_kernel, grid_spec=pltpu.PrefetchScalarGridSpec(num_s...  29 us
    pallas_call x1, Pallas kernels, main_part(): pl.pallas_call(main_kernel, grid_spec=pltpu.PrefetchScalarGridSpec(num_sc...  28.2 us
    all_to_all x1, waiting for transfers between devices, per_device(): lax.all_to_all(sums.reshape(devices, CAP, BS, C), ('tile', 'cam'), split_...  23.6 us
    all_to_all x1, starting transfers between devices, per_device(): lax.all_to_all(outgoing, ('tile', 'cam'), split_axis=0, concat_axis=0, ti...  12.6 us
    ppermute x4, starting transfers between devices, shifted(): return lax.ppermute(block, ('tile', 'cam'), pairs)  10.8 us
    ppermute x4, waiting for transfers between devices, shifted(): return lax.ppermute(block, ('tile', 'cam'), pairs)  9.11 us
    all_to_all x1, starting transfers between devices, per_device(): lax.all_to_all(sums.reshape(devices, CAP, BS, C), ('tile', 'cam'), split_...  5.71 us
  transfers between devices with their start and end apart: 6, of which 4 were waited for; matrix products, arithmetic and copies ran while one was open for 3% of the time, Pallas kernels for 33%

profile of v2, /device:TPU:1, one launch (start us, length us, event | category | flops | bytes accessed | tf_op | source)
XLA Modules:
  0.0 191.2 jit_solution(4155518336391577089)
XLA Ops:
  0.6 0.0 copy-start
  0.6 0.9 fusion.14
  1.5 3.9 %collective-permute-start = (bf16[1,128,128]{2,1,0:T(8,128)(2,1)S(1)}, bf16[1,128,128]{2,1,0:T(8,128)(2,1)S(1)}, u32[]{:S(2)}, u32[]{:S(2)}) collective-permute-start(bf16[1,128,128]{2,1,0:T(8,128)(2,1)S(1)} %get-tuple-element.44), channel_id=1, source_target_pairs={{0,1},{1,2},{2,3},{4,5},{5,6},{6,7},{8,9},{9,10},{10,11},{12,13},{... | collective-permute-start | bytes 98312 | tf_op jit(solution)/shard_map/ppermute | solution.py:293
  5.5 1.3 collective-permute-start.1
  6.8 5.4 %pack.1 = (bf16[128,4,64,128]{3,2,1,0:T(8,128)(2,1)}, bf16[32,64,128]{2,1,0:T(8,128)(2,1)}) custom-call(s32[1,2,128]{2,1,0:T(2,128)} %bitcast.32, bf16[32,64,128]{2,1,0:T(8,128)(2,1)} %bitcast.27, bf16[32,64,128]{2,1,0:T(8,128)(2,1)} %bitcast.28, bf16[32,64,128]{2,1,0:T(8,128)(2,1)} %bitcast.25), custom_call_target="tpu_custom_call" | custom-call | flops 10485760 | bytes 12582912 | tf_op jit(solution)/shard_map/pack/pallas_call | solution.py:59
  12.1 0.0 collective-permute-done
  12.2 0.0 collective-permute-done.1
  12.2 12.6 %all-to-all-start = ((bf16[128,4,64,128]{3,2,1,0:T(8,128)(2,1)}), bf16[128,4,64,128]{3,2,1,0:T(8,128)(2,1)}, u32[]{:S(2)}, u32[]{:S(2)}) async-start(bf16[128,4,64,128]{3,2,1,0:T(8,128)(2,1)} %get-tuple-element.27), calls=%async_computation | async-start | bytes 16777216 | tf_op jit(solution)/shard_map/all_to_all | solution.py:328
  24.7 29.0 %pixel_part.1 = (bf16[64,128,128]{2,1,0:T(8,128)(2,1)}, bf16[32,256,128]{2,1,0:T(8,128)(2,1)}, bf16[256,64,128]{2,1,0:T(8,128)(2,1)}, f32[64,128]{1,0:T(8,128)}, f32[64,128]{1,0:T(8,128)}) custom-call(s32[6,32]{1,0:T(8,128)} %bitcast.30, bf16[64,128,128]{2,1,0:T(8,128)(2,1)} %hidden.1, bf16[64,128,128]{2,1,0:T(8,128)(2,1)} %upstream.3, ...), custom_call_target="tpu_custom_call" | custom-call | flops 1258291200 | bytes 18874368 | tf_op jit(solution)/shard_map/pixel_part/pallas_call | solution.py:114
  53.7 0.8 pad_maximum_fusion.2
  54.5 3.0 %collective-permute-start.3 = (f32[66,128]{1,0:T(8,128)S(1)}, f32[66,128]{1,0:T(8,128)S(1)}, u32[]{:S(2)}, u32[]{:S(2)}) collective-permute-start(f32[66,128]{1,0:T(8,128)S(1)} %pad_maximum_fusion.2), channel_id=1, source_target_pairs={{0,124},{1,125},{2,126},{3,127},{4,0},{5,1},{6,2},{7,3},{8,4},{9,5... | collective-permute-start | bytes 101384 | tf_op jit(solution)/shard_map/ppermute | solution.py:293
  57.6 0.8 pad_maximum_fusion.1
  58.3 2.5 %collective-permute-start.2 = (f32[66,128]{1,0:T(8,128)S(1)}, f32[66,128]{1,0:T(8,128)S(1)}, u32[]{:S(2)}, u32[]{:S(2)}) collective-permute-start(f32[66,128]{1,0:T(8,128)S(1)} %pad_maximum_fusion.1), channel_id=1, source_target_pairs={{0,4},{1,5},{2,6},{3,7},{4,8},{5,9},{6,10},{7,11},{12,16},{13,17},... | collective-permute-start | bytes 101384 | tf_op jit(solution)/shard_map/ppermute | solution.py:293
  60.8 3.2 %pad_maximum_fusion.padded = bf16[66,128,128]{2,1,0:T(8,128)(2,1)} fusion(bf16[1,128,128]{2,1,0:T(8,128)(2,1)S(1)} %collective-permute-done.1, bf16[64,128,128]{2,1,0:T(8,128)(2,1)} %get-tuple-element.32, bf16[1,128,128]{2,1,0:T(8,128)(2,1)S(1)} %collective-permute-done), kind=kLoop, calls=%fused_computation.1 | loop fusion | flops 2162688 | bytes 4325376 | tf_op jit(solution)/shard_map/concatenate | solution.py:334
  64.1 5.7 %collective-permute-done.3.right = f32[66,128]{1,0:T(8,128)S(1)} collective-permute-done((f32[66,128]{1,0:T(8,128)S(1)}, f32[66,128]{1,0:T(8,128)S(1)}, u32[]{:S(2)}, u32[]{:S(2)}) %collective-permute-start.3) | collective-permute-done | bytes 33824 | tf_op jit(solution)/shard_map/ppermute | solution.py:293
  69.8 0.0 copy-start.3
  69.8 3.4 %collective-permute-done.2.left = f32[66,128]{1,0:T(8,128)S(1)} collective-permute-done((f32[66,128]{1,0:T(8,128)S(1)}, f32[66,128]{1,0:T(8,128)S(1)}, u32[]{:S(2)}, u32[]{:S(2)}) %collective-permute-start.2) | collective-permute-done | bytes 33824 | tf_op jit(solution)/shard_map/ppermute | solution.py:293
  73.2 0.0 copy-start.4
  73.2 54.7 %all-to-all-done.incoming = bf16[128,4,64,128]{3,2,1,0:T(8,128)(2,1)} async-done(((bf16[128,4,64,128]{3,2,1,0:T(8,128)(2,1)}), bf16[128,4,64,128]{3,2,1,0:T(8,128)(2,1)}, u32[]{:S(2)}, u32[]{:S(2)}) %all-to-all-start) | async-done | bytes 8388640 | tf_op jit(solution)/shard_map/all_to_all | solution.py:328
  127.9 0.0 copy-start.1
  127.9 0.0 copy-start.2
  127.9 0.0 copy-done.3
  127.9 0.0 copy-done.4
  127.9 5.7 %all-to-all-start.1 = ((bf16[128,2,64,128]{3,2,1,0:T(8,128)(2,1)}), bf16[128,2,64,128]{3,2,1,0:T(8,128)(2,1)}, u32[]{:S(2)}, u32[]{:S(2)}) async-start(bf16[128,2,64,128]{3,2,1,0:T(8,128)(2,1)} %bitcast.23), calls=%async_computation.1 | async-start | bytes 8388608 | tf_op jit(solution)/shard_map/all_to_all | solution.py:346
  133.6 0.0 copy-done
  133.6 0.0 copy-done.1
  133.6 0.0 copy-done.2
  133.7 1.3 convolution_add_fusion
  135.0 28.2 %main_part.1 = (bf16[32,256,384]{2,1,0:T(8,128)(2,1)}, bf16[64,128,128]{2,1,0:T(8,128)(2,1)}) custom-call(s32[6,32]{1,0:T(8,128)} %bitcast.31, bf16[128,4,64,128]{3,2,1,0:T(8,128)(2,1)} %all-to-all-done.incoming, bf16[32,256,128]{2,1,0:T(8,128)(2,1)} %get-tuple-element.34.mixed, bf16[64,128,128]{2,1,0:T(8,128)(2,1)} %pixels.1, bf16[32,256,384]{2,1,0:T(8,128)(2,1)} %mixing.3, ...), custom_call_target="tpu_custom_call" | custom-call | flops 2726297600 | bytes 31457280 | tf_op jit(solution)/shard_map/main_part/pallas_call | solution.py:197
  163.2 23.6 %all-to-all-done.1.received = bf16[128,2,64,128]{3,2,1,0:T(8,128)(2,1)} async-done(((bf16[128,2,64,128]{3,2,1,0:T(8,128)(2,1)}), bf16[128,2,64,128]{3,2,1,0:T(8,128)(2,1)}, u32[]{:S(2)}, u32[]{:S(2)}) %all-to-all-start.1) | async-done | bytes 4194336 | tf_op jit(solution)/shard_map/all_to_all | solution.py:346
  186.7 4.5 %return_part.1 = bf16[32,64,128]{2,1,0:T(8,128)(2,1)} custom-call(s32[1,2,128]{2,1,0:T(2,128)} %bitcast.33, bf16[128,2,64,128]{3,2,1,0:T(8,128)(2,1)} %all-to-all-done.1.received, f32[32,64,128]{2,1,0:T(8,128)} %bitcast.24), custom_call_target="tpu_custom_call" | custom-call | flops 4194304 | bytes 6291456 | tf_op jit(solution)/shard_map/return_part/pallas_call | solution.py:265
  (1 shorter events, 0.0 us)
Async XLA Ops:
  0.6 133.0 %copy-start = (bf16[128,128]{1,0:T(8,128)(2,1)S(1)}, bf16[128,128]{1,0:T(8,128)(2,1)}, u32[]{:S(2)}) copy-start(bf16[128,128]{1,0:T(8,128)(2,1)} %param.22) | copy-start | bytes 98308
  1.5 10.6 %collective-permute-start = (bf16[1,128,128]{2,1,0:T(8,128)(2,1)S(1)}, bf16[1,128,128]{2,1,0:T(8,128)(2,1)S(1)}, u32[]{:S(2)}, u32[]{:S(2)}) collective-permute-start(bf16[1,128,128]{2,1,0:T(8,128)(2,1)S(1)} %get-tuple-element.44), channel_id=1, source_target_pairs={{0,1},{1,2},{2,3},{4,5},{5,6},{6,7},{8,9},{9,10},{10,11},{12,13},{... | collective-permute-start | bytes 98312 | tf_op jit(solution)/shard_map/ppermute | solution.py:293
  5.5 6.7 %collective-permute-start.1 = (bf16[1,128,128]{2,1,0:T(8,128)(2,1)S(1)}, bf16[1,128,128]{2,1,0:T(8,128)(2,1)S(1)}, u32[]{:S(2)}, u32[]{:S(2)}) collective-permute-start(bf16[1,128,128]{2,1,0:T(8,128)(2,1)S(1)} %get-tuple-element.43), channel_id=1, source_target_pairs={{1,0},{2,1},{3,2},{5,4},{6,5},{7,6},{9,8},{10,9},{11,10},{13,12},{... | collective-permute-start | bytes 98312 | tf_op jit(solution)/shard_map/ppermute | solution.py:293
  12.2 115.7 %all-to-all-start = ((bf16[128,4,64,128]{3,2,1,0:T(8,128)(2,1)}), bf16[128,4,64,128]{3,2,1,0:T(8,128)(2,1)}, u32[]{:S(2)}, u32[]{:S(2)}) async-start(bf16[128,4,64,128]{3,2,1,0:T(8,128)(2,1)} %get-tuple-element.27), calls=%async_computation | async-start | bytes 16777216 | tf_op jit(solution)/shard_map/all_to_all | solution.py:328
  54.5 15.3 %collective-permute-start.3 = (f32[66,128]{1,0:T(8,128)S(1)}, f32[66,128]{1,0:T(8,128)S(1)}, u32[]{:S(2)}, u32[]{:S(2)}) collective-permute-start(f32[66,128]{1,0:T(8,128)S(1)} %pad_maximum_fusion.2), channel_id=1, source_target_pairs={{0,124},{1,125},{2,126},{3,127},{4,0},{5,1},{6,2},{7,3},{8,4},{9,5... | collective-permute-start | bytes 101384 | tf_op jit(solution)/shard_map/ppermute | solution.py:293
  58.3 14.9 %collective-permute-start.2 = (f32[66,128]{1,0:T(8,128)S(1)}, f32[66,128]{1,0:T(8,128)S(1)}, u32[]{:S(2)}, u32[]{:S(2)}) collective-permute-start(f32[66,128]{1,0:T(8,128)S(1)} %pad_maximum_fusion.1), channel_id=1, source_target_pairs={{0,4},{1,5},{2,6},{3,7},{4,8},{5,9},{6,10},{7,11},{12,16},{13,17},... | collective-permute-start | bytes 101384 | tf_op jit(solution)/shard_map/ppermute | solution.py:293
  69.8 58.1 %copy-start.3 = (f32[66,128]{1,0:T(8,128)}, f32[66,128]{1,0:T(8,128)S(1)}, u32[]{:S(2)}) copy-start(f32[66,128]{1,0:T(8,128)S(1)} %collective-permute-done.3.right) | copy-start | bytes 101380
  73.2 54.7 %copy-start.4 = (f32[66,128]{1,0:T(8,128)}, f32[66,128]{1,0:T(8,128)S(1)}, u32[]{:S(2)}) copy-start(f32[66,128]{1,0:T(8,128)S(1)} %collective-permute-done.2.left) | copy-start | bytes 101380
  127.9 5.7 %copy-start.1 = (bf16[2048,128]{1,0:T(8,128)(2,1)S(1)}, bf16[2048,128]{1,0:T(8,128)(2,1)}, u32[]{:S(2)}) copy-start(bf16[2048,128]{1,0:T(8,128)(2,1)} %param.17) | copy-start | bytes 1572868
  127.9 5.8 %copy-start.2 = (bf16[32,64,128]{2,1,0:T(8,128)(2,1)S(1)}, bf16[32,64,128]{2,1,0:T(8,128)(2,1)}, u32[]{:S(2)}) copy-start(bf16[32,64,128]{2,1,0:T(8,128)(2,1)} %get-tuple-element.23) | copy-start | bytes 1572868
  127.9 58.8 %all-to-all-start.1 = ((bf16[128,2,64,128]{3,2,1,0:T(8,128)(2,1)}), bf16[128,2,64,128]{3,2,1,0:T(8,128)(2,1)}, u32[]{:S(2)}, u32[]{:S(2)}) async-start(bf16[128,2,64,128]{3,2,1,0:T(8,128)(2,1)} %bitcast.23), calls=%async_computation.1 | async-start | bytes 8388608 | tf_op jit(solution)/shard_map/all_to_all | solution.py:346

commit v3 on v2

--- a/solution.py
+++ b/solution.py
@@ -148,7 +148,7 @@
 
 def main_kernel(
     neighbors, incoming, mixed, pixels, mixing, upstream, padded, left, right, kernel,
-    mixing_gradient, pixel_gradient, left_side, right_side,
+    mixing_gradient, pixel_gradient, totals, left_side, right_side,
 ):
     q = pl.program_id(0)
     for k in range(K):
@@ -190,6 +190,11 @@
         total = total + jnp.where(column == 0, sides[2][1], behind)
         pixel_gradient[r] = total.astype(jnp.bfloat16)
 
+        @pl.when(q == r * (PB - 1))
+        def _():
+            totals[2 * r : 2 * r + 1] = total[0:1]
+            totals[2 * r + 1 : 2 * r + 2] = total[COLS_DEV - 1 : COLS_DEV]
+
 
 def main_part(neighbors, incoming, mixed, pixels, mixing, upstream, padded, left, right, kernel):
     rows = pl.BlockSpec((2, COLS_DEV, C), lambda q, n: (q, 0, 0))
@@ -213,6 +218,7 @@
             out_specs=[
                 pl.BlockSpec((1, PIXB, K * BS), lambda q, n: (q, 0, 0)),
                 rows,
+                pl.BlockSpec((4, C), lambda q, n: (0, 0)),
             ],
             scratch_shapes=[
                 pltpu.VMEM((PIXB, 2 * C), jnp.bfloat16),
@@ -222,6 +228,7 @@
         out_shape=[
             jax.ShapeDtypeStruct((PB, PIXB, K * BS), jnp.bfloat16),
             jax.ShapeDtypeStruct((ROWS_DEV, COLS_DEV, C), jnp.bfloat16),
+            jax.ShapeDtypeStruct((4, C), jnp.float32),
         ],
         compiler_params=pltpu.CompilerParams(vmem_limit_bytes=VMEM),
         cost_estimate=pl.CostEstimate(
@@ -229,6 +236,31 @@
         ),
         name="main_part",
     )(neighbors, incoming, mixed, pixels, mixing, upstream, padded, left, right, kernel)
+
+
+def corner_kernel(totals, gains, corners, gradient, out):
+    i = pl.program_id(0)
+    value = totals[pl.ds(i, 1), :] + gains[pl.ds(i, 1), :] * corners[pl.ds(i, 1), :]
+    column = lax.broadcasted_iota(jnp.int32, (16, C), 0)
+    block = jnp.where(column == lax.rem(i, 2) * 15, value, gradient[0].astype(jnp.float32))
+    out[0] = block.astype(jnp.bfloat16)
+
+
+def corner_part(totals, gains, corners, gradient):
+    whole = pl.BlockSpec((4, C), lambda i: (0, 0))
+    ends = ROWS_DEV - 1, COLS_DEV // 16 - 1
+    block = pl.BlockSpec((1, 16, C), lambda i: (i // 2 * ends[0], i % 2 * ends[1], 0))
+    return pl.pallas_call(
+        corner_kernel,
+        grid=(4,),
+        in_specs=[whole, whole, whole, block],
+        out_specs=block,
+        out_shape=jax.ShapeDtypeStruct(gradient.shape, jnp.bfloat16),
+        input_output_aliases={3: 0},
+        compiler_params=pltpu.CompilerParams(vmem_limit_bytes=VMEM),
+        cost_estimate=pl.CostEstimate(flops=4096, bytes_accessed=65536, transcendentals=0),
+        name="corner_part",
+    )(totals, gains, corners, gradient)
 
 
 def return_kernel(targets, received, base, out, landed, sems, *totals):
@@ -314,9 +346,6 @@
     targets = jnp.transpose(send_list, (0, 2, 1))
     reads = neighbors.T
     blocks = (BLK_DEV, BS, C)
-    move = functools.partial(shifted, tiles=tiles, cams=cams)
-    above = move(slope_of(pixel_upstream[-1:], pixel_hidden[-1:]), tile_step=0, cam_step=1)
-    below = move(slope_of(pixel_upstream[:1], pixel_hidden[:1]), tile_step=0, cam_step=-1)
     outgoing, point_slope = pack(
         targets,
         points.reshape(blocks),
@@ -324,24 +353,27 @@
         point_upstream.reshape(blocks),
         devices,
     )
-    outgoing, reads, above, below = lax.optimization_barrier((outgoing, reads, above, below))
+    outgoing, reads = lax.optimization_barrier((outgoing, reads))
     incoming = lax.all_to_all(
         outgoing, ("tile", "cam"), split_axis=0, concat_axis=0, tiled=True
     )
     pixel_slope, mixed, sums, first, last = pixel_part(
         reads, pixel_hidden, pixel_upstream, mixing, pixel_weight, slots
     )
-    padded = jnp.concatenate([above, pixel_slope, below], axis=0)
-    first = jnp.concatenate(
-        [above[:, 0].astype(jnp.float32), first, below[:, 0].astype(jnp.float32)], axis=0
-    )
-    last = jnp.concatenate(
-        [above[:, -1].astype(jnp.float32), last, below[:, -1].astype(jnp.float32)], axis=0
-    )
-    rim_left = move(last, tile_step=1, cam_step=0)
-    rim_right = move(first, tile_step=-1, cam_step=0)
-    sums, incoming, rim_left, rim_right, padded = lax.optimization_barrier(
-        (sums, incoming, rim_left, rim_right, padded)
+    move = functools.partial(shifted, tiles=tiles, cams=cams)
+    padded = jnp.concatenate(
+        [
+            move(pixel_slope[-1:], tile_step=0, cam_step=1),
+            pixel_slope,
+            move(pixel_slope[:1], tile_step=0, cam_step=-1),
+        ],
+        axis=0,
+    )
+    edges = ((1, 1), (0, 0))
+    rim_left = jnp.pad(move(last, tile_step=1, cam_step=0), edges)
+    rim_right = jnp.pad(move(first, tile_step=-1, cam_step=0), edges)
+    sums, incoming, rim_left, rim_right, padded, point_slope = lax.optimization_barrier(
+        (sums, incoming, rim_left, rim_right, padded, point_slope)
     )
     received = lax.all_to_all(
         sums.reshape(devices, CAP, BS, C),
@@ -350,12 +382,24 @@
         concat_axis=0,
         tiled=True,
     )
-    mixing_gradient, pixel_gradient = main_part(
-        reads, incoming, mixed, pixels, mixing, pixel_upstream, padded, rim_left, rim_right, kernel
-    )
     base = point_upstream.astype(jnp.float32) + jnp.dot(
         point_slope.reshape(BLK_DEV * BS, C), point_weight.T, preferred_element_type=jnp.float32
     )
+    base, first, last = lax.optimization_barrier((base, first, last))
+    corners = jnp.concatenate(
+        [
+            move(last[-1:], tile_step=1, cam_step=1),
+            move(first[-1:], tile_step=-1, cam_step=1),
+            move(last[:1], tile_step=1, cam_step=-1),
+            move(first[:1], tile_step=-1, cam_step=-1),
+        ],
+        axis=0,
+    )
+    mixing_gradient, pixel_gradient, totals = main_part(
+        reads, incoming, mixed, pixels, mixing, pixel_upstream, padded, rim_left, rim_right, kernel
+    )
+    gains = jnp.stack([kernel[2, 2], kernel[2, 0], kernel[0, 2], kernel[0, 0]])
+    pixel_gradient = corner_part(totals, gains, corners, pixel_gradient)
     base, pixel_gradient = lax.optimization_barrier((base, pixel_gradient))
     point_gradient = return_part(targets, received, base.reshape(blocks))
     return (pixel_gradient, point_gradient.reshape(BLK_DEV * BS, C), mixing_gradient)

time: 193 us -> 191 us (0.990)
  the two profiles are of different devices: /device:TPU:1 before, /device:TPU:4 now
where the time goes in v3:
time: 191 us; the launch traced here: 189 us
  Pallas kernels  71.1 us (37%)
  starting transfers between devices  53.9 us (28%)
  waiting for transfers between devices  53.3 us (28%)
  other arithmetic  4.44 us (2%)
  local copies, waits for them, and re-layouts  4.2 us (2%)
    ppermute x8, waiting for transfers between devices, shifted(): return lax.ppermute(block, ('tile', 'cam'), pairs)  51.3 us
    ppermute x8, starting transfers between devices, shifted(): return lax.ppermute(block, ('tile', 'cam'), pairs)  34.2 us
    pallas_call x1, Pallas kernels, main_part(): pl.pallas_call(main_kernel, grid_spec=pltpu.PrefetchScalarGridSpec(num_sc...  29.7 us
    pallas_call x1, Pallas kernels, pixel_part(): pl.pallas_call(pixel_kernel, grid_spec=pltpu.PrefetchScalarGridSpec(num_s...  29 us
    all_to_all x1, starting transfers between devices, per_device(): lax.all_to_all(outgoing, ('tile', 'cam'), split_axis=0, concat_axis=0, ti...  11 us
    all_to_all x1, starting transfers between devices, per_device(): lax.all_to_all(sums.reshape(devices, CAP, BS, C), ('tile', 'cam'), split_...  8.73 us
    pallas_call x1, Pallas kernels, pack(): pl.pallas_call(pack_kernel, in_specs=[pl.BlockSpec(memory_space=pltpu.SME...  5.35 us
    pallas_call x1, Pallas kernels, return_part(): pl.pallas_call(return_kernel, in_specs=[pl.BlockSpec(memory_space=pltpu.S...  4.51 us
  transfers between devices with their start and end apart: 10, of which 2 were waited for; matrix products, arithmetic and copies ran while one was open for 5% of the time, Pallas kernels for 32%

profile of v3, /device:TPU:4, one launch (start us, length us, event | category | flops | bytes accessed | tf_op | source)
XLA Modules:
  0.0 189.1 jit_solution(620482894050363032)
XLA Ops:
  0.6 0.0 copy-start
  0.6 5.4 %pack.1 = (bf16[128,4,64,128]{3,2,1,0:T(8,128)(2,1)}, bf16[32,64,128]{2,1,0:T(8,128)(2,1)}) custom-call(s32[1,2,128]{2,1,0:T(2,128)} %bitcast.28, bf16[32,64,128]{2,1,0:T(8,128)(2,1)} %bitcast.23, bf16[32,64,128]{2,1,0:T(8,128)(2,1)} %bitcast.24, bf16[32,64,128]{2,1,0:T(8,128)(2,1)} %bitcast.21), custom_call_target="tpu_custom_call" | custom-call | flops 10485760 | bytes 12582912 | tf_op jit(solution)/shard_map/pack/pallas_call | solution.py:59
  6.0 11.0 %all-to-all-start = ((bf16[128,4,64,128]{3,2,1,0:T(8,128)(2,1)}), bf16[128,4,64,128]{3,2,1,0:T(8,128)(2,1)}, u32[]{:S(2)}, u32[]{:S(2)}) async-start(bf16[128,4,64,128]{3,2,1,0:T(8,128)(2,1)} %get-tuple-element.29), calls=%async_computation | async-start | bytes 16777216 | tf_op jit(solution)/shard_map/all_to_all | solution.py:357
  17.0 29.0 %pixel_part.1 = (bf16[64,128,128]{2,1,0:T(8,128)(2,1)}, bf16[32,256,128]{2,1,0:T(8,128)(2,1)}, bf16[256,64,128]{2,1,0:T(8,128)(2,1)}, f32[64,128]{1,0:T(8,128)}, f32[64,128]{1,0:T(8,128)}) custom-call(s32[6,32]{1,0:T(8,128)} %bitcast.26, bf16[64,128,128]{2,1,0:T(8,128)(2,1)} %hidden.1, bf16[64,128,128]{2,1,0:T(8,128)(2,1)} %upstream.3, ...), custom_call_target="tpu_custom_call" | custom-call | flops 1258291200 | bytes 18874368 | tf_op jit(solution)/shard_map/pixel_part/pallas_call | solution.py:114
  46.0 2.1 %collective-permute-start = (f32[64,128]{1,0:T(8,128)}, f32[64,128]{1,0:T(8,128)S(1)}, u32[]{:S(2)}, u32[]{:S(2)}) collective-permute-start(f32[64,128]{1,0:T(8,128)} %get-tuple-element.42), channel_id=1, source_target_pairs={{0,4},{1,5},{2,6},{3,7},{4,8},{5,9},{6,10},{7,11},{12,16},{13,17},... | collective-permute-start | bytes 98312 | tf_op jit(solution)/shard_map/ppermute | solution.py:325
  48.0 6.8 %collective-permute-start.1 = (f32[64,128]{1,0:T(8,128)}, f32[64,128]{1,0:T(8,128)S(1)}, u32[]{:S(2)}, u32[]{:S(2)}) collective-permute-start(f32[64,128]{1,0:T(8,128)} %get-tuple-element.43), channel_id=1, source_target_pairs={{0,124},{1,125},{2,126},{3,127},{4,0},{5,1},{6,2},{7,3},{8,4},{9,5... | collective-permute-start | bytes 98312 | tf_op jit(solution)/shard_map/ppermute | solution.py:325
  54.9 0.8 fusion
  55.7 3.1 %collective-permute-start.2 = (bf16[1,128,128]{2,1,0:T(8,128)(2,1)S(1)}, bf16[1,128,128]{2,1,0:T(8,128)(2,1)S(1)}, u32[]{:S(2)}, u32[]{:S(2)}) collective-permute-start(bf16[1,128,128]{2,1,0:T(8,128)(2,1)S(1)} %get-tuple-element.49), channel_id=1, source_target_pairs={{0,1},{1,2},{2,3},{4,5},{5,6},{6,7},{8,9},{9,10},{10,11},{12,13},{... | collective-permute-start | bytes 98312 | tf_op jit(solution)/shard_map/ppermute | solution.py:325
  58.7 2.8 %collective-permute-start.3 = (bf16[1,128,128]{2,1,0:T(8,128)(2,1)S(1)}, bf16[1,128,128]{2,1,0:T(8,128)(2,1)S(1)}, u32[]{:S(2)}, u32[]{:S(2)}) collective-permute-start(bf16[1,128,128]{2,1,0:T(8,128)(2,1)S(1)} %get-tuple-element.50), channel_id=1, source_target_pairs={{1,0},{2,1},{3,2},{5,4},{6,5},{7,6},{9,8},{10,9},{11,10},{13,12},{... | collective-permute-start | bytes 98312 | tf_op jit(solution)/shard_map/ppermute | solution.py:325
  61.5 51.3 %collective-permute-done = f32[64,128]{1,0:T(8,128)S(1)} collective-permute-done((f32[64,128]{1,0:T(8,128)}, f32[64,128]{1,0:T(8,128)S(1)}, u32[]{:S(2)}, u32[]{:S(2)}) %collective-permute-start) | collective-permute-done | bytes 32800 | tf_op jit(solution)/shard_map/ppermute | solution.py:325
  112.8 0.6 pad.7.left
  113.4 0.0 collective-permute-done.1
  113.4 0.6 pad.8.right
  114.0 0.0 collective-permute-done.2
  114.0 0.0 collective-permute-done.3
  114.0 3.2 %pad_maximum_fusion.padded = bf16[66,128,128]{2,1,0:T(8,128)(2,1)} fusion(bf16[1,128,128]{2,1,0:T(8,128)(2,1)S(1)} %collective-permute-done.3, bf16[64,128,128]{2,1,0:T(8,128)(2,1)} %get-tuple-element.32, bf16[1,128,128]{2,1,0:T(8,128)(2,1)S(1)} %collective-permute-done.2), kind=kLoop, calls=%fused_computation.1 | loop fusion | flops 2162688 | bytes 4325376 | tf_op jit(solution)/shard_map/concatenate | solution.py:364
  117.3 2.0 %all-to-all-done.incoming = bf16[128,4,64,128]{3,2,1,0:T(8,128)(2,1)} async-done(((bf16[128,4,64,128]{3,2,1,0:T(8,128)(2,1)}), bf16[128,4,64,128]{3,2,1,0:T(8,128)(2,1)}, u32[]{:S(2)}, u32[]{:S(2)}) %all-to-all-start) | async-done | bytes 8388640 | tf_op jit(solution)/shard_map/all_to_all | solution.py:357
  119.3 0.0 copy-start.1
  119.3 0.0 copy-start.2
  119.3 8.7 %all-to-all-start.1 = ((bf16[128,2,64,128]{3,2,1,0:T(8,128)(2,1)}), bf16[128,2,64,128]{3,2,1,0:T(8,128)(2,1)}, u32[]{:S(2)}, u32[]{:S(2)}) async-start(bf16[128,2,64,128]{3,2,1,0:T(8,128)(2,1)} %bitcast.19), calls=%async_computation.1 | async-start | bytes 8388608 | tf_op jit(solution)/shard_map/all_to_all | solution.py:378
  128.0 0.8 slice_bitcast_fusion.3
  128.8 0.6 pad_maximum_fusion.1.gains
  129.4 0.0 copy-done
  129.4 0.0 copy-done.1
  129.4 0.0 copy-done.2
  129.4 1.3 convolution_add_fusion
  130.7 0.7 fusion.1
  131.4 2.8 %collective-permute-start.4 = (f32[1,128]{1,0:T(1,128)S(1)}, f32[1,128]{1,0:T(1,128)S(1)}, u32[]{:S(2)}, u32[]{:S(2)}) collective-permute-start(f32[1,128]{1,0:T(1,128)S(1)} %get-tuple-element.51), channel_id=1, source_target_pairs={{0,5},{1,6},{2,7},{4,9},{5,10},{6,11},{12,17},{13,18},{14,19},{16,... | collective-permute-start | bytes 1544 | tf_op jit(solution)/shard_map/ppermute | solution.py:325
  134.2 0.7 fusion.2
  134.9 5.8 %collective-permute-start.5 = (f32[1,128]{1,0:T(1,128)S(1)}, f32[1,128]{1,0:T(1,128)S(1)}, u32[]{:S(2)}, u32[]{:S(2)}) collective-permute-start(f32[1,128]{1,0:T(1,128)S(1)} %get-tuple-element.53), channel_id=1, source_target_pairs={{0,125},{1,126},{2,127},{4,1},{5,2},{6,3},{8,5},{9,6},{10,7},{16,1... | collective-permute-start | bytes 1544 | tf_op jit(solution)/shard_map/ppermute | solution.py:325
  140.7 1.9 %collective-permute-start.6 = (f32[1,128]{1,0:T(1,128)S(1)}, f32[1,128]{1,0:T(1,128)S(1)}, u32[]{:S(2)}, u32[]{:S(2)}) collective-permute-start(f32[1,128]{1,0:T(1,128)S(1)} %get-tuple-element.52), channel_id=1, source_target_pairs={{1,4},{2,5},{3,6},{5,8},{6,9},{7,10},{13,16},{14,17},{15,18},{17,2... | collective-permute-start | bytes 1544 | tf_op jit(solution)/shard_map/ppermute | solution.py:325
  142.6 9.0 %collective-permute-start.7 = (f32[1,128]{1,0:T(1,128)S(1)}, f32[1,128]{1,0:T(1,128)S(1)}, u32[]{:S(2)}, u32[]{:S(2)}) collective-permute-start(f32[1,128]{1,0:T(1,128)S(1)} %get-tuple-element.54), channel_id=1, source_target_pairs={{1,124},{2,125},{3,126},{5,0},{6,1},{7,2},{9,4},{10,5},{11,6},{17,... | collective-permute-start | bytes 1544 | tf_op jit(solution)/shard_map/ppermute | solution.py:325
  151.7 29.7 %main_part.1 = (bf16[32,256,384]{2,1,0:T(8,128)(2,1)}, bf16[64,128,128]{2,1,0:T(8,128)(2,1)}, f32[4,128]{1,0:T(4,128)}) custom-call(s32[6,32]{1,0:T(8,128)} %bitcast.27, bf16[128,4,64,128]{3,2,1,0:T(8,128)(2,1)} %all-to-all-done.incoming, bf16[32,256,128]{2,1,0:T(8,128)(2,1)} %get-tuple-element.37.mixed, bf16[64,128,128]{2,1,0:T(8,128)(2,1)} %pixels.1, ...), custom_call_target="tpu_custom_call" | custom-call | flops 2726297600 | bytes 31457280 | tf_op jit(solution)/shard_map/main_part/pallas_call | solution.py:202
  181.3 0.0 collective-permute-done.4
  181.3 0.0 collective-permute-done.5
  181.3 0.0 collective-permute-done.6
  181.3 0.0 collective-permute-done.7
  181.4 0.6 pad_maximum_fusion.2.corners
  182.0 2.6 %corner_part.1 = bf16[64,128,128]{2,1,0:T(8,128)(2,1)} custom-call(f32[4,128]{1,0:T(4,128)} %get-tuple-element.41.totals, f32[4,128]{1,0:T(4,128)} %pad_maximum_fusion.1.gains, f32[4,128]{1,0:T(4,128)} %pad_maximum_fusion.2.corners, bf16[64,128,128]{2,1,0:T(8,128)(2,1)} %get-tuple-element.44.gradient), custom_call_target="tpu_custom_call", output_to_operand_aliasing={{}: (3, {})} | custom-call | flops 4096 | bytes 65536 | tf_op jit(solution)/shard_map/corner_part/pallas_call | solution.py:253
  184.6 0.0 all-to-all-done.1.received
  184.6 4.5 %return_part.1 = bf16[32,64,128]{2,1,0:T(8,128)(2,1)} custom-call(s32[1,2,128]{2,1,0:T(2,128)} %bitcast.29, bf16[128,2,64,128]{3,2,1,0:T(8,128)(2,1)} %all-to-all-done.1.received, f32[32,64,128]{2,1,0:T(8,128)} %bitcast.20), custom_call_target="tpu_custom_call" | custom-call | flops 4194304 | bytes 6291456 | tf_op jit(solution)/shard_map/return_part/pallas_call | solution.py:297
Async XLA Ops:
  0.6 128.7 %copy-start = (bf16[128,128]{1,0:T(8,128)(2,1)S(1)}, bf16[128,128]{1,0:T(8,128)(2,1)}, u32[]{:S(2)}) copy-start(bf16[128,128]{1,0:T(8,128)(2,1)} %param.22) | copy-start | bytes 98308
  6.0 113.3 %all-to-all-start = ((bf16[128,4,64,128]{3,2,1,0:T(8,128)(2,1)}), bf16[128,4,64,128]{3,2,1,0:T(8,128)(2,1)}, u32[]{:S(2)}, u32[]{:S(2)}) async-start(bf16[128,4,64,128]{3,2,1,0:T(8,128)(2,1)} %get-tuple-element.29), calls=%async_computation | async-start | bytes 16777216 | tf_op jit(solution)/shard_map/all_to_all | solution.py:357
  46.0 66.8 %collective-permute-start = (f32[64,128]{1,0:T(8,128)}, f32[64,128]{1,0:T(8,128)S(1)}, u32[]{:S(2)}, u32[]{:S(2)}) collective-permute-start(f32[64,128]{1,0:T(8,128)} %get-tuple-element.42), channel_id=1, source_target_pairs={{0,4},{1,5},{2,6},{3,7},{4,8},{5,9},{6,10},{7,11},{12,16},{13,17},... | collective-permute-start | bytes 98312 | tf_op jit(solution)/shard_map/ppermute | solution.py:325
  48.0 65.4 %collective-permute-start.1 = (f32[64,128]{1,0:T(8,128)}, f32[64,128]{1,0:T(8,128)S(1)}, u32[]{:S(2)}, u32[]{:S(2)}) collective-permute-start(f32[64,128]{1,0:T(8,128)} %get-tuple-element.43), channel_id=1, source_target_pairs={{0,124},{1,125},{2,126},{3,127},{4,0},{5,1},{6,2},{7,3},{8,4},{9,5... | collective-permute-start | bytes 98312 | tf_op jit(solution)/shard_map/ppermute | solution.py:325
  55.7 58.4 %collective-permute-start.2 = (bf16[1,128,128]{2,1,0:T(8,128)(2,1)S(1)}, bf16[1,128,128]{2,1,0:T(8,128)(2,1)S(1)}, u32[]{:S(2)}, u32[]{:S(2)}) collective-permute-start(bf16[1,128,128]{2,1,0:T(8,128)(2,1)S(1)} %get-tuple-element.49), channel_id=1, source_target_pairs={{0,1},{1,2},{2,3},{4,5},{5,6},{6,7},{8,9},{9,10},{10,11},{12,13},{... | collective-permute-start | bytes 98312 | tf_op jit(solution)/shard_map/ppermute | solution.py:325
  58.7 55.3 %collective-permute-start.3 = (bf16[1,128,128]{2,1,0:T(8,128)(2,1)S(1)}, bf16[1,128,128]{2,1,0:T(8,128)(2,1)S(1)}, u32[]{:S(2)}, u32[]{:S(2)}) collective-permute-start(bf16[1,128,128]{2,1,0:T(8,128)(2,1)S(1)} %get-tuple-element.50), channel_id=1, source_target_pairs={{1,0},{2,1},{3,2},{5,4},{6,5},{7,6},{9,8},{10,9},{11,10},{13,12},{... | collective-permute-start | bytes 98312 | tf_op jit(solution)/shard_map/ppermute | solution.py:325
  119.3 10.1 %copy-start.1 = (bf16[2048,128]{1,0:T(8,128)(2,1)S(1)}, bf16[2048,128]{1,0:T(8,128)(2,1)}, u32[]{:S(2)}) copy-start(bf16[2048,128]{1,0:T(8,128)(2,1)} %param.17) | copy-start | bytes 1572868
  119.3 10.1 %copy-start.2 = (bf16[32,64,128]{2,1,0:T(8,128)(2,1)S(1)}, bf16[32,64,128]{2,1,0:T(8,128)(2,1)}, u32[]{:S(2)}) copy-start(bf16[32,64,128]{2,1,0:T(8,128)(2,1)} %get-tuple-element.34) | copy-start | bytes 1572868
  119.3 65.3 %all-to-all-start.1 = ((bf16[128,2,64,128]{3,2,1,0:T(8,128)(2,1)}), bf16[128,2,64,128]{3,2,1,0:T(8,128)(2,1)}, u32[]{:S(2)}, u32[]{:S(2)}) async-start(bf16[128,2,64,128]{3,2,1,0:T(8,128)(2,1)} %bitcast.19), calls=%async_computation.1 | async-start | bytes 8388608 | tf_op jit(solution)/shard_map/all_to_all | solution.py:378
  131.4 49.9 %collective-permute-start.4 = (f32[1,128]{1,0:T(1,128)S(1)}, f32[1,128]{1,0:T(1,128)S(1)}, u32[]{:S(2)}, u32[]{:S(2)}) collective-permute-start(f32[1,128]{1,0:T(1,128)S(1)} %get-tuple-element.51), channel_id=1, source_target_pairs={{0,5},{1,6},{2,7},{4,9},{5,10},{6,11},{12,17},{13,18},{14,19},{16,... | collective-permute-start | bytes 1544 | tf_op jit(solution)/shard_map/ppermute | solution.py:325
  134.9 46.4 %collective-permute-start.5 = (f32[1,128]{1,0:T(1,128)S(1)}, f32[1,128]{1,0:T(1,128)S(1)}, u32[]{:S(2)}, u32[]{:S(2)}) collective-permute-start(f32[1,128]{1,0:T(1,128)S(1)} %get-tuple-element.53), channel_id=1, source_target_pairs={{0,125},{1,126},{2,127},{4,1},{5,2},{6,3},{8,5},{9,6},{10,7},{16,1... | collective-permute-start | bytes 1544 | tf_op jit(solution)/shard_map/ppermute | solution.py:325
  140.7 40.6 %collective-permute-start.6 = (f32[1,128]{1,0:T(1,128)S(1)}, f32[1,128]{1,0:T(1,128)S(1)}, u32[]{:S(2)}, u32[]{:S(2)}) collective-permute-start(f32[1,128]{1,0:T(1,128)S(1)} %get-tuple-element.52), channel_id=1, source_target_pairs={{1,4},{2,5},{3,6},{5,8},{6,9},{7,10},{13,16},{14,17},{15,18},{17,2... | collective-permute-start | bytes 1544 | tf_op jit(solution)/shard_map/ppermute | solution.py:325
  142.6 38.7 %collective-permute-start.7 = (f32[1,128]{1,0:T(1,128)S(1)}, f32[1,128]{1,0:T(1,128)S(1)}, u32[]{:S(2)}, u32[]{:S(2)}) collective-permute-start(f32[1,128]{1,0:T(1,128)S(1)} %get-tuple-element.54), channel_id=1, source_target_pairs={{1,124},{2,125},{3,126},{5,0},{6,1},{7,2},{9,4},{10,5},{11,6},{17,... | collective-permute-start | bytes 1544 | tf_op jit(solution)/shard_map/ppermute | solution.py:325

commit v4 on v2

--- a/solution.py
+++ b/solution.py
@@ -31,7 +31,18 @@
     return (upstream.astype(jnp.float32) * slope).astype(jnp.bfloat16)
 
 
-def pack_kernel(targets, points, hidden, upstream, out, slope, sem):
+def pack_kernel(
+    targets, points_in, hidden_in, upstream_in, out, slope, points, hidden, upstream, sem, sems
+):
+    loads = [
+        pltpu.make_async_copy(source, target, sems.at[i])
+        for i, (source, target) in enumerate(
+            ((points_in, points), (hidden_in, hidden), (upstream_in, upstream))
+        )
+    ]
+    for load in loads:
+        load.start()
+
     def send(source, first):
         def body(i, carry):
             for j in range(DESTS):
@@ -48,23 +59,27 @@
         slope[part] = slope_of(upstream[part], hidden[part])
         return carry
 
+    loads[0].wait()
     send(points, 0)
+    loads[1].wait()
+    loads[2].wait()
     lax.fori_loop(0, BLK_DEV // 2, fill, 0)
     send(slope, CAP)
     pltpu.make_async_copy(out, out, sem).wait()
 
 
 def pack(targets, points, hidden, upstream, devices):
-    whole = pl.BlockSpec(memory_space=pltpu.VMEM)
+    anywhere = pl.BlockSpec(memory_space=pl.ANY)
     return pl.pallas_call(
         pack_kernel,
-        in_specs=[pl.BlockSpec(memory_space=pltpu.SMEM), whole, whole, whole],
-        out_specs=[pl.BlockSpec(memory_space=pl.ANY), whole],
+        in_specs=[pl.BlockSpec(memory_space=pltpu.SMEM), anywhere, anywhere, anywhere],
+        out_specs=[anywhere, pl.BlockSpec(memory_space=pltpu.VMEM)],
         out_shape=[
             jax.ShapeDtypeStruct((devices, 2 * CAP, BS, C), jnp.bfloat16),
             jax.ShapeDtypeStruct((BLK_DEV, BS, C), jnp.bfloat16),
         ],
-        scratch_shapes=[pltpu.SemaphoreType.DMA(())],
+        scratch_shapes=[pltpu.VMEM((BLK_DEV, BS, C), jnp.bfloat16)] * 3
+        + [pltpu.SemaphoreType.DMA(()), pltpu.SemaphoreType.DMA((3,))],
         compiler_params=pltpu.CompilerParams(vmem_limit_bytes=VMEM),
         cost_estimate=pl.CostEstimate(flops=10 * MIB, bytes_accessed=12 * MIB, transcendentals=0),
         name="pack",
@@ -147,8 +162,8 @@
 
 
 def main_kernel(
-    neighbors, incoming, mixed, pixels, mixing, upstream, padded, left, right, kernel,
-    mixing_gradient, pixel_gradient, left_side, right_side,
+    neighbors, incoming, mixed, pixels, mixing, upstream, slope, above, below, left, right, kernel,
+    mixing_gradient, pixel_gradient, totals, left_side, right_side,
 ):
     q = pl.program_id(0)
     for k in range(K):
@@ -167,31 +182,54 @@
     ).astype(jnp.bfloat16)
     term = jnp.dot(mixing[0], right_side[:, C : 2 * C], preferred_element_type=jnp.float32)
     column = lax.broadcasted_iota(jnp.int32, (COLS_DEV, C), 0)
+    before = jnp.maximum(2 * q - 1, 0)
+    after = jnp.minimum(2 * q + 2, ROWS_DEV - 1)
+    top = q == 0
+    bottom = q == PB - 1
+
+    def wide(piece):
+        return piece.astype(jnp.float32)
+
+    rows = [
+        jnp.where(top, wide(above[0]), wide(slope[before])),
+        wide(slope[2 * q]),
+        wide(slope[2 * q + 1]),
+        jnp.where(bottom, wide(below[0]), wide(slope[after])),
+    ]
+
+    def rim(side):
+        zero = jnp.zeros((1, C), jnp.float32)
+        return [
+            jnp.where(top, zero, side[pl.ds(before, 1), :]),
+            side[pl.ds(2 * q, 1), :],
+            side[pl.ds(2 * q + 1, 1), :],
+            jnp.where(bottom, zero, side[pl.ds(after, 1), :]),
+        ]
+
+    rims = {0: rim(right), 2: rim(left)}
+    gains = [[kernel[a, e : e + 1, :] for e in range(3)] for a in range(3)]
+
+    def mix(pieces, r, e):
+        return sum(gains[a][e] * pieces[r + 2 - a] for a in range(3))
+
     for r in range(2):
-        row = 2 * q + r
-        total = upstream[r].astype(jnp.float32) + term[r * COLS_DEV : (r + 1) * COLS_DEV]
-        sides = []
-        for e in range(3):
-            part = None
-            edge = None
-            for a in range(3):
-                gain = kernel[a, e : e + 1, :]
-                piece = padded[row + 2 - a].astype(jnp.float32) * gain
-                part = piece if part is None else part + piece
-                if e != 1:
-                    rim = right if e == 0 else left
-                    corner = rim[pl.ds(row + 2 - a, 1), :] * gain
-                    edge = corner if edge is None else edge + corner
-            sides.append((part, edge))
-        total = total + sides[1][0]
-        ahead = pltpu.roll(sides[0][0], COLS_DEV - 1, 0)
-        total = total + jnp.where(column == COLS_DEV - 1, sides[0][1], ahead)
-        behind = pltpu.roll(sides[2][0], 1, 0)
-        total = total + jnp.where(column == 0, sides[2][1], behind)
+        total = wide(upstream[r]) + term[r * COLS_DEV : (r + 1) * COLS_DEV]
+        total = total + mix(rows, r, 1)
+        ahead = pltpu.roll(mix(rows, r, 0), COLS_DEV - 1, 0)
+        total = total + jnp.where(column == COLS_DEV - 1, mix(rims[0], r, 0), ahead)
+        behind = pltpu.roll(mix(rows, r, 2), 1, 0)
+        total = total + jnp.where(column == 0, mix(rims[2], r, 2), behind)
         pixel_gradient[r] = total.astype(jnp.bfloat16)
 
-
-def main_part(neighbors, incoming, mixed, pixels, mixing, upstream, padded, left, right, kernel):
+        @pl.when(q == r * (PB - 1))
+        def _():
+            totals[2 * r : 2 * r + 1] = total[0:1]
+            totals[2 * r + 1 : 2 * r + 2] = total[COLS_DEV - 1 : COLS_DEV]
+
+
+def main_part(
+    neighbors, incoming, mixed, pixels, mixing, upstream, slope, above, below, left, right, kernel
+):
     rows = pl.BlockSpec((2, COLS_DEV, C), lambda q, n: (q, 0, 0))
     once = pl.Buffered(1)
     return pl.pallas_call(
@@ -205,7 +243,9 @@
                 rows,
                 pl.BlockSpec((1, PIXB, K * BS), lambda q, n: (q, 0, 0)),
                 rows,
-                pl.BlockSpec(padded.shape, lambda q, n: (0, 0, 0), pipeline_mode=once),
+                pl.BlockSpec(slope.shape, lambda q, n: (0, 0, 0), pipeline_mode=once),
+                pl.BlockSpec(above.shape, lambda q, n: (0, 0, 0)),
+                pl.BlockSpec(below.shape, lambda q, n: (0, 0, 0)),
                 pl.BlockSpec(left.shape, lambda q, n: (0, 0)),
                 pl.BlockSpec(right.shape, lambda q, n: (0, 0)),
                 pl.BlockSpec((3, 3, C), lambda q, n: (0, 0, 0)),
@@ -213,6 +253,7 @@
             out_specs=[
                 pl.BlockSpec((1, PIXB, K * BS), lambda q, n: (q, 0, 0)),
                 rows,
+                pl.BlockSpec((4, C), lambda q, n: (0, 0)),
             ],
             scratch_shapes=[
                 pltpu.VMEM((PIXB, 2 * C), jnp.bfloat16),
@@ -222,27 +263,52 @@
         out_shape=[
             jax.ShapeDtypeStruct((PB, PIXB, K * BS), jnp.bfloat16),
             jax.ShapeDtypeStruct((ROWS_DEV, COLS_DEV, C), jnp.bfloat16),
+            jax.ShapeDtypeStruct((4, C), jnp.float32),
         ],
         compiler_params=pltpu.CompilerParams(vmem_limit_bytes=VMEM),
         cost_estimate=pl.CostEstimate(
             flops=2600 * MIB, bytes_accessed=30 * MIB, transcendentals=0
         ),
         name="main_part",
-    )(neighbors, incoming, mixed, pixels, mixing, upstream, padded, left, right, kernel)
-
-
-def return_kernel(targets, received, base, out, landed, sems, *totals):
+    )(
+        neighbors, incoming, mixed, pixels, mixing, upstream, slope, above, below, left, right,
+        kernel,
+    )
+
+
+def return_kernel(
+    targets, received, base, totals, gains, corner_0, corner_1, corner_2, corner_3, gradient,
+    out, fixed, landed, sems, tiles, tile_sems, *sums,
+):
     parts = received.shape[0] // OWNERS
 
     def fetch(i):
         part = pl.ds(i * OWNERS, OWNERS)
         return pltpu.make_async_copy(received.at[part], landed.at[part], sems.at[i])
 
+    def place(ref, i):
+        return ref.at[i // 2 * (ROWS_DEV - 1), pl.ds(i % 2 * (COLS_DEV - 16), 16)]
+
+    def load(i):
+        return pltpu.make_async_copy(place(gradient, i), tiles.at[i], tile_sems.at[i])
+
+    def store(i):
+        return pltpu.make_async_copy(tiles.at[i], place(fixed, i), tile_sems.at[i])
+
+    for i in range(4):
+        load(i).start()
     for i in range(parts):
         fetch(i).start()
-    totals[0][...] = base[...]
-    for total in totals[1:]:
+    sums[0][...] = base[...]
+    for total in sums[1:]:
         total[...] = jnp.zeros_like(total)
+    row = lax.broadcasted_iota(jnp.int32, (16, C), 0)
+    for i, corner in enumerate((corner_0, corner_1, corner_2, corner_3)):
+        load(i).wait()
+        value = totals[i : i + 1, :] + gains[i : i + 1, :] * corner[...]
+        tile = jnp.where(row == i % 2 * 15, value, tiles[i].astype(jnp.float32))
+        tiles[i] = tile.astype(jnp.bfloat16)
+        store(i).start()
 
     def body(i, carry):
         fetch(i).wait()
@@ -250,36 +316,44 @@
             for s in range(CAP):
                 o = i * OWNERS + j
                 block = targets[0, s, o]
-                totals[(j * CAP + s) % SPREAD][block] += landed[o, s].astype(jnp.float32)
+                sums[(j * CAP + s) % SPREAD][block] += landed[o, s].astype(jnp.float32)
         return carry
 
     lax.fori_loop(0, parts, body, 0)
-    whole = totals[0][...]
-    for total in totals[1:]:
+    whole = sums[0][...]
+    for total in sums[1:]:
         whole = whole + total[...]
     out[...] = whole.astype(jnp.bfloat16)
-
-
-def return_part(targets, received, base):
+    for i in range(4):
+        store(i).wait()
+
+
+def return_part(targets, received, base, totals, gains, corners, gradient):
     whole = pl.BlockSpec(memory_space=pltpu.VMEM)
+    anywhere = pl.BlockSpec(memory_space=pl.ANY)
+    parts = received.shape[0] // OWNERS
     return pl.pallas_call(
         return_kernel,
-        in_specs=[
-            pl.BlockSpec(memory_space=pltpu.SMEM),
-            pl.BlockSpec(memory_space=pl.ANY),
-            whole,
-        ],
-        out_specs=whole,
+        in_specs=[pl.BlockSpec(memory_space=pltpu.SMEM), anywhere]
+        + [whole] * 7
+        + [anywhere],
+        out_specs=[whole, anywhere],
         scratch_shapes=[
             pltpu.VMEM(received.shape, jnp.bfloat16),
-            pltpu.SemaphoreType.DMA((received.shape[0] // OWNERS,)),
+            pltpu.SemaphoreType.DMA((parts,)),
+            pltpu.VMEM((4, 16, C), jnp.bfloat16),
+            pltpu.SemaphoreType.DMA((4,)),
         ]
         + [pltpu.VMEM((BLK_DEV, BS, C), jnp.float32)] * SPREAD,
-        out_shape=jax.ShapeDtypeStruct((BLK_DEV, BS, C), jnp.bfloat16),
+        out_shape=[
+            jax.ShapeDtypeStruct((BLK_DEV, BS, C), jnp.bfloat16),
+            jax.ShapeDtypeStruct(gradient.shape, jnp.bfloat16),
+        ],
+        input_output_aliases={9: 1},
         compiler_params=pltpu.CompilerParams(vmem_limit_bytes=VMEM),
         cost_estimate=pl.CostEstimate(flops=4 * MIB, bytes_accessed=6 * MIB, transcendentals=0),
         name="return_part",
-    )(targets, received, base)
+    )(targets, received, base, totals, gains, *corners, gradient)
 
 
 def shifted(block, tiles, cams, tile_step, cam_step):
@@ -314,9 +388,6 @@
     targets = jnp.transpose(send_list, (0, 2, 1))
     reads = neighbors.T
     blocks = (BLK_DEV, BS, C)
-    move = functools.partial(shifted, tiles=tiles, cams=cams)
-    above = move(slope_of(pixel_upstream[-1:], pixel_hidden[-1:]), tile_step=0, cam_step=1)
-    below = move(slope_of(pixel_upstream[:1], pixel_hidden[:1]), tile_step=0, cam_step=-1)
     outgoing, point_slope = pack(
         targets,
         points.reshape(blocks),
@@ -324,24 +395,20 @@
         point_upstream.reshape(blocks),
         devices,
     )
-    outgoing, reads, above, below = lax.optimization_barrier((outgoing, reads, above, below))
+    outgoing, reads = lax.optimization_barrier((outgoing, reads))
     incoming = lax.all_to_all(
         outgoing, ("tile", "cam"), split_axis=0, concat_axis=0, tiled=True
     )
     pixel_slope, mixed, sums, first, last = pixel_part(
         reads, pixel_hidden, pixel_upstream, mixing, pixel_weight, slots
     )
-    padded = jnp.concatenate([above, pixel_slope, below], axis=0)
-    first = jnp.concatenate(
-        [above[:, 0].astype(jnp.float32), first, below[:, 0].astype(jnp.float32)], axis=0
-    )
-    last = jnp.concatenate(
-        [above[:, -1].astype(jnp.float32), last, below[:, -1].astype(jnp.float32)], axis=0
-    )
+    move = functools.partial(shifted, tiles=tiles, cams=cams)
+    above = move(pixel_slope[-1:], tile_step=0, cam_step=1)
+    below = move(pixel_slope[:1], tile_step=0, cam_step=-1)
     rim_left = move(last, tile_step=1, cam_step=0)
     rim_right = move(first, tile_step=-1, cam_step=0)
-    sums, incoming, rim_left, rim_right, padded = lax.optimization_barrier(
-        (sums, incoming, rim_left, rim_right, padded)
+    sums, incoming, above, below, rim_left, rim_right, point_slope = lax.optimization_barrier(
+        (sums, incoming, above, below, rim_left, rim_right, point_slope)
     )
     received = lax.all_to_all(
         sums.reshape(devices, CAP, BS, C),
@@ -350,14 +417,24 @@
         concat_axis=0,
         tiled=True,
     )
-    mixing_gradient, pixel_gradient = main_part(
-        reads, incoming, mixed, pixels, mixing, pixel_upstream, padded, rim_left, rim_right, kernel
-    )
     base = point_upstream.astype(jnp.float32) + jnp.dot(
         point_slope.reshape(BLK_DEV * BS, C), point_weight.T, preferred_element_type=jnp.float32
     )
-    base, pixel_gradient = lax.optimization_barrier((base, pixel_gradient))
-    point_gradient = return_part(targets, received, base.reshape(blocks))
+    base, first, last = lax.optimization_barrier((base, first, last))
+    corners = (
+        move(last[-1:], tile_step=1, cam_step=1),
+        move(first[-1:], tile_step=-1, cam_step=1),
+        move(last[:1], tile_step=1, cam_step=-1),
+        move(first[:1], tile_step=-1, cam_step=-1),
+    )
+    mixing_gradient, pixel_gradient, totals = main_part(
+        reads, incoming, mixed, pixels, mixing, pixel_upstream,
+        pixel_slope, above, below, rim_left, rim_right, kernel,
+    )
+    gains = jnp.stack([kernel[2, 2], kernel[2, 0], kernel[0, 2], kernel[0, 0]])
+    point_gradient, pixel_gradient = return_part(
+        targets, received, base.reshape(blocks), totals, gains, corners, pixel_gradient
+    )
     return (pixel_gradient, point_gradient.reshape(BLK_DEV * BS, C), mixing_gradient)
 
 

time: 193 us -> 188 us (0.974)
  waiting for transfers between devices: 87.4 us -> 74.1 us
  starting transfers between devices: 29.1 us -> 37.3 us
  other arithmetic: 5.65 us -> 0.59 us
  local copies, waits for them, and re-layouts: 0.02 us -> 3.01 us
  Pallas kernels: 67 us -> 69.4 us
    ppermute x4 -> x8, waiting for transfers between devices: 9.11 us -> 60.8 us  [shifted(): return lax.ppermute(block, ('tile', 'cam'), pairs)]
    all_to_all x1, waiting for transfers between devices: 54.7 us -> 7.73 us  [per_device(): lax.all_to_all(outgoing, ('tile', 'cam'), split_axis=0, concat_axis=0, ti...]
    all_to_all x1, waiting for transfers between devices: 23.6 us -> 5.53 us  [per_device(): lax.all_to_all(sums.reshape(devices, CAP, BS, C), ('tile', 'cam'), split_...]
    ppermute x4 -> x8, starting transfers between devices: 10.8 us -> 19.5 us  [shifted(): return lax.ppermute(block, ('tile', 'cam'), pairs)]
    concatenate x3 -> x0, other arithmetic: 4.77 us -> none  [the longest x1 3.24 us: per_device(): padded = jnp.concatenate([above, pixel_slope, below], axis=0)]
    slice x0 -> x3, local copies, waits for them, and re-layouts: none -> 2.2 us  [the longest x1 0.78 us: per_device(): below = move(pixel_slope[:1], tile_step=0, cam_step=-1)]
  transfers between devices with their start and end apart: 6 -> 10, of which waited for: 4 -> 7; matrix products, arithmetic and copies ran while one was open for 3% -> 3% of each run, Pallas kernels for 33% -> 31%
where the time goes in v4:
time: 188 us; the launch traced here: 187 us
  waiting for transfers between devices  74.1 us (39%)
  Pallas kernels  69.4 us (37%)
  starting transfers between devices  37.3 us (20%)
  local copies, waits for them, and re-layouts  3.01 us (2%)
    ppermute x8, waiting for transfers between devices, shifted(): return lax.ppermute(block, ('tile', 'cam'), pairs)  60.8 us
    pallas_call x1, Pallas kernels, main_part(): pl.pallas_call(main_kernel, grid_spec=pltpu.PrefetchScalarGridSpec(num_sc...  29.5 us
    pallas_call x1, Pallas kernels, pixel_part(): pl.pallas_call(pixel_kernel, grid_spec=pltpu.PrefetchScalarGridSpec(num_s...  29 us
    ppermute x8, starting transfers between devices, shifted(): return lax.ppermute(block, ('tile', 'cam'), pairs)  19.5 us
    all_to_all x1, starting transfers between devices, per_device(): lax.all_to_all(outgoing, ('tile', 'cam'), split_axis=0, concat_axis=0, ti...  12 us
    all_to_all x1, waiting for transfers between devices, per_device(): lax.all_to_all(outgoing, ('tile', 'cam'), split_axis=0, concat_axis=0, ti...  7.73 us
    pallas_call x1, Pallas kernels, pack(): pl.pallas_call(pack_kernel, in_specs=[pl.BlockSpec(memory_space=pltpu.SME...  5.98 us
    all_to_all x1, starting transfers between devices, per_device(): lax.all_to_all(sums.reshape(devices, CAP, BS, C), ('tile', 'cam'), split_...  5.86 us
  transfers between devices with their start and end apart: 10, of which 7 were waited for; matrix products, arithmetic and copies ran while one was open for 3% of the time, Pallas kernels for 31%

profile of v4, /device:TPU:1, one launch (start us, length us, event | category | flops | bytes accessed | tf_op | source)
XLA Modules:
  0.0 186.5 jit_solution(5269458596599273884)
XLA Ops:
  0.6 0.0 copy-start
  0.6 6.0 %pack.1 = (bf16[128,4,64,128]{3,2,1,0:T(8,128)(2,1)}, bf16[32,64,128]{2,1,0:T(8,128)(2,1)}) custom-call(s32[1,2,128]{2,1,0:T(2,128)} %bitcast.27, bf16[32,64,128]{2,1,0:T(8,128)(2,1)} %bitcast.22, bf16[32,64,128]{2,1,0:T(8,128)(2,1)} %bitcast.23, bf16[32,64,128]{2,1,0:T(8,128)(2,1)} %bitcast.21), custom_call_target="tpu_custom_call" | custom-call | flops 10485760 | bytes 12582912 | tf_op jit(solution)/shard_map/pack/pallas_call | solution.py:73
  6.6 12.0 %all-to-all-start = ((bf16[128,4,64,128]{3,2,1,0:T(8,128)(2,1)}), bf16[128,4,64,128]{3,2,1,0:T(8,128)(2,1)}, u32[]{:S(2)}, u32[]{:S(2)}) async-start(bf16[128,4,64,128]{3,2,1,0:T(8,128)(2,1)} %get-tuple-element.30), calls=%async_computation | async-start | bytes 16777216 | tf_op jit(solution)/shard_map/all_to_all | solution.py:399
  18.6 29.0 %pixel_part.1 = (bf16[64,128,128]{2,1,0:T(8,128)(2,1)}, bf16[32,256,128]{2,1,0:T(8,128)(2,1)}, bf16[256,64,128]{2,1,0:T(8,128)(2,1)}, f32[64,128]{1,0:T(8,128)}, f32[64,128]{1,0:T(8,128)}) custom-call(s32[6,32]{1,0:T(8,128)} %bitcast.25, bf16[64,128,128]{2,1,0:T(8,128)(2,1)} %hidden.1, bf16[64,128,128]{2,1,0:T(8,128)(2,1)} %upstream.3, ...), custom_call_target="tpu_custom_call" | custom-call | flops 1258291200 | bytes 18874368 | tf_op jit(solution)/shard_map/pixel_part/pallas_call | solution.py:129
  47.6 0.8 fusion
  48.4 3.3 %collective-permute-start = (bf16[1,128,128]{2,1,0:T(8,128)(2,1)S(1)}, bf16[1,128,128]{2,1,0:T(8,128)(2,1)S(1)}, u32[]{:S(2)}, u32[]{:S(2)}) collective-permute-start(bf16[1,128,128]{2,1,0:T(8,128)(2,1)S(1)} %get-tuple-element.52), channel_id=1, source_target_pairs={{0,1},{1,2},{2,3},{4,5},{5,6},{6,7},{8,9},{9,10},{10,11},{12,13},{... | collective-permute-start | bytes 98312 | tf_op jit(solution)/shard_map/ppermute | solution.py:367
  51.7 1.3 collective-permute-start.1
  53.0 3.7 %collective-permute-start.2 = (f32[64,128]{1,0:T(8,128)}, f32[64,128]{1,0:T(8,128)S(1)}, u32[]{:S(2)}, u32[]{:S(2)}) collective-permute-start(f32[64,128]{1,0:T(8,128)} %get-tuple-element.45), channel_id=1, source_target_pairs={{0,4},{1,5},{2,6},{3,7},{4,8},{5,9},{6,10},{7,11},{12,16},{13,17},... | collective-permute-start | bytes 98312 | tf_op jit(solution)/shard_map/ppermute | solution.py:367
  56.7 1.9 %collective-permute-start.3 = (f32[64,128]{1,0:T(8,128)}, f32[64,128]{1,0:T(8,128)S(1)}, u32[]{:S(2)}, u32[]{:S(2)}) collective-permute-start(f32[64,128]{1,0:T(8,128)} %get-tuple-element.46), channel_id=1, source_target_pairs={{0,124},{1,125},{2,126},{3,127},{4,0},{5,1},{6,2},{7,3},{8,4},{9,5... | collective-permute-start | bytes 98312 | tf_op jit(solution)/shard_map/ppermute | solution.py:367
  58.7 48.8 %collective-permute-done.above = bf16[1,128,128]{2,1,0:T(8,128)(2,1)S(1)} collective-permute-done((bf16[1,128,128]{2,1,0:T(8,128)(2,1)S(1)}, bf16[1,128,128]{2,1,0:T(8,128)(2,1)S(1)}, u32[]{:S(2)}, u32[]{:S(2)}) %collective-permute-start) | collective-permute-done | bytes 32800 | tf_op jit(solution)/shard_map/ppermute | solution.py:367
  107.4 0.0 copy-start.3
  107.4 7.2 %collective-permute-done.1.below = bf16[1,128,128]{2,1,0:T(8,128)(2,1)S(1)} collective-permute-done((bf16[1,128,128]{2,1,0:T(8,128)(2,1)S(1)}, bf16[1,128,128]{2,1,0:T(8,128)(2,1)S(1)}, u32[]{:S(2)}, u32[]{:S(2)}) %collective-permute-start.1) | collective-permute-done | bytes 32800 | tf_op jit(solution)/shard_map/ppermute | solution.py:367
  114.7 0.0 copy-start.4
  114.7 0.0 collective-permute-done.2.left
  114.7 0.0 copy-start.5
  114.7 0.0 collective-permute-done.3.right
  114.7 0.0 copy-start.6
  114.7 7.7 %all-to-all-done.incoming = bf16[128,4,64,128]{3,2,1,0:T(8,128)(2,1)} async-done(((bf16[128,4,64,128]{3,2,1,0:T(8,128)(2,1)}), bf16[128,4,64,128]{3,2,1,0:T(8,128)(2,1)}, u32[]{:S(2)}, u32[]{:S(2)}) %all-to-all-start) | async-done | bytes 8388640 | tf_op jit(solution)/shard_map/all_to_all | solution.py:399
  122.4 0.0 copy-start.1
  122.4 0.0 copy-start.2
  122.4 0.0 copy-done.3
  122.4 0.0 copy-done.4
  122.4 0.0 copy-done.5
  122.4 0.0 copy-done.6
  122.4 5.9 %all-to-all-start.1 = ((bf16[128,2,64,128]{3,2,1,0:T(8,128)(2,1)}), bf16[128,2,64,128]{3,2,1,0:T(8,128)(2,1)}, u32[]{:S(2)}, u32[]{:S(2)}) async-start(bf16[128,2,64,128]{3,2,1,0:T(8,128)(2,1)} %bitcast.19), calls=%async_computation.1 | async-start | bytes 8388608 | tf_op jit(solution)/shard_map/all_to_all | solution.py:413
  128.3 0.8 slice_bitcast_fusion.3
  129.1 0.6 pad_maximum_fusion.gains
  129.7 0.0 copy-done
  129.7 0.0 copy-done.1
  129.7 0.0 copy-done.2
  129.7 1.3 convolution_add_fusion
  131.0 0.7 fusion.2
  131.7 4.7 %collective-permute-start.4 = (f32[1,128]{1,0:T(1,128)S(1)}, f32[1,128]{1,0:T(1,128)S(1)}, u32[]{:S(2)}, u32[]{:S(2)}) collective-permute-start(f32[1,128]{1,0:T(1,128)S(1)} %get-tuple-element.56), channel_id=1, source_target_pairs={{0,5},{1,6},{2,7},{4,9},{5,10},{6,11},{12,17},{13,18},{14,19},{16,... | collective-permute-start | bytes 1544 | tf_op jit(solution)/shard_map/ppermute | solution.py:367
  136.4 0.7 fusion.1
  137.1 2.0 %collective-permute-start.5 = (f32[1,128]{1,0:T(1,128)S(1)}, f32[1,128]{1,0:T(1,128)S(1)}, u32[]{:S(2)}, u32[]{:S(2)}) collective-permute-start(f32[1,128]{1,0:T(1,128)S(1)} %get-tuple-element.54), channel_id=1, source_target_pairs={{0,125},{1,126},{2,127},{4,1},{5,2},{6,3},{8,5},{9,6},{10,7},{16,1... | collective-permute-start | bytes 1544 | tf_op jit(solution)/shard_map/ppermute | solution.py:367
  139.1 1.3 collective-permute-start.6
  140.4 1.3 collective-permute-start.7
  141.7 29.5 %main_part.1 = (bf16[32,256,384]{2,1,0:T(8,128)(2,1)}, bf16[64,128,128]{2,1,0:T(8,128)(2,1)}, f32[4,128]{1,0:T(4,128)}) custom-call(s32[6,32]{1,0:T(8,128)} %bitcast.26, bf16[128,4,64,128]{3,2,1,0:T(8,128)(2,1)} %all-to-all-done.incoming, bf16[32,256,128]{2,1,0:T(8,128)(2,1)} %get-tuple-element.39.mixed, bf16[64,128,128]{2,1,0:T(8,128)(2,1)} %pixels.1, ...), custom_call_target="tpu_custom_call" | custom-call | flops 2726297600 | bytes 31457280 | tf_op jit(solution)/shard_map/main_part/pallas_call | solution.py:235
  171.2 0.5 collective-permute-done.4.corner_0
  171.7 0.0 copy-start.7
  171.7 0.0 collective-permute-done.5.corner_1
  171.7 0.0 copy-start.8
  171.7 3.1 %collective-permute-done.6.corner_2 = f32[1,128]{1,0:T(1,128)S(1)} collective-permute-done((f32[1,128]{1,0:T(1,128)S(1)}, f32[1,128]{1,0:T(1,128)S(1)}, u32[]{:S(2)}, u32[]{:S(2)}) %collective-permute-start.6) | collective-permute-done | bytes 544 | tf_op jit(solution)/shard_map/ppermute | solution.py:367
  174.9 0.0 copy-start.9
  174.9 1.2 collective-permute-done.7.corner_3
  176.0 0.0 copy-start.10
  176.0 5.5 %all-to-all-done.1.received = bf16[128,2,64,128]{3,2,1,0:T(8,128)(2,1)} async-done(((bf16[128,2,64,128]{3,2,1,0:T(8,128)(2,1)}), bf16[128,2,64,128]{3,2,1,0:T(8,128)(2,1)}, u32[]{:S(2)}, u32[]{:S(2)}) %all-to-all-start.1) | async-done | bytes 4194336 | tf_op jit(solution)/shard_map/all_to_all | solution.py:413
  181.5 0.0 copy-done.7
  181.6 0.0 copy-done.8
  181.6 0.0 copy-done.9
  181.6 0.0 copy-done.10
  181.6 4.9 %return_part.1 = (bf16[32,64,128]{2,1,0:T(8,128)(2,1)}, bf16[64,128,128]{2,1,0:T(8,128)(2,1)}) custom-call(s32[1,2,128]{2,1,0:T(2,128)} %bitcast.28, bf16[128,2,64,128]{3,2,1,0:T(8,128)(2,1)} %all-to-all-done.1.received, f32[32,64,128]{2,1,0:T(8,128)} %bitcast.20, f32[4,128]{1,0:T(4,128)} %get-tuple-element.44.totals, ...), custom_call_target="tpu_custom_call", output_to_operand_aliasing={{1}: (9, {})} | custom-call | flops 4194304 | bytes 6291456 | tf_op jit(solution)/shard_map/return_part/pallas_call | solution.py:335
Async XLA Ops:
  0.6 129.0 %copy-start = (bf16[128,128]{1,0:T(8,128)(2,1)S(1)}, bf16[128,128]{1,0:T(8,128)(2,1)}, u32[]{:S(2)}) copy-start(bf16[128,128]{1,0:T(8,128)(2,1)} %param.22) | copy-start | bytes 98308
  6.6 115.8 %all-to-all-start = ((bf16[128,4,64,128]{3,2,1,0:T(8,128)(2,1)}), bf16[128,4,64,128]{3,2,1,0:T(8,128)(2,1)}, u32[]{:S(2)}, u32[]{:S(2)}) async-start(bf16[128,4,64,128]{3,2,1,0:T(8,128)(2,1)} %get-tuple-element.30), calls=%async_computation | async-start | bytes 16777216 | tf_op jit(solution)/shard_map/all_to_all | solution.py:399
  48.4 59.0 %collective-permute-start = (bf16[1,128,128]{2,1,0:T(8,128)(2,1)S(1)}, bf16[1,128,128]{2,1,0:T(8,128)(2,1)S(1)}, u32[]{:S(2)}, u32[]{:S(2)}) collective-permute-start(bf16[1,128,128]{2,1,0:T(8,128)(2,1)S(1)} %get-tuple-element.52), channel_id=1, source_target_pairs={{0,1},{1,2},{2,3},{4,5},{5,6},{6,7},{8,9},{9,10},{10,11},{12,13},{... | collective-permute-start | bytes 98312 | tf_op jit(solution)/shard_map/ppermute | solution.py:367
  51.7 63.0 %collective-permute-start.1 = (bf16[1,128,128]{2,1,0:T(8,128)(2,1)S(1)}, bf16[1,128,128]{2,1,0:T(8,128)(2,1)S(1)}, u32[]{:S(2)}, u32[]{:S(2)}) collective-permute-start(bf16[1,128,128]{2,1,0:T(8,128)(2,1)S(1)} %get-tuple-element.51), channel_id=1, source_target_pairs={{1,0},{2,1},{3,2},{5,4},{6,5},{7,6},{9,8},{10,9},{11,10},{13,12},{... | collective-permute-start | bytes 98312 | tf_op jit(solution)/shard_map/ppermute | solution.py:367
  53.0 61.7 %collective-permute-start.2 = (f32[64,128]{1,0:T(8,128)}, f32[64,128]{1,0:T(8,128)S(1)}, u32[]{:S(2)}, u32[]{:S(2)}) collective-permute-start(f32[64,128]{1,0:T(8,128)} %get-tuple-element.45), channel_id=1, source_target_pairs={{0,4},{1,5},{2,6},{3,7},{4,8},{5,9},{6,10},{7,11},{12,16},{13,17},... | collective-permute-start | bytes 98312 | tf_op jit(solution)/shard_map/ppermute | solution.py:367
  56.7 57.9 %collective-permute-start.3 = (f32[64,128]{1,0:T(8,128)}, f32[64,128]{1,0:T(8,128)S(1)}, u32[]{:S(2)}, u32[]{:S(2)}) collective-permute-start(f32[64,128]{1,0:T(8,128)} %get-tuple-element.46), channel_id=1, source_target_pairs={{0,124},{1,125},{2,126},{3,127},{4,0},{5,1},{6,2},{7,3},{8,4},{9,5... | collective-permute-start | bytes 98312 | tf_op jit(solution)/shard_map/ppermute | solution.py:367
  107.4 15.0 %copy-start.3 = (bf16[1,128,128]{2,1,0:T(8,128)(2,1)}, bf16[1,128,128]{2,1,0:T(8,128)(2,1)S(1)}, u32[]{:S(2)}) copy-start(bf16[1,128,128]{2,1,0:T(8,128)(2,1)S(1)} %collective-permute-done.above) | copy-start | bytes 98308
  114.7 7.8 %copy-start.4 = (bf16[1,128,128]{2,1,0:T(8,128)(2,1)}, bf16[1,128,128]{2,1,0:T(8,128)(2,1)S(1)}, u32[]{:S(2)}) copy-start(bf16[1,128,128]{2,1,0:T(8,128)(2,1)S(1)} %collective-permute-done.1.below) | copy-start | bytes 98308
  114.7 7.8 %copy-start.5 = (f32[64,128]{1,0:T(8,128)}, f32[64,128]{1,0:T(8,128)S(1)}, u32[]{:S(2)}) copy-start(f32[64,128]{1,0:T(8,128)S(1)} %collective-permute-done.2.left) | copy-start | bytes 98308
  114.7 7.8 %copy-start.6 = (f32[64,128]{1,0:T(8,128)}, f32[64,128]{1,0:T(8,128)S(1)}, u32[]{:S(2)}) copy-start(f32[64,128]{1,0:T(8,128)S(1)} %collective-permute-done.3.right) | copy-start | bytes 98308
  122.4 7.3 %copy-start.1 = (bf16[2048,128]{1,0:T(8,128)(2,1)S(1)}, bf16[2048,128]{1,0:T(8,128)(2,1)}, u32[]{:S(2)}) copy-start(bf16[2048,128]{1,0:T(8,128)(2,1)} %param.17) | copy-start | bytes 1572868
  122.4 7.3 %copy-start.2 = (bf16[32,64,128]{2,1,0:T(8,128)(2,1)S(1)}, bf16[32,64,128]{2,1,0:T(8,128)(2,1)}, u32[]{:S(2)}) copy-start(bf16[32,64,128]{2,1,0:T(8,128)(2,1)} %get-tuple-element.36) | copy-start | bytes 1572868
  122.4 59.1 %all-to-all-start.1 = ((bf16[128,2,64,128]{3,2,1,0:T(8,128)(2,1)}), bf16[128,2,64,128]{3,2,1,0:T(8,128)(2,1)}, u32[]{:S(2)}, u32[]{:S(2)}) async-start(bf16[128,2,64,128]{3,2,1,0:T(8,128)(2,1)} %bitcast.19), calls=%async_computation.1 | async-start | bytes 8388608 | tf_op jit(solution)/shard_map/all_to_all | solution.py:413
  131.7 40.0 %collective-permute-start.4 = (f32[1,128]{1,0:T(1,128)S(1)}, f32[1,128]{1,0:T(1,128)S(1)}, u32[]{:S(2)}, u32[]{:S(2)}) collective-permute-start(f32[1,128]{1,0:T(1,128)S(1)} %get-tuple-element.56), channel_id=1, source_target_pairs={{0,5},{1,6},{2,7},{4,9},{5,10},{6,11},{12,17},{13,18},{14,19},{16,... | collective-permute-start | bytes 1544 | tf_op jit(solution)/shard_map/ppermute | solution.py:367
  137.1 34.6 %collective-permute-start.5 = (f32[1,128]{1,0:T(1,128)S(1)}, f32[1,128]{1,0:T(1,128)S(1)}, u32[]{:S(2)}, u32[]{:S(2)}) collective-permute-start(f32[1,128]{1,0:T(1,128)S(1)} %get-tuple-element.54), channel_id=1, source_target_pairs={{0,125},{1,126},{2,127},{4,1},{5,2},{6,3},{8,5},{9,6},{10,7},{16,1... | collective-permute-start | bytes 1544 | tf_op jit(solution)/shard_map/ppermute | solution.py:367
  139.1 35.8 %collective-permute-start.6 = (f32[1,128]{1,0:T(1,128)S(1)}, f32[1,128]{1,0:T(1,128)S(1)}, u32[]{:S(2)}, u32[]{:S(2)}) collective-permute-start(f32[1,128]{1,0:T(1,128)S(1)} %get-tuple-element.55), channel_id=1, source_target_pairs={{1,4},{2,5},{3,6},{5,8},{6,9},{7,10},{13,16},{14,17},{15,18},{17,2... | collective-permute-start | bytes 1544 | tf_op jit(solution)/shard_map/ppermute | solution.py:367
  140.4 35.6 %collective-permute-start.7 = (f32[1,128]{1,0:T(1,128)S(1)}, f32[1,128]{1,0:T(1,128)S(1)}, u32[]{:S(2)}, u32[]{:S(2)}) collective-permute-start(f32[1,128]{1,0:T(1,128)S(1)} %get-tuple-element.53), channel_id=1, source_target_pairs={{1,124},{2,125},{3,126},{5,0},{6,1},{7,2},{9,4},{10,5},{11,6},{17,... | collective-permute-start | bytes 1544 | tf_op jit(solution)/shard_map/ppermute | solution.py:367
  171.7 9.8 %copy-start.7 = (f32[1,128]{1,0:T(1,128)}, f32[1,128]{1,0:T(1,128)S(1)}, u32[]{:S(2)}) copy-start(f32[1,128]{1,0:T(1,128)S(1)} %collective-permute-done.4.corner_0) | copy-start | bytes 1540
  171.7 9.8 %copy-start.8 = (f32[1,128]{1,0:T(1,128)}, f32[1,128]{1,0:T(1,128)S(1)}, u32[]{:S(2)}) copy-start(f32[1,128]{1,0:T(1,128)S(1)} %collective-permute-done.5.corner_1) | copy-start | bytes 1540
  174.9 6.7 %copy-start.9 = (f32[1,128]{1,0:T(1,128)}, f32[1,128]{1,0:T(1,128)S(1)}, u32[]{:S(2)}) copy-start(f32[1,128]{1,0:T(1,128)S(1)} %collective-permute-done.6.corner_2) | copy-start | bytes 1540
  176.0 5.5 %copy-start.10 = (f32[1,128]{1,0:T(1,128)}, f32[1,128]{1,0:T(1,128)S(1)}, u32[]{:S(2)}) copy-start(f32[1,128]{1,0:T(1,128)S(1)} %collective-permute-done.7.corner_3) | copy-start | bytes 1540

commit v5 on v4

--- a/solution.py
+++ b/solution.py
@@ -21,7 +21,7 @@
 VMEM = 60 * MIB
 DESTS = 4
 OWNERS = 16
-SPREAD = 4
+SPREAD = 2
 
 
 def slope_of(upstream, hidden):
@@ -31,18 +31,7 @@
     return (upstream.astype(jnp.float32) * slope).astype(jnp.bfloat16)
 
 
-def pack_kernel(
-    targets, points_in, hidden_in, upstream_in, out, slope, points, hidden, upstream, sem, sems
-):
-    loads = [
-        pltpu.make_async_copy(source, target, sems.at[i])
-        for i, (source, target) in enumerate(
-            ((points_in, points), (hidden_in, hidden), (upstream_in, upstream))
-        )
-    ]
-    for load in loads:
-        load.start()
-
+def pack_kernel(targets, points, hidden, upstream, out, slope, sem):
     def send(source, first):
         def body(i, carry):
             for j in range(DESTS):
@@ -59,27 +48,23 @@
         slope[part] = slope_of(upstream[part], hidden[part])
         return carry
 
-    loads[0].wait()
     send(points, 0)
-    loads[1].wait()
-    loads[2].wait()
     lax.fori_loop(0, BLK_DEV // 2, fill, 0)
     send(slope, CAP)
     pltpu.make_async_copy(out, out, sem).wait()
 
 
 def pack(targets, points, hidden, upstream, devices):
-    anywhere = pl.BlockSpec(memory_space=pl.ANY)
+    whole = pl.BlockSpec(memory_space=pltpu.VMEM)
     return pl.pallas_call(
         pack_kernel,
-        in_specs=[pl.BlockSpec(memory_space=pltpu.SMEM), anywhere, anywhere, anywhere],
-        out_specs=[anywhere, pl.BlockSpec(memory_space=pltpu.VMEM)],
+        in_specs=[pl.BlockSpec(memory_space=pltpu.SMEM), whole, whole, whole],
+        out_specs=[pl.BlockSpec(memory_space=pl.ANY), whole],
         out_shape=[
             jax.ShapeDtypeStruct((devices, 2 * CAP, BS, C), jnp.bfloat16),
             jax.ShapeDtypeStruct((BLK_DEV, BS, C), jnp.bfloat16),
         ],
-        scratch_shapes=[pltpu.VMEM((BLK_DEV, BS, C), jnp.bfloat16)] * 3
-        + [pltpu.SemaphoreType.DMA(()), pltpu.SemaphoreType.DMA((3,))],
+        scratch_shapes=[pltpu.SemaphoreType.DMA(())],
         compiler_params=pltpu.CompilerParams(vmem_limit_bytes=VMEM),
         cost_estimate=pl.CostEstimate(flops=10 * MIB, bytes_accessed=12 * MIB, transcendentals=0),
         name="pack",
@@ -278,7 +263,7 @@
 
 def return_kernel(
     targets, received, base, totals, gains, corner_0, corner_1, corner_2, corner_3, gradient,
-    out, fixed, landed, sems, tiles, tile_sems, *sums,
+    out, fixed, landed, sems, tiles, tile_sems, start, start_sem, *sums,
 ):
     parts = received.shape[0] // OWNERS
 
@@ -299,8 +284,9 @@
         load(i).start()
     for i in range(parts):
         fetch(i).start()
-    sums[0][...] = base[...]
-    for total in sums[1:]:
+    first = pltpu.make_async_copy(base, start, start_sem)
+    first.start()
+    for total in sums:
         total[...] = jnp.zeros_like(total)
     row = lax.broadcasted_iota(jnp.int32, (16, C), 0)
     for i, corner in enumerate((corner_0, corner_1, corner_2, corner_3)):
@@ -320,8 +306,9 @@
         return carry
 
     lax.fori_loop(0, parts, body, 0)
-    whole = sums[0][...]
-    for total in sums[1:]:
+    first.wait()
+    whole = start[...]
+    for total in sums:
         whole = whole + total[...]
     out[...] = whole.astype(jnp.bfloat16)
     for i in range(4):
@@ -334,8 +321,8 @@
     parts = received.shape[0] // OWNERS
     return pl.pallas_call(
         return_kernel,
-        in_specs=[pl.BlockSpec(memory_space=pltpu.SMEM), anywhere]
-        + [whole] * 7
+        in_specs=[pl.BlockSpec(memory_space=pltpu.SMEM), anywhere, anywhere]
+        + [whole] * 6
         + [anywhere],
         out_specs=[whole, anywhere],
         scratch_shapes=[
@@ -343,6 +330,8 @@
             pltpu.SemaphoreType.DMA((parts,)),
             pltpu.VMEM((4, 16, C), jnp.bfloat16),
             pltpu.SemaphoreType.DMA((4,)),
+            pltpu.VMEM((BLK_DEV, BS, C), jnp.float32),
+            pltpu.SemaphoreType.DMA(()),
         ]
         + [pltpu.VMEM((BLK_DEV, BS, C), jnp.float32)] * SPREAD,
         out_shape=[

time: 188 us -> 188 us (level)
  no operation moved by 1% of the time
where the time goes in v5:
time: 188 us; the launch traced here: 186 us
  waiting for transfers between devices  74 us (39%)
  Pallas kernels  68.7 us (37%)
  starting transfers between devices  37.3 us (20%)
  local copies, waits for them, and re-layouts  3.01 us (2%)
    ppermute x8, waiting for transfers between devices, shifted(): return lax.ppermute(block, ('tile', 'cam'), pairs)  60.8 us
    pallas_call x1, Pallas kernels, main_part(): pl.pallas_call(main_kernel, grid_spec=pltpu.PrefetchScalarGridSpec(num_sc...  29.5 us
    pallas_call x1, Pallas kernels, pixel_part(): pl.pallas_call(pixel_kernel, grid_spec=pltpu.PrefetchScalarGridSpec(num_s...  29 us
    ppermute x8, starting transfers between devices, shifted(): return lax.ppermute(block, ('tile', 'cam'), pairs)  19.5 us
    all_to_all x1, starting transfers between devices, per_device(): lax.all_to_all(outgoing, ('tile', 'cam'), split_axis=0, concat_axis=0, ti...  12 us
    all_to_all x1, waiting for transfers between devices, per_device(): lax.all_to_all(outgoing, ('tile', 'cam'), split_axis=0, concat_axis=0, ti...  7.73 us
    all_to_all x1, starting transfers between devices, per_device(): lax.all_to_all(sums.reshape(devices, CAP, BS, C), ('tile', 'cam'), split_...  5.86 us
    all_to_all x1, waiting for transfers between devices, per_device(): lax.all_to_all(sums.reshape(devices, CAP, BS, C), ('tile', 'cam'), split_...  5.53 us
  transfers between devices with their start and end apart: 10, of which 7 were waited for; matrix products, arithmetic and copies ran while one was open for 3% of the time, Pallas kernels for 31%

profile of v5, /device:TPU:1, one launch (start us, length us, event | category | flops | bytes accessed | tf_op | source)
XLA Modules:
  0.0 185.8 jit_solution(8376503463365715787)
XLA Ops:
  0.6 0.0 copy-start
  0.6 5.5 %pack.1 = (bf16[128,4,64,128]{3,2,1,0:T(8,128)(2,1)}, bf16[32,64,128]{2,1,0:T(8,128)(2,1)}) custom-call(s32[1,2,128]{2,1,0:T(2,128)} %bitcast.27, bf16[32,64,128]{2,1,0:T(8,128)(2,1)} %bitcast.22, bf16[32,64,128]{2,1,0:T(8,128)(2,1)} %bitcast.23, bf16[32,64,128]{2,1,0:T(8,128)(2,1)} %bitcast.21), custom_call_target="tpu_custom_call" | custom-call | flops 10485760 | bytes 12582912 | tf_op jit(solution)/shard_map/pack/pallas_call | solution.py:59
  6.2 12.0 %all-to-all-start = ((bf16[128,4,64,128]{3,2,1,0:T(8,128)(2,1)}), bf16[128,4,64,128]{3,2,1,0:T(8,128)(2,1)}, u32[]{:S(2)}, u32[]{:S(2)}) async-start(bf16[128,4,64,128]{3,2,1,0:T(8,128)(2,1)} %get-tuple-element.30), calls=%async_computation | async-start | bytes 16777216 | tf_op jit(solution)/shard_map/all_to_all | solution.py:388
  18.1 29.0 %pixel_part.1 = (bf16[64,128,128]{2,1,0:T(8,128)(2,1)}, bf16[32,256,128]{2,1,0:T(8,128)(2,1)}, bf16[256,64,128]{2,1,0:T(8,128)(2,1)}, f32[64,128]{1,0:T(8,128)}, f32[64,128]{1,0:T(8,128)}) custom-call(s32[6,32]{1,0:T(8,128)} %bitcast.25, bf16[64,128,128]{2,1,0:T(8,128)(2,1)} %hidden.1, bf16[64,128,128]{2,1,0:T(8,128)(2,1)} %upstream.3, ...), custom_call_target="tpu_custom_call" | custom-call | flops 1258291200 | bytes 18874368 | tf_op jit(solution)/shard_map/pixel_part/pallas_call | solution.py:114
  47.1 0.8 fusion
  47.9 3.3 %collective-permute-start = (bf16[1,128,128]{2,1,0:T(8,128)(2,1)S(1)}, bf16[1,128,128]{2,1,0:T(8,128)(2,1)S(1)}, u32[]{:S(2)}, u32[]{:S(2)}) collective-permute-start(bf16[1,128,128]{2,1,0:T(8,128)(2,1)S(1)} %get-tuple-element.52), channel_id=1, source_target_pairs={{0,1},{1,2},{2,3},{4,5},{5,6},{6,7},{8,9},{9,10},{10,11},{12,13},{... | collective-permute-start | bytes 98312 | tf_op jit(solution)/shard_map/ppermute | solution.py:356
  51.2 1.3 collective-permute-start.1
  52.5 3.8 %collective-permute-start.2 = (f32[64,128]{1,0:T(8,128)}, f32[64,128]{1,0:T(8,128)S(1)}, u32[]{:S(2)}, u32[]{:S(2)}) collective-permute-start(f32[64,128]{1,0:T(8,128)} %get-tuple-element.45), channel_id=1, source_target_pairs={{0,4},{1,5},{2,6},{3,7},{4,8},{5,9},{6,10},{7,11},{12,16},{13,17},... | collective-permute-start | bytes 98312 | tf_op jit(solution)/shard_map/ppermute | solution.py:356
  56.3 1.9 %collective-permute-start.3 = (f32[64,128]{1,0:T(8,128)}, f32[64,128]{1,0:T(8,128)S(1)}, u32[]{:S(2)}, u32[]{:S(2)}) collective-permute-start(f32[64,128]{1,0:T(8,128)} %get-tuple-element.46), channel_id=1, source_target_pairs={{0,124},{1,125},{2,126},{3,127},{4,0},{5,1},{6,2},{7,3},{8,4},{9,5... | collective-permute-start | bytes 98312 | tf_op jit(solution)/shard_map/ppermute | solution.py:356
  58.2 48.8 %collective-permute-done.above = bf16[1,128,128]{2,1,0:T(8,128)(2,1)S(1)} collective-permute-done((bf16[1,128,128]{2,1,0:T(8,128)(2,1)S(1)}, bf16[1,128,128]{2,1,0:T(8,128)(2,1)S(1)}, u32[]{:S(2)}, u32[]{:S(2)}) %collective-permute-start) | collective-permute-done | bytes 32800 | tf_op jit(solution)/shard_map/ppermute | solution.py:356
  107.0 0.0 copy-start.3
  107.0 7.2 %collective-permute-done.1.below = bf16[1,128,128]{2,1,0:T(8,128)(2,1)S(1)} collective-permute-done((bf16[1,128,128]{2,1,0:T(8,128)(2,1)S(1)}, bf16[1,128,128]{2,1,0:T(8,128)(2,1)S(1)}, u32[]{:S(2)}, u32[]{:S(2)}) %collective-permute-start.1) | collective-permute-done | bytes 32800 | tf_op jit(solution)/shard_map/ppermute | solution.py:356
  114.2 0.0 copy-start.4
  114.2 0.0 collective-permute-done.2.left
  114.2 0.0 copy-start.5
  114.2 0.0 collective-permute-done.3.right
  114.2 0.0 copy-start.6
  114.2 7.7 %all-to-all-done.incoming = bf16[128,4,64,128]{3,2,1,0:T(8,128)(2,1)} async-done(((bf16[128,4,64,128]{3,2,1,0:T(8,128)(2,1)}), bf16[128,4,64,128]{3,2,1,0:T(8,128)(2,1)}, u32[]{:S(2)}, u32[]{:S(2)}) %all-to-all-start) | async-done | bytes 8388640 | tf_op jit(solution)/shard_map/all_to_all | solution.py:388
  121.9 0.0 copy-start.1
  121.9 0.0 copy-start.2
  121.9 0.0 copy-done.3
  121.9 0.0 copy-done.4
  121.9 0.0 copy-done.5
  122.0 0.0 copy-done.6
  122.0 5.9 %all-to-all-start.1 = ((bf16[128,2,64,128]{3,2,1,0:T(8,128)(2,1)}), bf16[128,2,64,128]{3,2,1,0:T(8,128)(2,1)}, u32[]{:S(2)}, u32[]{:S(2)}) async-start(bf16[128,2,64,128]{3,2,1,0:T(8,128)(2,1)} %bitcast.19), calls=%async_computation.1 | async-start | bytes 8388608 | tf_op jit(solution)/shard_map/all_to_all | solution.py:402
  127.8 0.8 slice_bitcast_fusion.3
  128.6 0.6 pad_maximum_fusion.gains
  129.2 0.0 copy-done
  129.2 0.0 copy-done.1
  129.2 0.0 copy-done.2
  129.2 1.3 convolution_add_fusion
  130.5 0.7 fusion.2
  131.2 4.7 %collective-permute-start.4 = (f32[1,128]{1,0:T(1,128)S(1)}, f32[1,128]{1,0:T(1,128)S(1)}, u32[]{:S(2)}, u32[]{:S(2)}) collective-permute-start(f32[1,128]{1,0:T(1,128)S(1)} %get-tuple-element.56), channel_id=1, source_target_pairs={{0,5},{1,6},{2,7},{4,9},{5,10},{6,11},{12,17},{13,18},{14,19},{16,... | collective-permute-start | bytes 1544 | tf_op jit(solution)/shard_map/ppermute | solution.py:356
  135.9 0.7 fusion.1
  136.6 2.0 %collective-permute-start.5 = (f32[1,128]{1,0:T(1,128)S(1)}, f32[1,128]{1,0:T(1,128)S(1)}, u32[]{:S(2)}, u32[]{:S(2)}) collective-permute-start(f32[1,128]{1,0:T(1,128)S(1)} %get-tuple-element.54), channel_id=1, source_target_pairs={{0,125},{1,126},{2,127},{4,1},{5,2},{6,3},{8,5},{9,6},{10,7},{16,1... | collective-permute-start | bytes 1544 | tf_op jit(solution)/shard_map/ppermute | solution.py:356
  138.6 1.3 collective-permute-start.6
  139.9 1.3 collective-permute-start.7
  141.2 29.5 %main_part.1 = (bf16[32,256,384]{2,1,0:T(8,128)(2,1)}, bf16[64,128,128]{2,1,0:T(8,128)(2,1)}, f32[4,128]{1,0:T(4,128)}) custom-call(s32[6,32]{1,0:T(8,128)} %bitcast.26, bf16[128,4,64,128]{3,2,1,0:T(8,128)(2,1)} %all-to-all-done.incoming, bf16[32,256,128]{2,1,0:T(8,128)(2,1)} %get-tuple-element.39.mixed, bf16[64,128,128]{2,1,0:T(8,128)(2,1)} %pixels.1, ...), custom_call_target="tpu_custom_call" | custom-call | flops 2726297600 | bytes 31457280 | tf_op jit(solution)/shard_map/main_part/pallas_call | solution.py:220
  170.7 0.5 collective-permute-done.4.corner_0
  171.3 0.0 copy-start.7
  171.3 0.0 collective-permute-done.5.corner_1
  171.3 0.0 copy-start.8
  171.3 3.1 %collective-permute-done.6.corner_2 = f32[1,128]{1,0:T(1,128)S(1)} collective-permute-done((f32[1,128]{1,0:T(1,128)S(1)}, f32[1,128]{1,0:T(1,128)S(1)}, u32[]{:S(2)}, u32[]{:S(2)}) %collective-permute-start.6) | collective-permute-done | bytes 544 | tf_op jit(solution)/shard_map/ppermute | solution.py:356
  174.4 0.0 copy-start.9
  174.4 1.2 collective-permute-done.7.corner_3
  175.5 0.0 copy-start.10
  175.5 5.5 %all-to-all-done.1.received = bf16[128,2,64,128]{3,2,1,0:T(8,128)(2,1)} async-done(((bf16[128,2,64,128]{3,2,1,0:T(8,128)(2,1)}), bf16[128,2,64,128]{3,2,1,0:T(8,128)(2,1)}, u32[]{:S(2)}, u32[]{:S(2)}) %all-to-all-start.1) | async-done | bytes 4194336 | tf_op jit(solution)/shard_map/all_to_all | solution.py:402
  181.1 0.0 copy-done.7
  181.1 0.0 copy-done.8
  181.1 0.0 copy-done.9
  181.1 0.0 copy-done.10
  181.1 4.7 %return_part.1 = (bf16[32,64,128]{2,1,0:T(8,128)(2,1)}, bf16[64,128,128]{2,1,0:T(8,128)(2,1)}) custom-call(s32[1,2,128]{2,1,0:T(2,128)} %bitcast.28, bf16[128,2,64,128]{3,2,1,0:T(8,128)(2,1)} %all-to-all-done.1.received, f32[32,64,128]{2,1,0:T(8,128)} %bitcast.20, f32[4,128]{1,0:T(4,128)} %get-tuple-element.44.totals, ...), custom_call_target="tpu_custom_call", output_to_operand_aliasing={{1}: (9, {})} | custom-call | flops 4194304 | bytes 6291456 | tf_op jit(solution)/shard_map/return_part/pallas_call | solution.py:322
Async XLA Ops:
  0.6 128.6 %copy-start = (bf16[128,128]{1,0:T(8,128)(2,1)S(1)}, bf16[128,128]{1,0:T(8,128)(2,1)}, u32[]{:S(2)}) copy-start(bf16[128,128]{1,0:T(8,128)(2,1)} %param.22) | copy-start | bytes 98308
  6.2 115.8 %all-to-all-start = ((bf16[128,4,64,128]{3,2,1,0:T(8,128)(2,1)}), bf16[128,4,64,128]{3,2,1,0:T(8,128)(2,1)}, u32[]{:S(2)}, u32[]{:S(2)}) async-start(bf16[128,4,64,128]{3,2,1,0:T(8,128)(2,1)} %get-tuple-element.30), calls=%async_computation | async-start | bytes 16777216 | tf_op jit(solution)/shard_map/all_to_all | solution.py:388
  47.9 59.0 %collective-permute-start = (bf16[1,128,128]{2,1,0:T(8,128)(2,1)S(1)}, bf16[1,128,128]{2,1,0:T(8,128)(2,1)S(1)}, u32[]{:S(2)}, u32[]{:S(2)}) collective-permute-start(bf16[1,128,128]{2,1,0:T(8,128)(2,1)S(1)} %get-tuple-element.52), channel_id=1, source_target_pairs={{0,1},{1,2},{2,3},{4,5},{5,6},{6,7},{8,9},{9,10},{10,11},{12,13},{... | collective-permute-start | bytes 98312 | tf_op jit(solution)/shard_map/ppermute | solution.py:356
  51.2 63.0 %collective-permute-start.1 = (bf16[1,128,128]{2,1,0:T(8,128)(2,1)S(1)}, bf16[1,128,128]{2,1,0:T(8,128)(2,1)S(1)}, u32[]{:S(2)}, u32[]{:S(2)}) collective-permute-start(bf16[1,128,128]{2,1,0:T(8,128)(2,1)S(1)} %get-tuple-element.51), channel_id=1, source_target_pairs={{1,0},{2,1},{3,2},{5,4},{6,5},{7,6},{9,8},{10,9},{11,10},{13,12},{... | collective-permute-start | bytes 98312 | tf_op jit(solution)/shard_map/ppermute | solution.py:356
  52.5 61.7 %collective-permute-start.2 = (f32[64,128]{1,0:T(8,128)}, f32[64,128]{1,0:T(8,128)S(1)}, u32[]{:S(2)}, u32[]{:S(2)}) collective-permute-start(f32[64,128]{1,0:T(8,128)} %get-tuple-element.45), channel_id=1, source_target_pairs={{0,4},{1,5},{2,6},{3,7},{4,8},{5,9},{6,10},{7,11},{12,16},{13,17},... | collective-permute-start | bytes 98312 | tf_op jit(solution)/shard_map/ppermute | solution.py:356
  56.3 57.9 %collective-permute-start.3 = (f32[64,128]{1,0:T(8,128)}, f32[64,128]{1,0:T(8,128)S(1)}, u32[]{:S(2)}, u32[]{:S(2)}) collective-permute-start(f32[64,128]{1,0:T(8,128)} %get-tuple-element.46), channel_id=1, source_target_pairs={{0,124},{1,125},{2,126},{3,127},{4,0},{5,1},{6,2},{7,3},{8,4},{9,5... | collective-permute-start | bytes 98312 | tf_op jit(solution)/shard_map/ppermute | solution.py:356
  107.0 15.0 %copy-start.3 = (bf16[1,128,128]{2,1,0:T(8,128)(2,1)}, bf16[1,128,128]{2,1,0:T(8,128)(2,1)S(1)}, u32[]{:S(2)}) copy-start(bf16[1,128,128]{2,1,0:T(8,128)(2,1)S(1)} %collective-permute-done.above) | copy-start | bytes 98308
  114.2 7.8 %copy-start.4 = (bf16[1,128,128]{2,1,0:T(8,128)(2,1)}, bf16[1,128,128]{2,1,0:T(8,128)(2,1)S(1)}, u32[]{:S(2)}) copy-start(bf16[1,128,128]{2,1,0:T(8,128)(2,1)S(1)} %collective-permute-done.1.below) | copy-start | bytes 98308
  114.2 7.8 %copy-start.5 = (f32[64,128]{1,0:T(8,128)}, f32[64,128]{1,0:T(8,128)S(1)}, u32[]{:S(2)}) copy-start(f32[64,128]{1,0:T(8,128)S(1)} %collective-permute-done.2.left) | copy-start | bytes 98308
  114.2 7.8 %copy-start.6 = (f32[64,128]{1,0:T(8,128)}, f32[64,128]{1,0:T(8,128)S(1)}, u32[]{:S(2)}) copy-start(f32[64,128]{1,0:T(8,128)S(1)} %collective-permute-done.3.right) | copy-start | bytes 98308
  121.9 7.3 %copy-start.1 = (bf16[2048,128]{1,0:T(8,128)(2,1)S(1)}, bf16[2048,128]{1,0:T(8,128)(2,1)}, u32[]{:S(2)}) copy-start(bf16[2048,128]{1,0:T(8,128)(2,1)} %param.17) | copy-start | bytes 1572868
  121.9 7.3 %copy-start.2 = (bf16[32,64,128]{2,1,0:T(8,128)(2,1)S(1)}, bf16[32,64,128]{2,1,0:T(8,128)(2,1)}, u32[]{:S(2)}) copy-start(bf16[32,64,128]{2,1,0:T(8,128)(2,1)} %get-tuple-element.36) | copy-start | bytes 1572868
  122.0 59.1 %all-to-all-start.1 = ((bf16[128,2,64,128]{3,2,1,0:T(8,128)(2,1)}), bf16[128,2,64,128]{3,2,1,0:T(8,128)(2,1)}, u32[]{:S(2)}, u32[]{:S(2)}) async-start(bf16[128,2,64,128]{3,2,1,0:T(8,128)(2,1)} %bitcast.19), calls=%async_computation.1 | async-start | bytes 8388608 | tf_op jit(solution)/shard_map/all_to_all | solution.py:402
  131.2 40.0 %collective-permute-start.4 = (f32[1,128]{1,0:T(1,128)S(1)}, f32[1,128]{1,0:T(1,128)S(1)}, u32[]{:S(2)}, u32[]{:S(2)}) collective-permute-start(f32[1,128]{1,0:T(1,128)S(1)} %get-tuple-element.56), channel_id=1, source_target_pairs={{0,5},{1,6},{2,7},{4,9},{5,10},{6,11},{12,17},{13,18},{14,19},{16,... | collective-permute-start | bytes 1544 | tf_op jit(solution)/shard_map/ppermute | solution.py:356
  136.6 34.6 %collective-permute-start.5 = (f32[1,128]{1,0:T(1,128)S(1)}, f32[1,128]{1,0:T(1,128)S(1)}, u32[]{:S(2)}, u32[]{:S(2)}) collective-permute-start(f32[1,128]{1,0:T(1,128)S(1)} %get-tuple-element.54), channel_id=1, source_target_pairs={{0,125},{1,126},{2,127},{4,1},{5,2},{6,3},{8,5},{9,6},{10,7},{16,1... | collective-permute-start | bytes 1544 | tf_op jit(solution)/shard_map/ppermute | solution.py:356
  138.6 35.8 %collective-permute-start.6 = (f32[1,128]{1,0:T(1,128)S(1)}, f32[1,128]{1,0:T(1,128)S(1)}, u32[]{:S(2)}, u32[]{:S(2)}) collective-permute-start(f32[1,128]{1,0:T(1,128)S(1)} %get-tuple-element.55), channel_id=1, source_target_pairs={{1,4},{2,5},{3,6},{5,8},{6,9},{7,10},{13,16},{14,17},{15,18},{17,2... | collective-permute-start | bytes 1544 | tf_op jit(solution)/shard_map/ppermute | solution.py:356
  139.9 35.6 %collective-permute-start.7 = (f32[1,128]{1,0:T(1,128)S(1)}, f32[1,128]{1,0:T(1,128)S(1)}, u32[]{:S(2)}, u32[]{:S(2)}) collective-permute-start(f32[1,128]{1,0:T(1,128)S(1)} %get-tuple-element.53), channel_id=1, source_target_pairs={{1,124},{2,125},{3,126},{5,0},{6,1},{7,2},{9,4},{10,5},{11,6},{17,... | collective-permute-start | bytes 1544 | tf_op jit(solution)/shard_map/ppermute | solution.py:356
  171.3 9.8 %copy-start.7 = (f32[1,128]{1,0:T(1,128)}, f32[1,128]{1,0:T(1,128)S(1)}, u32[]{:S(2)}) copy-start(f32[1,128]{1,0:T(1,128)S(1)} %collective-permute-done.4.corner_0) | copy-start | bytes 1540
  171.3 9.8 %copy-start.8 = (f32[1,128]{1,0:T(1,128)}, f32[1,128]{1,0:T(1,128)S(1)}, u32[]{:S(2)}) copy-start(f32[1,128]{1,0:T(1,128)S(1)} %collective-permute-done.5.corner_1) | copy-start | bytes 1540
  174.4 6.7 %copy-start.9 = (f32[1,128]{1,0:T(1,128)}, f32[1,128]{1,0:T(1,128)S(1)}, u32[]{:S(2)}) copy-start(f32[1,128]{1,0:T(1,128)S(1)} %collective-permute-done.6.corner_2) | copy-start | bytes 1540
  175.5 5.5 %copy-start.10 = (f32[1,128]{1,0:T(1,128)}, f32[1,128]{1,0:T(1,128)S(1)}, u32[]{:S(2)}) copy-start(f32[1,128]{1,0:T(1,128)S(1)} %collective-permute-done.7.corner_3) | copy-start | bytes 1540

commit v6 on v5

--- a/solution.py
+++ b/solution.py
@@ -24,6 +24,14 @@
 SPREAD = 2
 
 
+def peer_at(position):
+    return (position & 99) | ((position >> 2) & 4) | ((position & 12) << 1)
+
+
+def position_of(peer):
+    return (peer & 99) | ((peer & 4) << 2) | ((peer >> 1) & 12)
+
+
 def slope_of(upstream, hidden):
     argument = hidden.astype(jnp.float32)
     logistic = 0.5 + 0.5 * jnp.tanh(0.5 * argument)
@@ -37,7 +45,7 @@
             for j in range(DESTS):
                 d = i * DESTS + j
                 for s in range(CAP):
-                    block = source.at[targets[0, s, d]]
+                    block = source.at[targets[0, s, peer_at(d)]]
                     pltpu.make_async_copy(block, out.at[d, first + s], sem).start()
             return carry
 
@@ -97,7 +105,7 @@
         mixing[0], projected, (((0,), (0,)), ((), ())), preferred_element_type=jnp.float32
     )
     for k in range(K):
-        slot = neighbors[k, q]
+        slot = position_of(lax.div(neighbors[k, q], CAP)) * CAP + lax.rem(neighbors[k, q], CAP)
         total[slot] += term[k * BS : (k + 1) * BS]
 
     @pl.when(q == PB - 1)
@@ -153,7 +161,7 @@
     q = pl.program_id(0)
     for k in range(K):
         slot = neighbors[k, q]
-        owner = lax.div(slot, CAP)
+        owner = position_of(lax.div(slot, CAP))
         place = lax.rem(slot, CAP)
         right_side[k * BS : (k + 1) * BS, 0:C] = incoming[owner, place]
         right_side[k * BS : (k + 1) * BS, C : 2 * C] = incoming[owner, CAP + place]
@@ -301,7 +309,7 @@
         for j in range(OWNERS):
             for s in range(CAP):
                 o = i * OWNERS + j
-                block = targets[0, s, o]
+                block = targets[0, s, peer_at(o)]
                 sums[(j * CAP + s) % SPREAD][block] += landed[o, s].astype(jnp.float32)
         return carry
 
@@ -374,6 +382,7 @@
     cams = lax.axis_size("cam")
     devices = tiles * cams
     slots = devices * CAP
+    peers = [[peer_at(p) for p in range(devices)]]
     targets = jnp.transpose(send_list, (0, 2, 1))
     reads = neighbors.T
     blocks = (BLK_DEV, BS, C)
@@ -386,7 +395,12 @@
     )
     outgoing, reads = lax.optimization_barrier((outgoing, reads))
     incoming = lax.all_to_all(
-        outgoing, ("tile", "cam"), split_axis=0, concat_axis=0, tiled=True
+        outgoing,
+        ("tile", "cam"),
+        split_axis=0,
+        concat_axis=0,
+        tiled=True,
+        axis_index_groups=peers,
     )
     pixel_slope, mixed, sums, first, last = pixel_part(
         reads, pixel_hidden, pixel_upstream, mixing, pixel_weight, slots
@@ -405,6 +419,7 @@
         split_axis=0,
         concat_axis=0,
         tiled=True,
+        axis_index_groups=peers,
     )
     base = point_upstream.astype(jnp.float32) + jnp.dot(
         point_slope.reshape(BLK_DEV * BS, C), point_weight.T, preferred_element_type=jnp.float32

time: 188 us -> 197 us (1.048)
  starting transfers between devices: 37.3 us -> 50.8 us
  waiting for transfers between devices: 74 us -> 67.9 us
    all_to_all x1, starting transfers between devices: 5.86 us -> 19.3 us  [per_device(): lax.all_to_all(sums.reshape(devices, CAP, BS, C), ('tile', 'cam'), split_...]
    all_to_all x1, waiting for transfers between devices: 7.73 us -> 4.13 us  [per_device(): lax.all_to_all(outgoing, ('tile', 'cam'), split_axis=0, concat_axis=0, ti...]
  transfers between devices with their start and end apart: 10 -> 10, of which waited for: 7 -> 7; matrix products, arithmetic and copies ran while one was open for 3% -> 3% of each run, Pallas kernels for 31% -> 30%
where the time goes in v6:
time: 197 us; the launch traced here: 193 us
  Pallas kernels  68.9 us (35%)
  waiting for transfers between devices  67.9 us (34%)
  starting transfers between devices  50.8 us (26%)
  local copies, waits for them, and re-layouts  3.01 us (2%)
    ppermute x8, waiting for transfers between devices, shifted(): return lax.ppermute(block, ('tile', 'cam'), pairs)  60.2 us
    pallas_call x1, Pallas kernels, main_part(): pl.pallas_call(main_kernel, grid_spec=pltpu.PrefetchScalarGridSpec(num_sc...  29.5 us
    pallas_call x1, Pallas kernels, pixel_part(): pl.pallas_call(pixel_kernel, grid_spec=pltpu.PrefetchScalarGridSpec(num_s...  29 us
    ppermute x8, starting transfers between devices, shifted(): return lax.ppermute(block, ('tile', 'cam'), pairs)  19.5 us
    all_to_all x1, starting transfers between devices, per_device(): lax.all_to_all(sums.reshape(devices, CAP, BS, C), ('tile', 'cam'), split_...  19.3 us
    all_to_all x1, starting transfers between devices, per_device(): lax.all_to_all(outgoing, ('tile', 'cam'), split_axis=0, concat_axis=0, ti...  12 us
    pallas_call x1, Pallas kernels, pack(): pl.pallas_call(pack_kernel, in_specs=[pl.BlockSpec(memory_space=pltpu.SME...  5.72 us
    pallas_call x1, Pallas kernels, return_part(): pl.pallas_call(return_kernel, in_specs=[pl.BlockSpec(memory_space=pltpu.S...  4.67 us
  transfers between devices with their start and end apart: 10, of which 7 were waited for; matrix products, arithmetic and copies ran while one was open for 3% of the time, Pallas kernels for 30%

profile of v6, /device:TPU:1, one launch (start us, length us, event | category | flops | bytes accessed | tf_op | source)
XLA Modules:
  0.0 193.3 jit_solution(13130392877579663547)
XLA Ops:
  0.6 0.0 copy-start
  0.6 5.7 %pack.1 = (bf16[128,4,64,128]{3,2,1,0:T(8,128)(2,1)}, bf16[32,64,128]{2,1,0:T(8,128)(2,1)}) custom-call(s32[1,2,128]{2,1,0:T(2,128)} %bitcast.27, bf16[32,64,128]{2,1,0:T(8,128)(2,1)} %bitcast.22, bf16[32,64,128]{2,1,0:T(8,128)(2,1)} %bitcast.23, bf16[32,64,128]{2,1,0:T(8,128)(2,1)} %bitcast.21), custom_call_target="tpu_custom_call" | custom-call | flops 10485760 | bytes 12582912 | tf_op jit(solution)/shard_map/pack/pallas_call | solution.py:67
  6.4 12.0 %all-to-all-start = ((bf16[128,4,64,128]{3,2,1,0:T(8,128)(2,1)}), bf16[128,4,64,128]{3,2,1,0:T(8,128)(2,1)}, u32[]{:S(2)}, u32[]{:S(2)}) async-start(bf16[128,4,64,128]{3,2,1,0:T(8,128)(2,1)} %get-tuple-element.30), calls=%async_computation | async-start | bytes 16777216 | tf_op jit(solution)/shard_map/all_to_all | solution.py:397
  18.3 29.0 %pixel_part.1 = (bf16[64,128,128]{2,1,0:T(8,128)(2,1)}, bf16[32,256,128]{2,1,0:T(8,128)(2,1)}, bf16[256,64,128]{2,1,0:T(8,128)(2,1)}, f32[64,128]{1,0:T(8,128)}, f32[64,128]{1,0:T(8,128)}) custom-call(s32[6,32]{1,0:T(8,128)} %bitcast.25, bf16[64,128,128]{2,1,0:T(8,128)(2,1)} %hidden.1, bf16[64,128,128]{2,1,0:T(8,128)(2,1)} %upstream.3, ...), custom_call_target="tpu_custom_call" | custom-call | flops 1258291200 | bytes 18874368 | tf_op jit(solution)/shard_map/pixel_part/pallas_call | solution.py:122
  47.4 0.8 fusion
  48.1 3.3 %collective-permute-start = (bf16[1,128,128]{2,1,0:T(8,128)(2,1)S(1)}, bf16[1,128,128]{2,1,0:T(8,128)(2,1)S(1)}, u32[]{:S(2)}, u32[]{:S(2)}) collective-permute-start(bf16[1,128,128]{2,1,0:T(8,128)(2,1)S(1)} %get-tuple-element.52), channel_id=1, source_target_pairs={{0,1},{1,2},{2,3},{4,5},{5,6},{6,7},{8,9},{9,10},{10,11},{12,13},{... | collective-permute-start | bytes 98312 | tf_op jit(solution)/shard_map/ppermute | solution.py:364
  51.4 1.3 collective-permute-start.1
  52.7 3.8 %collective-permute-start.2 = (f32[64,128]{1,0:T(8,128)}, f32[64,128]{1,0:T(8,128)S(1)}, u32[]{:S(2)}, u32[]{:S(2)}) collective-permute-start(f32[64,128]{1,0:T(8,128)} %get-tuple-element.45), channel_id=1, source_target_pairs={{0,4},{1,5},{2,6},{3,7},{4,8},{5,9},{6,10},{7,11},{12,16},{13,17},... | collective-permute-start | bytes 98312 | tf_op jit(solution)/shard_map/ppermute | solution.py:364
  56.5 1.9 collective-permute-start.3
  58.4 48.8 %collective-permute-done.above = bf16[1,128,128]{2,1,0:T(8,128)(2,1)S(1)} collective-permute-done((bf16[1,128,128]{2,1,0:T(8,128)(2,1)S(1)}, bf16[1,128,128]{2,1,0:T(8,128)(2,1)S(1)}, u32[]{:S(2)}, u32[]{:S(2)}) %collective-permute-start) | collective-permute-done | bytes 32800 | tf_op jit(solution)/shard_map/ppermute | solution.py:364
  107.2 0.0 copy-start.3
  107.2 6.7 %collective-permute-done.1.below = bf16[1,128,128]{2,1,0:T(8,128)(2,1)S(1)} collective-permute-done((bf16[1,128,128]{2,1,0:T(8,128)(2,1)S(1)}, bf16[1,128,128]{2,1,0:T(8,128)(2,1)S(1)}, u32[]{:S(2)}, u32[]{:S(2)}) %collective-permute-start.1) | collective-permute-done | bytes 32800 | tf_op jit(solution)/shard_map/ppermute | solution.py:364
  113.9 0.0 copy-start.4
  113.9 0.0 collective-permute-done.2.left
  113.9 0.0 copy-start.5
  113.9 0.0 collective-permute-done.3.right
  113.9 0.0 copy-start.6
  113.9 4.1 %all-to-all-done.incoming = bf16[128,4,64,128]{3,2,1,0:T(8,128)(2,1)} async-done(((bf16[128,4,64,128]{3,2,1,0:T(8,128)(2,1)}), bf16[128,4,64,128]{3,2,1,0:T(8,128)(2,1)}, u32[]{:S(2)}, u32[]{:S(2)}) %all-to-all-start) | async-done | bytes 8388640 | tf_op jit(solution)/shard_map/all_to_all | solution.py:397
  118.0 0.0 copy-start.1
  118.0 0.0 copy-start.2
  118.0 0.0 copy-done.3
  118.1 0.0 copy-done.4
  118.1 0.0 copy-done.5
  118.1 0.0 copy-done.6
  118.1 19.3 %all-to-all-start.1 = ((bf16[128,2,64,128]{3,2,1,0:T(8,128)(2,1)}), bf16[128,2,64,128]{3,2,1,0:T(8,128)(2,1)}, u32[]{:S(2)}, u32[]{:S(2)}) async-start(bf16[128,2,64,128]{3,2,1,0:T(8,128)(2,1)} %bitcast.19), calls=%async_computation.1 | async-start | bytes 8388608 | tf_op jit(solution)/shard_map/all_to_all | solution.py:416
  137.4 0.8 slice_bitcast_fusion.3
  138.2 0.6 pad_maximum_fusion.gains
  138.8 0.0 copy-done
  138.8 0.0 copy-done.1
  138.8 0.0 copy-done.2
  138.8 1.3 convolution_add_fusion
  140.1 0.7 fusion.2
  140.8 4.6 %collective-permute-start.4 = (f32[1,128]{1,0:T(1,128)S(1)}, f32[1,128]{1,0:T(1,128)S(1)}, u32[]{:S(2)}, u32[]{:S(2)}) collective-permute-start(f32[1,128]{1,0:T(1,128)S(1)} %get-tuple-element.56), channel_id=1, source_target_pairs={{0,5},{1,6},{2,7},{4,9},{5,10},{6,11},{12,17},{13,18},{14,19},{16,... | collective-permute-start | bytes 1544 | tf_op jit(solution)/shard_map/ppermute | solution.py:364
  145.4 0.7 fusion.1
  146.1 2.1 %collective-permute-start.5 = (f32[1,128]{1,0:T(1,128)S(1)}, f32[1,128]{1,0:T(1,128)S(1)}, u32[]{:S(2)}, u32[]{:S(2)}) collective-permute-start(f32[1,128]{1,0:T(1,128)S(1)} %get-tuple-element.54), channel_id=1, source_target_pairs={{0,125},{1,126},{2,127},{4,1},{5,2},{6,3},{8,5},{9,6},{10,7},{16,1... | collective-permute-start | bytes 1544 | tf_op jit(solution)/shard_map/ppermute | solution.py:364
  148.2 1.3 collective-permute-start.6
  149.5 1.3 collective-permute-start.7
  150.8 29.5 %main_part.1 = (bf16[32,256,384]{2,1,0:T(8,128)(2,1)}, bf16[64,128,128]{2,1,0:T(8,128)(2,1)}, f32[4,128]{1,0:T(4,128)}) custom-call(s32[6,32]{1,0:T(8,128)} %bitcast.26, bf16[128,4,64,128]{3,2,1,0:T(8,128)(2,1)} %all-to-all-done.incoming, bf16[32,256,128]{2,1,0:T(8,128)(2,1)} %get-tuple-element.39.mixed, bf16[64,128,128]{2,1,0:T(8,128)(2,1)} %pixels.1, ...), custom_call_target="tpu_custom_call" | custom-call | flops 2726297600 | bytes 31457280 | tf_op jit(solution)/shard_map/main_part/pallas_call | solution.py:228
  180.3 0.6 collective-permute-done.4.corner_0
  180.8 0.0 copy-start.7
  180.8 0.0 collective-permute-done.5.corner_1
  180.8 0.0 copy-start.8
  180.8 3.1 %collective-permute-done.6.corner_2 = f32[1,128]{1,0:T(1,128)S(1)} collective-permute-done((f32[1,128]{1,0:T(1,128)S(1)}, f32[1,128]{1,0:T(1,128)S(1)}, u32[]{:S(2)}, u32[]{:S(2)}) %collective-permute-start.6) | collective-permute-done | bytes 544 | tf_op jit(solution)/shard_map/ppermute | solution.py:364
  184.0 0.0 copy-start.9
  184.0 1.0 collective-permute-done.7.corner_3
  185.0 0.0 copy-start.10
  185.0 3.6 %all-to-all-done.1.received = bf16[128,2,64,128]{3,2,1,0:T(8,128)(2,1)} async-done(((bf16[128,2,64,128]{3,2,1,0:T(8,128)(2,1)}), bf16[128,2,64,128]{3,2,1,0:T(8,128)(2,1)}, u32[]{:S(2)}, u32[]{:S(2)}) %all-to-all-start.1) | async-done | bytes 4194336 | tf_op jit(solution)/shard_map/all_to_all | solution.py:416
  188.6 0.0 copy-done.7
  188.6 0.0 copy-done.8
  188.6 0.0 copy-done.9
  188.6 0.0 copy-done.10
  188.6 4.7 %return_part.1 = (bf16[32,64,128]{2,1,0:T(8,128)(2,1)}, bf16[64,128,128]{2,1,0:T(8,128)(2,1)}) custom-call(s32[1,2,128]{2,1,0:T(2,128)} %bitcast.28, bf16[128,2,64,128]{3,2,1,0:T(8,128)(2,1)} %all-to-all-done.1.received, f32[32,64,128]{2,1,0:T(8,128)} %bitcast.20, f32[4,128]{1,0:T(4,128)} %get-tuple-element.44.totals, ...), custom_call_target="tpu_custom_call", output_to_operand_aliasing={{1}: (9, {})} | custom-call | flops 4194304 | bytes 6291456 | tf_op jit(solution)/shard_map/return_part/pallas_call | solution.py:330
Async XLA Ops:
  0.6 138.1 %copy-start = (bf16[128,128]{1,0:T(8,128)(2,1)S(1)}, bf16[128,128]{1,0:T(8,128)(2,1)}, u32[]{:S(2)}) copy-start(bf16[128,128]{1,0:T(8,128)(2,1)} %param.22) | copy-start | bytes 98308
  6.4 111.7 %all-to-all-start = ((bf16[128,4,64,128]{3,2,1,0:T(8,128)(2,1)}), bf16[128,4,64,128]{3,2,1,0:T(8,128)(2,1)}, u32[]{:S(2)}, u32[]{:S(2)}) async-start(bf16[128,4,64,128]{3,2,1,0:T(8,128)(2,1)} %get-tuple-element.30), calls=%async_computation | async-start | bytes 16777216 | tf_op jit(solution)/shard_map/all_to_all | solution.py:397
  48.1 59.1 %collective-permute-start = (bf16[1,128,128]{2,1,0:T(8,128)(2,1)S(1)}, bf16[1,128,128]{2,1,0:T(8,128)(2,1)S(1)}, u32[]{:S(2)}, u32[]{:S(2)}) collective-permute-start(bf16[1,128,128]{2,1,0:T(8,128)(2,1)S(1)} %get-tuple-element.52), channel_id=1, source_target_pairs={{0,1},{1,2},{2,3},{4,5},{5,6},{6,7},{8,9},{9,10},{10,11},{12,13},{... | collective-permute-start | bytes 98312 | tf_op jit(solution)/shard_map/ppermute | solution.py:364
  51.4 62.5 %collective-permute-start.1 = (bf16[1,128,128]{2,1,0:T(8,128)(2,1)S(1)}, bf16[1,128,128]{2,1,0:T(8,128)(2,1)S(1)}, u32[]{:S(2)}, u32[]{:S(2)}) collective-permute-start(bf16[1,128,128]{2,1,0:T(8,128)(2,1)S(1)} %get-tuple-element.51), channel_id=1, source_target_pairs={{1,0},{2,1},{3,2},{5,4},{6,5},{7,6},{9,8},{10,9},{11,10},{13,12},{... | collective-permute-start | bytes 98312 | tf_op jit(solution)/shard_map/ppermute | solution.py:364
  52.7 61.2 %collective-permute-start.2 = (f32[64,128]{1,0:T(8,128)}, f32[64,128]{1,0:T(8,128)S(1)}, u32[]{:S(2)}, u32[]{:S(2)}) collective-permute-start(f32[64,128]{1,0:T(8,128)} %get-tuple-element.45), channel_id=1, source_target_pairs={{0,4},{1,5},{2,6},{3,7},{4,8},{5,9},{6,10},{7,11},{12,16},{13,17},... | collective-permute-start | bytes 98312 | tf_op jit(solution)/shard_map/ppermute | solution.py:364
  56.5 57.4 %collective-permute-start.3 = (f32[64,128]{1,0:T(8,128)}, f32[64,128]{1,0:T(8,128)S(1)}, u32[]{:S(2)}, u32[]{:S(2)}) collective-permute-start(f32[64,128]{1,0:T(8,128)} %get-tuple-element.46), channel_id=1, source_target_pairs={{0,124},{1,125},{2,126},{3,127},{4,0},{5,1},{6,2},{7,3},{8,4},{9,5... | collective-permute-start | bytes 98312 | tf_op jit(solution)/shard_map/ppermute | solution.py:364
  107.2 10.8 %copy-start.3 = (bf16[1,128,128]{2,1,0:T(8,128)(2,1)}, bf16[1,128,128]{2,1,0:T(8,128)(2,1)S(1)}, u32[]{:S(2)}) copy-start(bf16[1,128,128]{2,1,0:T(8,128)(2,1)S(1)} %collective-permute-done.above) | copy-start | bytes 98308
  113.9 4.2 %copy-start.4 = (bf16[1,128,128]{2,1,0:T(8,128)(2,1)}, bf16[1,128,128]{2,1,0:T(8,128)(2,1)S(1)}, u32[]{:S(2)}) copy-start(bf16[1,128,128]{2,1,0:T(8,128)(2,1)S(1)} %collective-permute-done.1.below) | copy-start | bytes 98308
  113.9 4.2 %copy-start.5 = (f32[64,128]{1,0:T(8,128)}, f32[64,128]{1,0:T(8,128)S(1)}, u32[]{:S(2)}) copy-start(f32[64,128]{1,0:T(8,128)S(1)} %collective-permute-done.2.left) | copy-start | bytes 98308
  113.9 4.2 %copy-start.6 = (f32[64,128]{1,0:T(8,128)}, f32[64,128]{1,0:T(8,128)S(1)}, u32[]{:S(2)}) copy-start(f32[64,128]{1,0:T(8,128)S(1)} %collective-permute-done.3.right) | copy-start | bytes 98308
  118.0 20.7 %copy-start.1 = (bf16[2048,128]{1,0:T(8,128)(2,1)S(1)}, bf16[2048,128]{1,0:T(8,128)(2,1)}, u32[]{:S(2)}) copy-start(bf16[2048,128]{1,0:T(8,128)(2,1)} %param.17) | copy-start | bytes 1572868
  118.0 20.7 %copy-start.2 = (bf16[32,64,128]{2,1,0:T(8,128)(2,1)S(1)}, bf16[32,64,128]{2,1,0:T(8,128)(2,1)}, u32[]{:S(2)}) copy-start(bf16[32,64,128]{2,1,0:T(8,128)(2,1)} %get-tuple-element.36) | copy-start | bytes 1572868
  118.1 70.5 %all-to-all-start.1 = ((bf16[128,2,64,128]{3,2,1,0:T(8,128)(2,1)}), bf16[128,2,64,128]{3,2,1,0:T(8,128)(2,1)}, u32[]{:S(2)}, u32[]{:S(2)}) async-start(bf16[128,2,64,128]{3,2,1,0:T(8,128)(2,1)} %bitcast.19), calls=%async_computation.1 | async-start | bytes 8388608 | tf_op jit(solution)/shard_map/all_to_all | solution.py:416
  140.8 40.0 %collective-permute-start.4 = (f32[1,128]{1,0:T(1,128)S(1)}, f32[1,128]{1,0:T(1,128)S(1)}, u32[]{:S(2)}, u32[]{:S(2)}) collective-permute-start(f32[1,128]{1,0:T(1,128)S(1)} %get-tuple-element.56), channel_id=1, source_target_pairs={{0,5},{1,6},{2,7},{4,9},{5,10},{6,11},{12,17},{13,18},{14,19},{16,... | collective-permute-start | bytes 1544 | tf_op jit(solution)/shard_map/ppermute | solution.py:364
  146.1 34.8 %collective-permute-start.5 = (f32[1,128]{1,0:T(1,128)S(1)}, f32[1,128]{1,0:T(1,128)S(1)}, u32[]{:S(2)}, u32[]{:S(2)}) collective-permute-start(f32[1,128]{1,0:T(1,128)S(1)} %get-tuple-element.54), channel_id=1, source_target_pairs={{0,125},{1,126},{2,127},{4,1},{5,2},{6,3},{8,5},{9,6},{10,7},{16,1... | collective-permute-start | bytes 1544 | tf_op jit(solution)/shard_map/ppermute | solution.py:364
  148.2 35.8 %collective-permute-start.6 = (f32[1,128]{1,0:T(1,128)S(1)}, f32[1,128]{1,0:T(1,128)S(1)}, u32[]{:S(2)}, u32[]{:S(2)}) collective-permute-start(f32[1,128]{1,0:T(1,128)S(1)} %get-tuple-element.55), channel_id=1, source_target_pairs={{1,4},{2,5},{3,6},{5,8},{6,9},{7,10},{13,16},{14,17},{15,18},{17,2... | collective-permute-start | bytes 1544 | tf_op jit(solution)/shard_map/ppermute | solution.py:364
  149.5 35.5 %collective-permute-start.7 = (f32[1,128]{1,0:T(1,128)S(1)}, f32[1,128]{1,0:T(1,128)S(1)}, u32[]{:S(2)}, u32[]{:S(2)}) collective-permute-start(f32[1,128]{1,0:T(1,128)S(1)} %get-tuple-element.53), channel_id=1, source_target_pairs={{1,124},{2,125},{3,126},{5,0},{6,1},{7,2},{9,4},{10,5},{11,6},{17,... | collective-permute-start | bytes 1544 | tf_op jit(solution)/shard_map/ppermute | solution.py:364
  180.8 7.8 %copy-start.7 = (f32[1,128]{1,0:T(1,128)}, f32[1,128]{1,0:T(1,128)S(1)}, u32[]{:S(2)}) copy-start(f32[1,128]{1,0:T(1,128)S(1)} %collective-permute-done.4.corner_0) | copy-start | bytes 1540
  180.8 7.8 %copy-start.8 = (f32[1,128]{1,0:T(1,128)}, f32[1,128]{1,0:T(1,128)S(1)}, u32[]{:S(2)}) copy-start(f32[1,128]{1,0:T(1,128)S(1)} %collective-permute-done.5.corner_1) | copy-start | bytes 1540
  184.0 4.6 %copy-start.9 = (f32[1,128]{1,0:T(1,128)}, f32[1,128]{1,0:T(1,128)S(1)}, u32[]{:S(2)}) copy-start(f32[1,128]{1,0:T(1,128)S(1)} %collective-permute-done.6.corner_2) | copy-start | bytes 1540
  185.0 3.6 %copy-start.10 = (f32[1,128]{1,0:T(1,128)}, f32[1,128]{1,0:T(1,128)S(1)}, u32[]{:S(2)}) copy-start(f32[1,128]{1,0:T(1,128)S(1)} %collective-permute-done.7.corner_3) | copy-start | bytes 1540

commit v7 on v6

--- a/solution.py
+++ b/solution.py
@@ -25,11 +25,10 @@
 
 
 def peer_at(position):
-    return (position & 99) | ((position >> 2) & 4) | ((position & 12) << 1)
-
-
-def position_of(peer):
-    return (peer & 99) | ((peer & 4) << 2) | ((peer >> 1) & 12)
+    return (position & 7) | ((position & 24) << 2) | ((position >> 2) & 24)
+
+
+position_of = peer_at
 
 
 def slope_of(upstream, hidden):

time: 197 us -> 187 us (0.949)
  starting transfers between devices: 50.8 us -> 36.1 us
  waiting for transfers between devices: 67.9 us -> 74.4 us
    all_to_all x1, starting transfers between devices: 19.3 us -> 4.91 us  [per_device(): lax.all_to_all(sums.reshape(devices, CAP, BS, C), ('tile', 'cam'), split_...]
    all_to_all x1, waiting for transfers between devices: 4.13 us -> 7.22 us  [per_device(): lax.all_to_all(outgoing, ('tile', 'cam'), split_axis=0, concat_axis=0, ti...]
  transfers between devices with their start and end apart: 10 -> 10, of which waited for: 7 -> 7; matrix products, arithmetic and copies ran while one was open for 3% -> 3% of each run, Pallas kernels for 30% -> 32%
where the time goes in v7:
time: 187 us; the launch traced here: 185 us
  waiting for transfers between devices  74.4 us (40%)
  Pallas kernels  68.9 us (37%)
  starting transfers between devices  36.1 us (19%)
  local copies, waits for them, and re-layouts  3.01 us (2%)
    ppermute x8, waiting for transfers between devices, shifted(): return lax.ppermute(block, ('tile', 'cam'), pairs)  61.8 us
    pallas_call x1, Pallas kernels, main_part(): pl.pallas_call(main_kernel, grid_spec=pltpu.PrefetchScalarGridSpec(num_sc...  29.5 us
    pallas_call x1, Pallas kernels, pixel_part(): pl.pallas_call(pixel_kernel, grid_spec=pltpu.PrefetchScalarGridSpec(num_s...  29 us
    ppermute x8, starting transfers between devices, shifted(): return lax.ppermute(block, ('tile', 'cam'), pairs)  19.3 us
    all_to_all x1, starting transfers between devices, per_device(): lax.all_to_all(outgoing, ('tile', 'cam'), split_axis=0, concat_axis=0, ti...  12 us
    all_to_all x1, waiting for transfers between devices, per_device(): lax.all_to_all(outgoing, ('tile', 'cam'), split_axis=0, concat_axis=0, ti...  7.22 us
    pallas_call x1, Pallas kernels, pack(): pl.pallas_call(pack_kernel, in_specs=[pl.BlockSpec(memory_space=pltpu.SME...  5.72 us
    all_to_all x1, waiting for transfers between devices, per_device(): lax.all_to_all(sums.reshape(devices, CAP, BS, C), ('tile', 'cam'), split_...  5.44 us
  transfers between devices with their start and end apart: 10, of which 7 were waited for; matrix products, arithmetic and copies ran while one was open for 3% of the time, Pallas kernels for 32%

profile of v7, /device:TPU:1, one launch (start us, length us, event | category | flops | bytes accessed | tf_op | source)
XLA Modules:
  0.0 185.2 jit_solution(4105445095058167427)
XLA Ops:
  0.6 0.0 copy-start
  0.6 5.7 %pack.1 = (bf16[128,4,64,128]{3,2,1,0:T(8,128)(2,1)}, bf16[32,64,128]{2,1,0:T(8,128)(2,1)}) custom-call(s32[1,2,128]{2,1,0:T(2,128)} %bitcast.27, bf16[32,64,128]{2,1,0:T(8,128)(2,1)} %bitcast.22, bf16[32,64,128]{2,1,0:T(8,128)(2,1)} %bitcast.23, bf16[32,64,128]{2,1,0:T(8,128)(2,1)} %bitcast.21), custom_call_target="tpu_custom_call" | custom-call | flops 10485760 | bytes 12582912 | tf_op jit(solution)/shard_map/pack/pallas_call | solution.py:66
  6.4 12.0 %all-to-all-start = ((bf16[128,4,64,128]{3,2,1,0:T(8,128)(2,1)}), bf16[128,4,64,128]{3,2,1,0:T(8,128)(2,1)}, u32[]{:S(2)}, u32[]{:S(2)}) async-start(bf16[128,4,64,128]{3,2,1,0:T(8,128)(2,1)} %get-tuple-element.30), calls=%async_computation | async-start | bytes 16777216 | tf_op jit(solution)/shard_map/all_to_all | solution.py:396
  18.3 29.0 %pixel_part.1 = (bf16[64,128,128]{2,1,0:T(8,128)(2,1)}, bf16[32,256,128]{2,1,0:T(8,128)(2,1)}, bf16[256,64,128]{2,1,0:T(8,128)(2,1)}, f32[64,128]{1,0:T(8,128)}, f32[64,128]{1,0:T(8,128)}) custom-call(s32[6,32]{1,0:T(8,128)} %bitcast.25, bf16[64,128,128]{2,1,0:T(8,128)(2,1)} %hidden.1, bf16[64,128,128]{2,1,0:T(8,128)(2,1)} %upstream.3, ...), custom_call_target="tpu_custom_call" | custom-call | flops 1258291200 | bytes 18874368 | tf_op jit(solution)/shard_map/pixel_part/pallas_call | solution.py:121
  47.4 0.8 fusion
  48.1 3.3 %collective-permute-start = (bf16[1,128,128]{2,1,0:T(8,128)(2,1)S(1)}, bf16[1,128,128]{2,1,0:T(8,128)(2,1)S(1)}, u32[]{:S(2)}, u32[]{:S(2)}) collective-permute-start(bf16[1,128,128]{2,1,0:T(8,128)(2,1)S(1)} %get-tuple-element.52), channel_id=1, source_target_pairs={{0,1},{1,2},{2,3},{4,5},{5,6},{6,7},{8,9},{9,10},{10,11},{12,13},{... | collective-permute-start | bytes 98312 | tf_op jit(solution)/shard_map/ppermute | solution.py:363
  51.4 1.3 collective-permute-start.1
  52.7 3.8 %collective-permute-start.2 = (f32[64,128]{1,0:T(8,128)}, f32[64,128]{1,0:T(8,128)S(1)}, u32[]{:S(2)}, u32[]{:S(2)}) collective-permute-start(f32[64,128]{1,0:T(8,128)} %get-tuple-element.45), channel_id=1, source_target_pairs={{0,4},{1,5},{2,6},{3,7},{4,8},{5,9},{6,10},{7,11},{12,16},{13,17},... | collective-permute-start | bytes 98312 | tf_op jit(solution)/shard_map/ppermute | solution.py:363
  56.5 1.9 %collective-permute-start.3 = (f32[64,128]{1,0:T(8,128)}, f32[64,128]{1,0:T(8,128)S(1)}, u32[]{:S(2)}, u32[]{:S(2)}) collective-permute-start(f32[64,128]{1,0:T(8,128)} %get-tuple-element.46), channel_id=1, source_target_pairs={{0,124},{1,125},{2,126},{3,127},{4,0},{5,1},{6,2},{7,3},{8,4},{9,5... | collective-permute-start | bytes 98312 | tf_op jit(solution)/shard_map/ppermute | solution.py:363
  58.4 51.3 %collective-permute-done.above = bf16[1,128,128]{2,1,0:T(8,128)(2,1)S(1)} collective-permute-done((bf16[1,128,128]{2,1,0:T(8,128)(2,1)S(1)}, bf16[1,128,128]{2,1,0:T(8,128)(2,1)S(1)}, u32[]{:S(2)}, u32[]{:S(2)}) %collective-permute-start) | collective-permute-done | bytes 32800 | tf_op jit(solution)/shard_map/ppermute | solution.py:363
  109.8 0.0 copy-start.3
  109.8 5.5 %collective-permute-done.1.below = bf16[1,128,128]{2,1,0:T(8,128)(2,1)S(1)} collective-permute-done((bf16[1,128,128]{2,1,0:T(8,128)(2,1)S(1)}, bf16[1,128,128]{2,1,0:T(8,128)(2,1)S(1)}, u32[]{:S(2)}, u32[]{:S(2)}) %collective-permute-start.1) | collective-permute-done | bytes 32800 | tf_op jit(solution)/shard_map/ppermute | solution.py:363
  115.3 0.0 copy-start.4
  115.3 0.0 collective-permute-done.2.left
  115.3 0.0 copy-start.5
  115.3 0.0 collective-permute-done.3.right
  115.3 0.0 copy-start.6
  115.3 7.2 %all-to-all-done.incoming = bf16[128,4,64,128]{3,2,1,0:T(8,128)(2,1)} async-done(((bf16[128,4,64,128]{3,2,1,0:T(8,128)(2,1)}), bf16[128,4,64,128]{3,2,1,0:T(8,128)(2,1)}, u32[]{:S(2)}, u32[]{:S(2)}) %all-to-all-start) | async-done | bytes 8388640 | tf_op jit(solution)/shard_map/all_to_all | solution.py:396
  122.5 0.0 copy-start.1
  122.5 0.0 copy-start.2
  122.5 0.0 copy-done.3
  122.5 0.0 copy-done.4
  122.5 0.0 copy-done.5
  122.5 0.0 copy-done.6
  122.5 4.9 %all-to-all-start.1 = ((bf16[128,2,64,128]{3,2,1,0:T(8,128)(2,1)}), bf16[128,2,64,128]{3,2,1,0:T(8,128)(2,1)}, u32[]{:S(2)}, u32[]{:S(2)}) async-start(bf16[128,2,64,128]{3,2,1,0:T(8,128)(2,1)} %bitcast.19), calls=%async_computation.1 | async-start | bytes 8388608 | tf_op jit(solution)/shard_map/all_to_all | solution.py:415
  127.5 0.8 slice_bitcast_fusion.3
  128.2 0.6 pad_maximum_fusion.gains
  128.8 0.0 copy-done
  128.8 0.0 copy-done.1
  128.8 0.0 copy-done.2
  128.8 1.3 convolution_add_fusion
  130.1 0.7 fusion.2
  130.8 4.4 %collective-permute-start.4 = (f32[1,128]{1,0:T(1,128)S(1)}, f32[1,128]{1,0:T(1,128)S(1)}, u32[]{:S(2)}, u32[]{:S(2)}) collective-permute-start(f32[1,128]{1,0:T(1,128)S(1)} %get-tuple-element.56), channel_id=1, source_target_pairs={{0,5},{1,6},{2,7},{4,9},{5,10},{6,11},{12,17},{13,18},{14,19},{16,... | collective-permute-start | bytes 1544 | tf_op jit(solution)/shard_map/ppermute | solution.py:363
  135.2 0.7 fusion.1
  135.9 2.1 %collective-permute-start.5 = (f32[1,128]{1,0:T(1,128)S(1)}, f32[1,128]{1,0:T(1,128)S(1)}, u32[]{:S(2)}, u32[]{:S(2)}) collective-permute-start(f32[1,128]{1,0:T(1,128)S(1)} %get-tuple-element.54), channel_id=1, source_target_pairs={{0,125},{1,126},{2,127},{4,1},{5,2},{6,3},{8,5},{9,6},{10,7},{16,1... | collective-permute-start | bytes 1544 | tf_op jit(solution)/shard_map/ppermute | solution.py:363
  138.0 1.3 collective-permute-start.6
  139.3 1.3 collective-permute-start.7
  140.6 29.5 %main_part.1 = (bf16[32,256,384]{2,1,0:T(8,128)(2,1)}, bf16[64,128,128]{2,1,0:T(8,128)(2,1)}, f32[4,128]{1,0:T(4,128)}) custom-call(s32[6,32]{1,0:T(8,128)} %bitcast.26, bf16[128,4,64,128]{3,2,1,0:T(8,128)(2,1)} %all-to-all-done.incoming, bf16[32,256,128]{2,1,0:T(8,128)(2,1)} %get-tuple-element.39.mixed, bf16[64,128,128]{2,1,0:T(8,128)(2,1)} %pixels.1, ...), custom_call_target="tpu_custom_call" | custom-call | flops 2726297600 | bytes 31457280 | tf_op jit(solution)/shard_map/main_part/pallas_call | solution.py:227
  170.1 0.6 collective-permute-done.4.corner_0
  170.7 0.0 copy-start.7
  170.7 0.0 collective-permute-done.5.corner_1
  170.7 0.0 copy-start.8
  170.7 3.1 %collective-permute-done.6.corner_2 = f32[1,128]{1,0:T(1,128)S(1)} collective-permute-done((f32[1,128]{1,0:T(1,128)S(1)}, f32[1,128]{1,0:T(1,128)S(1)}, u32[]{:S(2)}, u32[]{:S(2)}) %collective-permute-start.6) | collective-permute-done | bytes 544 | tf_op jit(solution)/shard_map/ppermute | solution.py:363
  173.8 0.0 copy-start.9
  173.8 1.2 collective-permute-done.7.corner_3
  175.0 0.0 copy-start.10
  175.0 5.4 %all-to-all-done.1.received = bf16[128,2,64,128]{3,2,1,0:T(8,128)(2,1)} async-done(((bf16[128,2,64,128]{3,2,1,0:T(8,128)(2,1)}), bf16[128,2,64,128]{3,2,1,0:T(8,128)(2,1)}, u32[]{:S(2)}, u32[]{:S(2)}) %all-to-all-start.1) | async-done | bytes 4194336 | tf_op jit(solution)/shard_map/all_to_all | solution.py:415
  180.5 0.0 copy-done.7
  180.5 0.0 copy-done.8
  180.5 0.0 copy-done.9
  180.5 0.0 copy-done.10
  180.5 4.7 %return_part.1 = (bf16[32,64,128]{2,1,0:T(8,128)(2,1)}, bf16[64,128,128]{2,1,0:T(8,128)(2,1)}) custom-call(s32[1,2,128]{2,1,0:T(2,128)} %bitcast.28, bf16[128,2,64,128]{3,2,1,0:T(8,128)(2,1)} %all-to-all-done.1.received, f32[32,64,128]{2,1,0:T(8,128)} %bitcast.20, f32[4,128]{1,0:T(4,128)} %get-tuple-element.44.totals, ...), custom_call_target="tpu_custom_call", output_to_operand_aliasing={{1}: (9, {})} | custom-call | flops 4194304 | bytes 6291456 | tf_op jit(solution)/shard_map/return_part/pallas_call | solution.py:329
Async XLA Ops:
  0.6 128.2 %copy-start = (bf16[128,128]{1,0:T(8,128)(2,1)S(1)}, bf16[128,128]{1,0:T(8,128)(2,1)}, u32[]{:S(2)}) copy-start(bf16[128,128]{1,0:T(8,128)(2,1)} %param.22) | copy-start | bytes 98308
  6.4 116.1 %all-to-all-start = ((bf16[128,4,64,128]{3,2,1,0:T(8,128)(2,1)}), bf16[128,4,64,128]{3,2,1,0:T(8,128)(2,1)}, u32[]{:S(2)}, u32[]{:S(2)}) async-start(bf16[128,4,64,128]{3,2,1,0:T(8,128)(2,1)} %get-tuple-element.30), calls=%async_computation | async-start | bytes 16777216 | tf_op jit(solution)/shard_map/all_to_all | solution.py:396
  48.1 61.6 %collective-permute-start = (bf16[1,128,128]{2,1,0:T(8,128)(2,1)S(1)}, bf16[1,128,128]{2,1,0:T(8,128)(2,1)S(1)}, u32[]{:S(2)}, u32[]{:S(2)}) collective-permute-start(bf16[1,128,128]{2,1,0:T(8,128)(2,1)S(1)} %get-tuple-element.52), channel_id=1, source_target_pairs={{0,1},{1,2},{2,3},{4,5},{5,6},{6,7},{8,9},{9,10},{10,11},{12,13},{... | collective-permute-start | bytes 98312 | tf_op jit(solution)/shard_map/ppermute | solution.py:363
  51.4 63.8 %collective-permute-start.1 = (bf16[1,128,128]{2,1,0:T(8,128)(2,1)S(1)}, bf16[1,128,128]{2,1,0:T(8,128)(2,1)S(1)}, u32[]{:S(2)}, u32[]{:S(2)}) collective-permute-start(bf16[1,128,128]{2,1,0:T(8,128)(2,1)S(1)} %get-tuple-element.51), channel_id=1, source_target_pairs={{1,0},{2,1},{3,2},{5,4},{6,5},{7,6},{9,8},{10,9},{11,10},{13,12},{... | collective-permute-start | bytes 98312 | tf_op jit(solution)/shard_map/ppermute | solution.py:363
  52.7 62.5 %collective-permute-start.2 = (f32[64,128]{1,0:T(8,128)}, f32[64,128]{1,0:T(8,128)S(1)}, u32[]{:S(2)}, u32[]{:S(2)}) collective-permute-start(f32[64,128]{1,0:T(8,128)} %get-tuple-element.45), channel_id=1, source_target_pairs={{0,4},{1,5},{2,6},{3,7},{4,8},{5,9},{6,10},{7,11},{12,16},{13,17},... | collective-permute-start | bytes 98312 | tf_op jit(solution)/shard_map/ppermute | solution.py:363
  56.5 58.8 %collective-permute-start.3 = (f32[64,128]{1,0:T(8,128)}, f32[64,128]{1,0:T(8,128)S(1)}, u32[]{:S(2)}, u32[]{:S(2)}) collective-permute-start(f32[64,128]{1,0:T(8,128)} %get-tuple-element.46), channel_id=1, source_target_pairs={{0,124},{1,125},{2,126},{3,127},{4,0},{5,1},{6,2},{7,3},{8,4},{9,5... | collective-permute-start | bytes 98312 | tf_op jit(solution)/shard_map/ppermute | solution.py:363
  109.8 12.8 %copy-start.3 = (bf16[1,128,128]{2,1,0:T(8,128)(2,1)}, bf16[1,128,128]{2,1,0:T(8,128)(2,1)S(1)}, u32[]{:S(2)}) copy-start(bf16[1,128,128]{2,1,0:T(8,128)(2,1)S(1)} %collective-permute-done.above) | copy-start | bytes 98308
  115.3 7.3 %copy-start.4 = (bf16[1,128,128]{2,1,0:T(8,128)(2,1)}, bf16[1,128,128]{2,1,0:T(8,128)(2,1)S(1)}, u32[]{:S(2)}) copy-start(bf16[1,128,128]{2,1,0:T(8,128)(2,1)S(1)} %collective-permute-done.1.below) | copy-start | bytes 98308
  115.3 7.3 %copy-start.5 = (f32[64,128]{1,0:T(8,128)}, f32[64,128]{1,0:T(8,128)S(1)}, u32[]{:S(2)}) copy-start(f32[64,128]{1,0:T(8,128)S(1)} %collective-permute-done.2.left) | copy-start | bytes 98308
  115.3 7.3 %copy-start.6 = (f32[64,128]{1,0:T(8,128)}, f32[64,128]{1,0:T(8,128)S(1)}, u32[]{:S(2)}) copy-start(f32[64,128]{1,0:T(8,128)S(1)} %collective-permute-done.3.right) | copy-start | bytes 98308
  122.5 6.3 %copy-start.1 = (bf16[2048,128]{1,0:T(8,128)(2,1)S(1)}, bf16[2048,128]{1,0:T(8,128)(2,1)}, u32[]{:S(2)}) copy-start(bf16[2048,128]{1,0:T(8,128)(2,1)} %param.17) | copy-start | bytes 1572868
  122.5 6.3 %copy-start.2 = (bf16[32,64,128]{2,1,0:T(8,128)(2,1)S(1)}, bf16[32,64,128]{2,1,0:T(8,128)(2,1)}, u32[]{:S(2)}) copy-start(bf16[32,64,128]{2,1,0:T(8,128)(2,1)} %get-tuple-element.36) | copy-start | bytes 1572868
  122.5 57.9 %all-to-all-start.1 = ((bf16[128,2,64,128]{3,2,1,0:T(8,128)(2,1)}), bf16[128,2,64,128]{3,2,1,0:T(8,128)(2,1)}, u32[]{:S(2)}, u32[]{:S(2)}) async-start(bf16[128,2,64,128]{3,2,1,0:T(8,128)(2,1)} %bitcast.19), calls=%async_computation.1 | async-start | bytes 8388608 | tf_op jit(solution)/shard_map/all_to_all | solution.py:415
  130.8 39.8 %collective-permute-start.4 = (f32[1,128]{1,0:T(1,128)S(1)}, f32[1,128]{1,0:T(1,128)S(1)}, u32[]{:S(2)}, u32[]{:S(2)}) collective-permute-start(f32[1,128]{1,0:T(1,128)S(1)} %get-tuple-element.56), channel_id=1, source_target_pairs={{0,5},{1,6},{2,7},{4,9},{5,10},{6,11},{12,17},{13,18},{14,19},{16,... | collective-permute-start | bytes 1544 | tf_op jit(solution)/shard_map/ppermute | solution.py:363
  135.9 34.8 %collective-permute-start.5 = (f32[1,128]{1,0:T(1,128)S(1)}, f32[1,128]{1,0:T(1,128)S(1)}, u32[]{:S(2)}, u32[]{:S(2)}) collective-permute-start(f32[1,128]{1,0:T(1,128)S(1)} %get-tuple-element.54), channel_id=1, source_target_pairs={{0,125},{1,126},{2,127},{4,1},{5,2},{6,3},{8,5},{9,6},{10,7},{16,1... | collective-permute-start | bytes 1544 | tf_op jit(solution)/shard_map/ppermute | solution.py:363
  138.0 35.8 %collective-permute-start.6 = (f32[1,128]{1,0:T(1,128)S(1)}, f32[1,128]{1,0:T(1,128)S(1)}, u32[]{:S(2)}, u32[]{:S(2)}) collective-permute-start(f32[1,128]{1,0:T(1,128)S(1)} %get-tuple-element.55), channel_id=1, source_target_pairs={{1,4},{2,5},{3,6},{5,8},{6,9},{7,10},{13,16},{14,17},{15,18},{17,2... | collective-permute-start | bytes 1544 | tf_op jit(solution)/shard_map/ppermute | solution.py:363
  139.3 35.7 %collective-permute-start.7 = (f32[1,128]{1,0:T(1,128)S(1)}, f32[1,128]{1,0:T(1,128)S(1)}, u32[]{:S(2)}, u32[]{:S(2)}) collective-permute-start(f32[1,128]{1,0:T(1,128)S(1)} %get-tuple-element.53), channel_id=1, source_target_pairs={{1,124},{2,125},{3,126},{5,0},{6,1},{7,2},{9,4},{10,5},{11,6},{17,... | collective-permute-start | bytes 1544 | tf_op jit(solution)/shard_map/ppermute | solution.py:363
  170.7 9.8 %copy-start.7 = (f32[1,128]{1,0:T(1,128)}, f32[1,128]{1,0:T(1,128)S(1)}, u32[]{:S(2)}) copy-start(f32[1,128]{1,0:T(1,128)S(1)} %collective-permute-done.4.corner_0) | copy-start | bytes 1540
  170.7 9.8 %copy-start.8 = (f32[1,128]{1,0:T(1,128)}, f32[1,128]{1,0:T(1,128)S(1)}, u32[]{:S(2)}) copy-start(f32[1,128]{1,0:T(1,128)S(1)} %collective-permute-done.5.corner_1) | copy-start | bytes 1540
  173.8 6.7 %copy-start.9 = (f32[1,128]{1,0:T(1,128)}, f32[1,128]{1,0:T(1,128)S(1)}, u32[]{:S(2)}) copy-start(f32[1,128]{1,0:T(1,128)S(1)} %collective-permute-done.6.corner_2) | copy-start | bytes 1540
  175.0 5.5 %copy-start.10 = (f32[1,128]{1,0:T(1,128)}, f32[1,128]{1,0:T(1,128)S(1)}, u32[]{:S(2)}) copy-start(f32[1,128]{1,0:T(1,128)S(1)} %collective-permute-done.7.corner_3) | copy-start | bytes 1540
